TPU v7x, 32 devices: a whole 2x2x4 slice. The times are simulated.
32 devices in a mesh: wide: 16 (over z, y, core), narrow: 2 (over x).
Axes of the slice: x: 2, y: 2, z: 4, core: 2. Of those that a mesh axis runs over, the one named last changes fastest.
Arguments:
- dark: bfloat16 [64, 16, 2, 16], P(None, None, 'narrow'), may hold values from -6 to 6
- w_enc: bfloat16 [27, 64, 64], replicated, may hold values from -0.15625 to 0.15625
- up_weight: bfloat16 [512, 16, 64], replicated, may hold values from -0.75 to 0.75
- w_dec: bfloat16 [27, 16, 16], replicated, may hold values from -0.3125 to 0.3125
- cotangent: bfloat16 [16, 128, 16, 128], P(None, 'wide', 'narrow'), may hold values from -6 to 6
Outputs:
- grad_dark: float32 [64, 16, 2, 16], P(None, None, 'narrow')
- grad_w_enc: float32 [27, 64, 64], replicated
- grad_up_weight: float32 [512, 16, 64], P(('wide', 'narrow'))
- grad_w_dec: float32 [27, 16, 16], replicated
All inputs are finite; a program needn't handle non-finite values.
Results may differ from a plain program's by a relative error of at most 0.0053.
Values may be sent and summed in bfloat16 or wider, within the bound.
No kernel may reach another device: no remote copies, remote signals or barrier semaphores. Data moves between devices by JAX's collectives and lax.ppermute only.
A program may use at most 64 MiB of HBM per device.

v0:
```python
import math

import jax
import jax.numpy as jnp
from jax import lax
from jax.sharding import PartitionSpec as P

RATIO = 8


def padded_2(block, sides, width):
    for axis, dim in sides:
        count = lax.axis_size(axis)
        forward = [(i, i + 1) for i in range(count - 1)]
        backward = [(target, source) for source, target in forward]
        low = lax.ppermute(
            lax.slice_in_dim(block, block.shape[dim] - width, None, axis=dim), axis, forward
        )
        high = lax.ppermute(lax.slice_in_dim(block, 0, width, axis=dim), axis, backward)
        block = jnp.concatenate([low, block, high], axis=dim)
    return block


def silu_slope(values):
    sigma = jax.nn.sigmoid(values)
    return sigma * (1.0 + values * (1.0 - sigma))


def coarse_margin(field):
    return padded_2(field, (("narrow", 2),), 1)


def pad_coarse(field):
    return jnp.pad(field, ((0, 0), (1, 1), (0, 0), (1, 1)))


def pad_fine(field):
    return jnp.pad(field, ((0, 0), (0, 0), (0, 0), (1, 1)))


def flatten(kernel):
    return kernel.transpose(1, 0, 2).reshape(kernel.shape[1], -1)


def transposed(kernel):
    return kernel[::-1].transpose(2, 0, 1).reshape(kernel.shape[2], -1)


def unflatten(flat):
    return flat.reshape(flat.shape[0], 27, -1).transpose(1, 0, 2)


def columns(padded, first, count, depth, width):
    pieces = []
    for shift_x in range(3):
        for shift_z in range(3):
            for shift_y in range(3):
                pieces.append(
                    padded[
                        :,
                        first + shift_x : first + shift_x + count,
                        shift_z : shift_z + depth,
                        shift_y : shift_y + width,
                    ]
                )
    return jnp.concatenate(pieces, 0)


def block_size(planes):
    return planes // 4


def convolve_blocks(padded, flat):
    planes = padded.shape[1] - 2
    depth = padded.shape[2] - 2
    width = padded.shape[3] - 2
    block = block_size(planes)
    results = []
    for first in range(0, planes, block):
        stacked = columns(padded, first, block, depth, width)
        results.append(
            jnp.einsum("ok,kxzy->oxzy", flat, stacked, preferred_element_type=jnp.float32)
        )
    return jnp.concatenate(results, 1)


def upsample(table, enc_planes, ratio, fine_ch):
    chans = enc_planes.shape[0]
    planes = enc_planes.shape[1]
    depth = enc_planes.shape[2]
    width = enc_planes.shape[3]
    up_rows = jnp.dot(
        table, enc_planes.reshape(chans, planes * depth * width), preferred_element_type=jnp.float32
    )
    return (
        up_rows.reshape(ratio, ratio, ratio, fine_ch, planes, depth, width)
        .transpose(3, 4, 0, 5, 1, 6, 2)
        .reshape(fine_ch, planes * ratio, depth * ratio, width * ratio)
        .astype(jnp.bfloat16)
    )


def on_device(dark, w_enc, up_weight, w_dec, cotangent):
    ratio = RATIO
    chans = dark.shape[0]
    fine_ch = w_dec.shape[1]
    subs = up_weight.shape[0]
    wide_count = lax.axis_size("wide")
    narrow_count = lax.axis_size("narrow")
    coarse_planes = dark.shape[1]
    own_planes = coarse_planes // wide_count
    depth = dark.shape[2]
    width = dark.shape[3]
    first_plane = lax.axis_index("wide") * own_planes
    dark_padded = pad_coarse(coarse_margin(dark))
    enc_flat_kernel = flatten(w_enc)
    enc_pre = convolve_blocks(dark_padded, enc_flat_kernel)
    encoded = jax.nn.silu(enc_pre).astype(jnp.bfloat16)
    enc_window = lax.dynamic_slice_in_dim(
        jnp.pad(encoded, ((0, 0), (1, 1), (0, 0), (0, 0))), first_plane, own_planes + 2, 1
    )
    enc_own = enc_window[:, 1 : own_planes + 1]
    cells = own_planes * depth * width
    enc_flat = enc_own.reshape(chans, cells)
    table = up_weight.reshape(subs * fine_ch, chans)
    fine_planes = own_planes * ratio
    fine_depth = depth * ratio
    fine_width = width * ratio
    upsampled = upsample(table, enc_own, ratio, fine_ch)
    up_padded = pad_fine(padded_2(upsampled, (("wide", 1), ("narrow", 2)), 1))
    dec_flat = flatten(w_dec)
    cot_float = cotangent.astype(jnp.float32)
    block = block_size(fine_planes)
    grad_pieces = []
    dec_total = jnp.zeros((fine_ch, 27 * fine_ch), jnp.float32)
    for first in range(0, fine_planes, block):
        stacked = columns(up_padded, first, block, fine_depth, fine_width)
        pre_block = jnp.einsum(
            "ok,kxzy->oxzy", dec_flat, stacked, preferred_element_type=jnp.float32
        )
        piece = (cot_float[:, first : first + block] * silu_slope(pre_block)).astype(jnp.bfloat16)
        dec_total = dec_total + jnp.einsum(
            "oxzy,kxzy->ok", piece, stacked, preferred_element_type=jnp.float32
        )
        grad_pieces.append(piece)
    dec_grad = jnp.concatenate(grad_pieces, 1)
    grad_padded = pad_fine(padded_2(dec_grad, (("wide", 1), ("narrow", 2)), 1))
    back_up = convolve_blocks(grad_padded, transposed(w_dec))
    up_grad = (cot_float + back_up).astype(jnp.bfloat16)
    grad_rows = (
        up_grad.reshape(fine_ch, own_planes, ratio, depth, ratio, width, ratio)
        .transpose(2, 4, 6, 0, 1, 3, 5)
        .reshape(subs * fine_ch, cells)
    )
    enc_grad_own = (
        jnp.einsum("kc,kn->cn", table, grad_rows, preferred_element_type=jnp.float32)
        .reshape(chans, own_planes, depth, width)
        .astype(jnp.bfloat16)
    )
    enc_grad = lax.all_gather(enc_grad_own, "wide", axis=1, tiled=True)
    enc_pre_grad = (enc_grad.astype(jnp.float32) * silu_slope(enc_pre)).astype(jnp.bfloat16)
    grad_own = lax.dynamic_slice_in_dim(enc_pre_grad, first_plane, own_planes, 1)
    dark_own = lax.dynamic_slice_in_dim(dark_padded, first_plane, own_planes + 2, 1)
    stacked_own = columns(dark_own, 0, own_planes, depth, width)
    enc_total = jnp.einsum(
        "oxzy,kxzy->ok", grad_own, stacked_own, preferred_element_type=jnp.float32
    )
    grad_dark = convolve_blocks(pad_coarse(coarse_margin(enc_pre_grad)), transposed(w_enc))
    coarse_count = coarse_planes * depth * narrow_count * width
    coarse_scale = 1.0 / math.sqrt(coarse_count)
    fine_scale = 1.0 / math.sqrt(coarse_count * subs)
    owners = wide_count * narrow_count
    own_rows = subs // owners
    enc_sum, dec_sum, up_sum = lax.psum(
        (
            enc_total,
            dec_total,
            jnp.einsum(
                "kn,cn->kc", grad_rows, enc_flat, preferred_element_type=jnp.float32
            ).reshape(subs, fine_ch, chans),
        ),
        ("wide", "narrow"),
    )
    up_own = lax.dynamic_slice_in_dim(
        up_sum, lax.axis_index(("wide", "narrow")) * own_rows, own_rows, 0
    )
    return (
        grad_dark,
        unflatten(enc_sum) * coarse_scale,
        up_own * coarse_scale,
        unflatten(dec_sum) * fine_scale,
    )


def solution(mesh):
    in_specs = (P(None, None, "narrow", None), P(), P(), P(), P(None, "wide", "narrow", None))
    out_specs = (P(None, None, "narrow", None), P(), P(("wide", "narrow"), None, None), P())
    return jax.shard_map(
        on_device, mesh=mesh, in_specs=in_specs, out_specs=out_specs, check_vma=False
    )
```

profile of v0, /device:TPU:0, one launch (start us, length us, event | category | flops | bytes accessed | tf_op | source)
XLA Modules:
  0.0 328.7 jit_solution(9364406737006700190)
XLA Ops:
  7.2 4.8 %collective-permute-start = (bf16[64,16,1,16]{0,3,1,2:T(8,128)(2,1)}, bf16[64,16,1,16]{0,3,1,2:T(8,128)(2,1)S(1)}, u32[]{:S(2)}, u32[]{:S(2)}) collective-permute-start(bf16[64,16,1,16]{0,3,1,2:T(8,128)(2,1)} %bitcast.229), channel_id=1, source_target_pairs={{0,1},{2,3},{4,5},{6,7},{8,9},{10,11},{12,13},{14,15},{16,17},{18,... | collective-permute-start | bytes 98312 | tf_op jit(solution)/shard_map/ppermute | solution.py:16
  12.1 1.3 collective-permute-start.1
  13.4 1.5 fusion.88
  14.9 1.3 copy.39
  16.6 3.0 copy.48
  20.4 0.7 fusion.78
  21.2 0.7 fusion.79
  21.9 0.8 fusion.80
  23.3 0.7 fusion.87
  24.7 1.1 concatenate.180
  26.0 1.1 concatenate.182
  27.4 1.1 concatenate.184
  29.9 2.7 convert_element_type.71
  32.6 3.5 %copy.96 = bf16[8,8,8,16,1,1,16]{3,2,6,1,0,5,4:T(8,128)(2,1)} copy(bf16[8,8,8,16,1,1,16]{3,2,1,0,6,5,4:T(8,128)(2,1)} %convert_element_type.71) | data formatting | bytes 524288 | tf_op jit(solution)/shard_map/convert_element_type | solution.py:99
  36.1 1.9 copy.50
  38.7 1.4 collective-permute-start.2
  40.1 1.3 collective-permute-start.3
  41.4 1.0 copy_convert_fusion
  42.4 1.0 rev.7
  44.3 0.7 collective-permute-done.3
  45.0 4.6 %collective-permute-start.4 = (bf16[16,10,1,128]{3,0,2,1:T(8,128)(2,1)S(1)}, bf16[16,10,1,128]{3,0,2,1:T(8,128)(2,1)S(1)}, u32[]{:S(2)}, u32[]{:S(2)}) collective-permute-start(bf16[16,10,1,128]{3,0,2,1:T(8,128)(2,1)S(1)} %get-tuple-element.286), channel_id=1, source_target_pairs={{0,1},{2,3},{4,5},{6,7},{8,9},{10,11},{12,13},{14,15},{16,17},{18,... | collective-permute-start | bytes 122888 | tf_op jit(solution)/shard_map/ppermute | solution.py:16
  49.6 1.3 collective-permute-start.5
  50.9 0.7 constant_dynamic-slice_fusion.26
  51.6 1.4 concatenate.219
  53.0 2.5 collective-permute-done.5
  59.1 3.1 collective-permute-start.6
  67.2 1.3 collective-permute-start.7
  68.6 45.2 %psum.23 = f32[16,432]{1,0:T(8,128)S(1)} all-reduce(f32[16,432]{1,0:T(8,128)S(1)} %fusion.4), channel_id=1, replica_groups=mesh['wide'=16,'narrow'=2] {'wide','narrow'}, use_global_device_ids=true, to_apply=%region_2.3 | all-reduce | flops 6912 | bytes 55296 | tf_op jit(solution)/shard_map/psum | solution.py:174
  114.5 4.1 %collective-permute-start.8 = (bf16[16,10,1,128]{3,0,2,1:T(8,128)(2,1)}, bf16[16,10,1,128]{3,0,2,1:T(8,128)(2,1)S(1)}, u32[]{:S(2)}, u32[]{:S(2)}) collective-permute-start(bf16[16,10,1,128]{3,0,2,1:T(8,128)(2,1)} %get-tuple-element.282), channel_id=1, source_target_pairs={{0,1},{2,3},{4,5},{6,7},{8,9},{10,11},{12,13},{14,15},{16,17},{18,... | collective-permute-start | bytes 122888 | tf_op jit(solution)/shard_map/ppermute | solution.py:16
  118.6 1.3 collective-permute-start.9
  120.6 0.9 mul.135
  121.4 0.8 copy.75
  122.3 2.5 collective-permute-done.9
  132.2 1.8 copy.64
  133.9 4.1 %copy.70 = bf16[8,8,8,16,1,1,16]{6,3,2,1,0,5,4:T(8,128)(2,1)} copy(bf16[8,8,8,16,1,1,16]{3,2,6,1,0,5,4:T(8,128)(2,1)} %bitcast.218) | data formatting | bytes 524288 | tf_op jit(solution)/shard_map/transpose | solution.py:152
  138.0 3.5 %copy.65 = bf16[8,8,8,16,1,1,16]{3,2,1,0,6,5,4:T(8,128)(2,1)} copy(bf16[8,8,8,16,1,1,16]{3,2,6,1,0,5,4:T(8,128)(2,1)} %bitcast.219) | data formatting | bytes 524288 | tf_op jit(solution)/shard_map/transpose | solution.py:152
  141.5 4.7 %reshape.344 = bf16[8192,16]{0,1:T(8,128)(2,1)S(1)} reshape(bf16[8,8,8,16,1,1,16]{3,2,1,0,6,5,4:T(8,128)(2,1)} %copy.65) | data formatting | bytes 524288 | tf_op jit(solution)/shard_map/reshape | solution.py:153
  146.7 19.6 %all-gather = bf16[64,256]{0,1:T(8,128)(2,1)S(1)} all-gather(bf16[64,16]{0,1:T(8,128)(2,1)S(1)} %fusion.7), channel_id=2, replica_groups=mesh['wide'=16,'narrow'=2] {'wide'}, dimensions={1}, use_global_device_ids=true | all-gather | bytes 34816 | tf_op jit(solution)/shard_map/all_gather | solution.py:160
  166.3 2.2 collective-permute-start.10
  168.6 1.5 collective-permute-start.11
  170.1 2.8 fusion.1
  173.0 1.0 fusion.58
  174.0 0.7 collective-permute-done.11
  177.5 139.8 %all-reduce.8.cloned.1.call-done = (f32[64,1728]{1,0:T(8,128)}, f32[512,16,64]{2,0,1:T(8,128)}) async-done(((f32[64,1728]{1,0:T(8,128)}, f32[512,16,64]{2,0,1:T(8,128)}), (f32[64,1728]{1,0:T(8,128)}, f32[512,16,64]{2,0,1:T(8,128)})) %all-reduce.8.cloned.1.call-update) | async-done | bytes 2539536 | tf_op jit(solution)/shard_map/psum | solution.py:174
  317.3 1.1 broadcast_multiply_fusion
  318.8 1.4 copy.73
  320.2 0.9 dynamic-slice_multiply_fusion
  321.1 0.7 copy.74
  (284 shorter events, 25.8 us)
Async XLA Ops:
  7.2 310.1 %all-reduce.8.cloned.1.call-start = ((), (), s32[]{:S(2)}) async-start(), calls=%async_computation | async-start | bytes 9306112 | tf_op jit(solution)/shard_map/psum | solution.py:174
  7.2 12.4 %collective-permute-start = (bf16[64,16,1,16]{0,3,1,2:T(8,128)(2,1)}, bf16[64,16,1,16]{0,3,1,2:T(8,128)(2,1)S(1)}, u32[]{:S(2)}, u32[]{:S(2)}) collective-permute-start(bf16[64,16,1,16]{0,3,1,2:T(8,128)(2,1)} %bitcast.229), channel_id=1, source_target_pairs={{0,1},{2,3},{4,5},{6,7},{8,9},{10,11},{12,13},{14,15},{16,17},{18,... | collective-permute-start | bytes 98312 | tf_op jit(solution)/shard_map/ppermute | solution.py:16
  12.1 7.6 %collective-permute-start.1 = (bf16[64,16,1,16]{0,3,1,2:T(8,128)(2,1)}, bf16[64,16,1,16]{0,3,1,2:T(8,128)(2,1)S(1)}, u32[]{:S(2)}, u32[]{:S(2)}) collective-permute-start(bf16[64,16,1,16]{0,3,1,2:T(8,128)(2,1)} %bitcast.230), channel_id=1, source_target_pairs={{1,0},{3,2},{5,4},{7,6},{9,8},{11,10},{13,12},{15,14},{17,16},{19,... | collective-permute-start | bytes 98312 | tf_op jit(solution)/shard_map/ppermute | solution.py:19
  16.6 3.1 copy-start.4
  21.1 4.9 %copy-start.19 = (bf16[64,4,1,16]{0,3,1,2:T(8,128)(2,1)S(1)}, bf16[64,4,1,16]{0,3,1,2:T(8,128)(2,1)}, u32[]{:S(2)}) copy-start(bf16[64,4,1,16]{0,3,1,2:T(8,128)(2,1)} %get-tuple-element.345) | copy-start | bytes 24580
  21.1 4.9 %copy-start.20 = (bf16[64,4,1,16]{0,3,1,2:T(8,128)(2,1)S(1)}, bf16[64,4,1,16]{0,3,1,2:T(8,128)(2,1)}, u32[]{:S(2)}) copy-start(bf16[64,4,1,16]{0,3,1,2:T(8,128)(2,1)} %get-tuple-element.346) | copy-start | bytes 24580
  21.1 4.9 %copy-start.21 = (bf16[64,4,1,16]{0,3,1,2:T(8,128)(2,1)S(1)}, bf16[64,4,1,16]{0,3,1,2:T(8,128)(2,1)}, u32[]{:S(2)}) copy-start(bf16[64,4,1,16]{0,3,1,2:T(8,128)(2,1)} %get-tuple-element.347) | copy-start | bytes 24580
  23.9 3.4 %copy-start.24 = (bf16[64,4,1,16]{0,3,1,2:T(8,128)(2,1)S(1)}, bf16[64,4,1,16]{0,3,1,2:T(8,128)(2,1)}, u32[]{:S(2)}) copy-start(bf16[64,4,1,16]{0,3,1,2:T(8,128)(2,1)} %get-tuple-element.243) | copy-start | bytes 24580
  23.9 3.5 %copy-start.25 = (bf16[64,4,1,16]{0,3,1,2:T(8,128)(2,1)S(1)}, bf16[64,4,1,16]{0,3,1,2:T(8,128)(2,1)}, u32[]{:S(2)}) copy-start(bf16[64,4,1,16]{0,3,1,2:T(8,128)(2,1)} %get-tuple-element.244) | copy-start | bytes 24580
  24.0 3.5 %copy-start.26 = (bf16[64,4,1,16]{0,3,1,2:T(8,128)(2,1)S(1)}, bf16[64,4,1,16]{0,3,1,2:T(8,128)(2,1)}, u32[]{:S(2)}) copy-start(bf16[64,4,1,16]{0,3,1,2:T(8,128)(2,1)} %get-tuple-element.245) | copy-start | bytes 24580
  24.6 2.8 copy-start.28
  24.6 4.1 %copy-start.22 = (bf16[64,4,1,16]{0,3,1,2:T(8,128)(2,1)S(1)}, bf16[64,4,1,16]{0,3,1,2:T(8,128)(2,1)}, u32[]{:S(2)}) copy-start(bf16[64,4,1,16]{0,3,1,2:T(8,128)(2,1)} %get-tuple-element.330) | copy-start | bytes 24580
  24.6 4.1 %copy-start.23 = (bf16[64,4,1,16]{0,3,1,2:T(8,128)(2,1)S(1)}, bf16[64,4,1,16]{0,3,1,2:T(8,128)(2,1)}, u32[]{:S(2)}) copy-start(bf16[64,4,1,16]{0,3,1,2:T(8,128)(2,1)} %get-tuple-element.331) | copy-start | bytes 24580
  24.7 4.1 %copy-start.27 = (bf16[64,4,1,16]{0,3,1,2:T(8,128)(2,1)S(1)}, bf16[64,4,1,16]{0,3,1,2:T(8,128)(2,1)}, u32[]{:S(2)}) copy-start(bf16[64,4,1,16]{0,3,1,2:T(8,128)(2,1)} %get-tuple-element.351) | copy-start | bytes 24580
  26.0 3.2 copy-start.5
  27.4 2.5 copy-start.7
  28.7 1.2 copy-start.9
  29.2 3.4 %copy-start.11 = (f32[64,4,1,16]{0,3,1,2:T(8,128)}, f32[64,4,1,16]{0,3,1,2:T(8,128)S(1)}, u32[]{:S(2)}) copy-start(f32[64,4,1,16]{0,3,1,2:T(8,128)S(1)} %convolution_bitcast_fusion.16) | copy-start | bytes 49156
  36.1 5.3 %copy-start.2 = (bf16[16,8,8,128]{3,2,1,0:T(8,128)(2,1)S(1)}, bf16[16,8,8,128]{3,2,1,0:T(8,128)(2,1)}, u32[]{:S(2)}) copy-start(bf16[16,8,8,128]{3,2,1,0:T(8,128)(2,1)} %param.9) | copy-start | bytes 786436
  36.1 7.3 %copy-start.13 = (bf16[27,16,16]{0,2,1:T(8,128)(2,1)S(1)}, bf16[27,16,16]{0,2,1:T(8,128)(2,1)}, u32[]{:S(2)}) copy-start(bf16[27,16,16]{0,2,1:T(8,128)(2,1)} %param.8) | copy-start | bytes 41476
  38.7 5.6 %collective-permute-start.2 = (bf16[16,1,8,128]{3,0,2,1:T(8,128)(2,1)}, bf16[16,1,8,128]{3,0,2,1:T(8,128)(2,1)S(1)}, u32[]{:S(2)}, u32[]{:S(2)}) collective-permute-start(bf16[16,1,8,128]{3,0,2,1:T(8,128)(2,1)} %get-tuple-element.297), channel_id=1, source_target_pairs={{0,2},{2,4},{4,6},{6,8},{8,10},{10,12},{12,14},{14,16},{16,18},{18... | collective-permute-start | bytes 98312 | tf_op jit(solution)/shard_map/ppermute | solution.py:16
  40.1 4.9 %collective-permute-start.3 = (bf16[16,1,8,128]{3,0,2,1:T(8,128)(2,1)}, bf16[16,1,8,128]{3,0,2,1:T(8,128)(2,1)S(1)}, u32[]{:S(2)}, u32[]{:S(2)}) collective-permute-start(bf16[16,1,8,128]{3,0,2,1:T(8,128)(2,1)} %get-tuple-element.298), channel_id=1, source_target_pairs={{2,0},{4,2},{6,4},{8,6},{10,8},{12,10},{14,12},{16,14},{18,16},{20... | collective-permute-start | bytes 98312 | tf_op jit(solution)/shard_map/ppermute | solution.py:19
  45.0 8.0 %collective-permute-start.4 = (bf16[16,10,1,128]{3,0,2,1:T(8,128)(2,1)S(1)}, bf16[16,10,1,128]{3,0,2,1:T(8,128)(2,1)S(1)}, u32[]{:S(2)}, u32[]{:S(2)}) collective-permute-start(bf16[16,10,1,128]{3,0,2,1:T(8,128)(2,1)S(1)} %get-tuple-element.286), channel_id=1, source_target_pairs={{0,1},{2,3},{4,5},{6,7},{8,9},{10,11},{12,13},{14,15},{16,17},{18,... | collective-permute-start | bytes 122888 | tf_op jit(solution)/shard_map/ppermute | solution.py:16
  49.6 5.9 %collective-permute-start.5 = (bf16[16,10,1,128]{3,0,2,1:T(8,128)(2,1)S(1)}, bf16[16,10,1,128]{3,0,2,1:T(8,128)(2,1)S(1)}, u32[]{:S(2)}, u32[]{:S(2)}) collective-permute-start(bf16[16,10,1,128]{3,0,2,1:T(8,128)(2,1)S(1)} %get-tuple-element.287), channel_id=1, source_target_pairs={{1,0},{3,2},{5,4},{7,6},{9,8},{11,10},{13,12},{15,14},{17,16},{19,... | collective-permute-start | bytes 122888 | tf_op jit(solution)/shard_map/ppermute | solution.py:19
  57.6 1.0 copy-start.1
  59.1 4.4 %collective-permute-start.6 = (bf16[16,1,8,128]{3,0,2,1:T(8,128)(2,1)S(1)}, bf16[16,1,8,128]{3,0,2,1:T(8,128)(2,1)S(1)}, u32[]{:S(2)}, u32[]{:S(2)}) collective-permute-start(bf16[16,1,8,128]{3,0,2,1:T(8,128)(2,1)S(1)} %slice.2093), channel_id=1, source_target_pairs={{0,2},{2,4},{4,6},{6,8},{8,10},{10,12},{12,14},{14,16},{16,18},{18... | collective-permute-start | bytes 98312 | tf_op jit(solution)/shard_map/ppermute | solution.py:16
  63.5 0.6 copy-start.17
  67.2 46.6 %collective-permute-start.7 = (bf16[16,1,8,128]{3,0,2,1:T(8,128)(2,1)S(1)}, bf16[16,1,8,128]{3,0,2,1:T(8,128)(2,1)S(1)}, u32[]{:S(2)}, u32[]{:S(2)}) collective-permute-start(bf16[16,1,8,128]{3,0,2,1:T(8,128)(2,1)S(1)} %slice.2150), channel_id=1, source_target_pairs={{2,0},{4,2},{6,4},{8,6},{10,8},{12,10},{14,12},{16,14},{18,16},{20... | collective-permute-start | bytes 98312 | tf_op jit(solution)/shard_map/ppermute | solution.py:19
  113.8 4.8 %copy-start.15 = (bf16[16,1,8,128]{3,0,2,1:T(8,128)(2,1)}, bf16[16,1,8,128]{3,0,2,1:T(8,128)(2,1)S(1)}, u32[]{:S(2)}) copy-start(bf16[16,1,8,128]{3,0,2,1:T(8,128)(2,1)S(1)} %collective-permute-done.7) | copy-start | bytes 98308
  114.5 7.8 %collective-permute-start.8 = (bf16[16,10,1,128]{3,0,2,1:T(8,128)(2,1)}, bf16[16,10,1,128]{3,0,2,1:T(8,128)(2,1)S(1)}, u32[]{:S(2)}, u32[]{:S(2)}) collective-permute-start(bf16[16,10,1,128]{3,0,2,1:T(8,128)(2,1)} %get-tuple-element.282), channel_id=1, source_target_pairs={{0,1},{2,3},{4,5},{6,7},{8,9},{10,11},{12,13},{14,15},{16,17},{18,... | collective-permute-start | bytes 122888 | tf_op jit(solution)/shard_map/ppermute | solution.py:16
  118.6 6.1 %collective-permute-start.9 = (bf16[16,10,1,128]{3,0,2,1:T(8,128)(2,1)}, bf16[16,10,1,128]{3,0,2,1:T(8,128)(2,1)S(1)}, u32[]{:S(2)}, u32[]{:S(2)}) collective-permute-start(bf16[16,10,1,128]{3,0,2,1:T(8,128)(2,1)} %get-tuple-element.283), channel_id=1, source_target_pairs={{1,0},{3,2},{5,4},{7,6},{9,8},{11,10},{13,12},{15,14},{17,16},{19,... | collective-permute-start | bytes 122888 | tf_op jit(solution)/shard_map/ppermute | solution.py:19
  122.3 3.0 copy-start.18
  129.1 0.9 copy-start.16
  131.0 1.0 copy-start.3
  146.2 20.0 %copy-start.6 = (f32[64,4,1,16]{0,3,1,2:T(8,128)S(1)}, f32[64,4,1,16]{0,3,1,2:T(8,128)}, u32[]{:S(2)}) copy-start(f32[64,4,1,16]{0,3,1,2:T(8,128)} %copy-done.5) | copy-start | bytes 49156
  146.3 20.0 %copy-start.8 = (f32[64,4,1,16]{0,3,1,2:T(8,128)S(1)}, f32[64,4,1,16]{0,3,1,2:T(8,128)}, u32[]{:S(2)}) copy-start(f32[64,4,1,16]{0,3,1,2:T(8,128)} %copy-done.7) | copy-start | bytes 49156
  146.3 20.0 %copy-start.10 = (f32[64,4,1,16]{0,3,1,2:T(8,128)S(1)}, f32[64,4,1,16]{0,3,1,2:T(8,128)}, u32[]{:S(2)}) copy-start(f32[64,4,1,16]{0,3,1,2:T(8,128)} %copy-done.9) | copy-start | bytes 49156
  146.3 20.0 %copy-start.12 = (f32[64,4,1,16]{0,3,1,2:T(8,128)S(1)}, f32[64,4,1,16]{0,3,1,2:T(8,128)}, u32[]{:S(2)}) copy-start(f32[64,4,1,16]{0,3,1,2:T(8,128)} %copy-done.11) | copy-start | bytes 49156
  146.3 23.8 %copy-start = (bf16[8,8,8,16,1,1,16]{6,3,2,1,0,5,4:T(8,128)(2,1)S(1)}, bf16[8,8,8,16,1,1,16]{6,3,2,1,0,5,4:T(8,128)(2,1)}, u32[]{:S(2)}) copy-start(bf16[8,8,8,16,1,1,16]{6,3,2,1,0,5,4:T(8,128)(2,1)} %copy.70) | copy-start | bytes 786436
  166.3 7.7 %collective-permute-start.10 = (bf16[64,16,1,16]{0,3,1,2:T(8,128)(2,1)S(1)}, bf16[64,16,1,16]{0,3,1,2:T(8,128)(2,1)S(1)}, u32[]{:S(2)}, u32[]{:S(2)}) collective-permute-start(bf16[64,16,1,16]{0,3,1,2:T(8,128)(2,1)S(1)} %fusion.41), channel_id=1, source_target_pairs={{0,1},{2,3},{4,5},{6,7},{8,9},{10,11},{12,13},{14,15},{16,17},{18,... | collective-permute-start | bytes 98312 | tf_op jit(solution)/shard_map/ppermute | solution.py:16
  168.6 6.2 %collective-permute-start.11 = (bf16[64,16,1,16]{0,3,1,2:T(8,128)(2,1)S(1)}, bf16[64,16,1,16]{0,3,1,2:T(8,128)(2,1)S(1)}, u32[]{:S(2)}, u32[]{:S(2)}) collective-permute-start(bf16[64,16,1,16]{0,3,1,2:T(8,128)(2,1)S(1)} %fusion.41), channel_id=1, source_target_pairs={{1,0},{3,2},{5,4},{7,6},{9,8},{11,10},{13,12},{15,14},{17,16},{19,... | collective-permute-start | bytes 98312 | tf_op jit(solution)/shard_map/ppermute | solution.py:19
  170.1 2.8 copy-start.14
Sparse Core Ops, SparseCore 0:
  174.2 143.1 all-reduce.7
where the time goes:
time: 330 us; the launch traced here: 329 us
  waiting for transfers between devices  146 us (44%)
  blocking collectives  64.8 us (20%)
  local copies, waits for them, and re-layouts  55.7 us (17%)
  starting transfers between devices  28.4 us (9%)
  between operations  15.6 us (5%)
  matrix products  11.8 us (4%)
  other arithmetic  6.25 us (2%)
    psum x1, waiting for transfers between devices, on_device(): lax.psum((enc_total, dec_total, jnp.einsum('kn,cn->kc', grad_rows, enc_fl...  140 us
    psum x1, blocking collectives, on_device(): lax.psum((enc_total, dec_total, jnp.einsum('kn,cn->kc', grad_rows, enc_fl...  45.2 us
    ppermute x6, starting transfers between devices, padded_2(): lax.ppermute(lax.slice_in_dim(block, block.shape[dim] - width, None, axis...  20.3 us
    all_gather x1, blocking collectives, on_device(): enc_grad = lax.all_gather(enc_grad_own, 'wide', axis=1, tiled=True)  19.6 us
    unnamed x179, local copies, waits for them, and re-layouts  13.7 us
    convert_element_type x3, local copies, waits for them, and re-layouts, upsample(): return up_rows.reshape(ratio, ratio, ratio, fine_ch, planes, depth, width...  8.13 us
    ppermute x6, starting transfers between devices, padded_2(): lax.ppermute(lax.slice_in_dim(block, 0, width, axis=dim), axis, backward)  7.99 us
    transpose x2, local copies, waits for them, and re-layouts, on_device(): grad_rows = up_grad.reshape(fine_ch, own_planes, ratio, depth, ratio, wid...  7.63 us
  transfers between devices with their start and end apart: 13, of which 5 were waited for; matrix products, arithmetic and copies ran while one was open for 6% of the time, Pallas kernels for 0%

commit v1 on v0

v1 whole, which is shorter than its diff:
```python
import functools
import math

import jax
import jax.numpy as jnp
from jax import lax
from jax.experimental import pallas as pl
from jax.experimental.pallas import tpu as pltpu
from jax.sharding import PartitionSpec as P

RATIO = 8
F32 = jnp.float32
BF16 = jnp.bfloat16
VMEM_LIMIT = 48 * 1024 * 1024
VMEM = pltpu.VMEM
AXES = ("wide", "narrow")


def slope_of(values):
    sigma = jax.nn.sigmoid(values)
    return sigma * (1.0 + values * (1.0 - sigma))


def dot(left, right):
    return jnp.dot(left, right, preferred_element_type=F32)


def dot_nt(left, right):
    return lax.dot_general(left, right, (((1,), (1,)), ((), ())), preferred_element_type=F32)


def dot_tn(left, right):
    return lax.dot_general(left, right, (((0,), (0,)), ((), ())), preferred_element_type=F32)


def iota(shape, dim):
    return lax.broadcasted_iota(jnp.int32, shape, dim)


def one_hot(condition):
    return jnp.where(condition, 1.0, 0.0).astype(BF16)


def row_place(rows, columns, fine_ch):
    index = iota((rows, columns), 0)
    return place(index, fine_ch)


def place(index, fine_ch):
    main = fine_ch * RATIO
    over = index - main
    channel = jnp.where(index < main, index // RATIO, over % fine_ch)
    z = jnp.where(index < main, index % RATIO, jnp.where(over < fine_ch, -1, RATIO))
    return channel, z


def lane_shift(values, by):
    width = values.shape[1]
    lane = iota(values.shape, 1)
    if by > 0:
        return jnp.where(lane < by, 0.0, pltpu.roll(values, by, 1))
    return jnp.where(lane >= width + by, 0.0, pltpu.roll(values, width + by, 1))


def three_lanes(values):
    return jnp.concatenate(
        [
            lane_shift(values, 1).astype(BF16),
            values.astype(BF16),
            lane_shift(values, -1).astype(BF16),
        ],
        0,
    )


def prepare_kernel(table_ref, dec_ref, enc_ref, wide_ref, conv_ref, back_ref, enc3_ref):
    fine_ch = dec_ref.shape[1]
    chans = table_ref.shape[-1]
    for i in range(RATIO):
        rows = [
            table_ref[i, :, k].reshape(RATIO * fine_ch, chans) for k in range(RATIO)
        ]
        wide_ref[i] = jnp.concatenate(rows, 1)
    for ab in range(9):
        enc3_ref[ab] = jnp.concatenate([enc_ref[3 * ab + e] for e in range(3)], 1)
    rows = fine_ch * (RATIO + 2)
    columns = fine_ch * (RATIO + 4)
    channel, _ = row_place(rows, fine_ch, fine_ch)
    pick = one_hot(channel == iota((rows, fine_ch), 1))
    spread = one_hot(iota((fine_ch, columns), 0) == iota((fine_ch, columns), 1) % fine_ch)
    _, z_out = row_place(rows, columns, fine_ch)
    z_in = iota((rows, columns), 1) // fine_ch - 2
    pieces = []
    for a in range(3):
        for e in range(3):
            piece = jnp.zeros((rows, columns), F32)
            for b in range(3):
                tap = dot(pick, dec_ref[9 * a + 3 * b + e]).astype(BF16)
                piece = jnp.where(z_in - z_out + 1 == b, dot(tap, spread), piece)
            pieces.append(piece)
    conv_ref[...] = jnp.concatenate(pieces, 1).astype(BF16)
    out_rows = fine_ch * RATIO
    pick = one_hot(iota((out_rows, fine_ch), 0) % fine_ch == iota((out_rows, fine_ch), 1))
    channel, _ = place(iota((fine_ch, rows), 1), fine_ch)
    spread = one_hot(iota((fine_ch, rows), 0) == channel)
    _, z_in = place(iota((out_rows, rows), 1), fine_ch)
    z_out = iota((out_rows, rows), 0) // fine_ch
    pieces = []
    for a in range(3):
        for e in range(3):
            piece = jnp.zeros((out_rows, rows), F32)
            for b in range(3):
                tap = dot_nt(pick, dec_ref[26 - (9 * a + 3 * b + e)]).astype(BF16)
                piece = jnp.where(z_in - z_out + 1 == b, dot(tap, spread), piece)
            pieces.append(piece)
    back_ref[...] = jnp.concatenate(pieces, 1).astype(BF16)


def shifted_rows(values, width):
    count = values.shape[0]
    block = min(count, 256)
    row = iota((block, block), 0)
    column = iota((block, block), 1)
    down = one_hot((column == row - 1) & (row % width > 0))
    up = one_hot((column == row + 1) & (row % width < width - 1))
    pieces = []
    for first in range(0, count, block):
        part = values[first : first + block]
        pieces.append(
            jnp.concatenate([dot(down, part), part.astype(F32), dot(up, part)], 1).astype(BF16)
        )
    return jnp.concatenate(pieces, 0)


def encode_kernel(
    place_ref, dark_ref, enc3_ref, wide_ref, pre_ref, encoded_ref, dark3_ref, up_ref, pad_ref
):
    depth, planes, width, chans = dark_ref.shape
    fine_rows = wide_ref.shape[1]
    fine_ch = fine_rows // RATIO
    dark3_ref[...] = jnp.zeros(dark3_ref.shape, BF16)
    for z in range(depth):
        rows = dark_ref[z].reshape(planes * width, chans)
        dark3_ref[1 : planes + 1, z + 1] = shifted_rows(rows, width).reshape(
            planes, width, 3 * chans
        )
    cells = planes * depth * width
    pre = jnp.zeros((cells, chans), F32)
    for a in range(3):
        for b in range(3):
            window = dark3_ref[a : a + planes, b : b + depth].reshape(cells, 3 * chans)
            pre = pre + dot_nt(window, enc3_ref[3 * a + b])
    pre_ref[...] = pre
    encoded = jax.nn.silu(pre).astype(BF16)
    encoded_ref[...] = encoded
    pad_ref[...] = jnp.zeros(pad_ref.shape, BF16)
    pad_ref[1 : planes + 1, 1 : depth + 1] = encoded.reshape(planes, depth, width, chans)
    first_x = place_ref[0]
    first_z = place_ref[1]
    fine_width = width * RATIO
    repeat = one_hot(
        iota((fine_width, width), 0) // RATIO == iota((fine_width, width), 1)
    )
    tile = one_hot(
        iota((chans, RATIO * chans), 0) == iota((chans, RATIO * chans), 1) % chans
    )
    shape = (fine_width, RATIO * chans)
    mask = iota(shape, 0) % RATIO == iota(shape, 1) // chans
    spread = {}
    for dx in range(3):
        for dz in range(3):
            cell = pad_ref[first_x + dx, first_z + dz]
            tiled = dot(cell, tile).astype(BF16)
            spread[dx, dz] = jnp.where(mask, dot(repeat, tiled), 0.0).astype(BF16)
    margin = 2 * fine_ch
    plan = ((0, range(RATIO - 2, RATIO), 0), (1, range(RATIO), 2), (2, range(2), RATIO + 2))
    for dx, picks, base in plan:
        count = len(picks)
        low = dot_nt(
            jnp.concatenate([wide_ref[i, fine_rows - margin :] for i in picks], 0), spread[dx, 0]
        )
        middle = dot_nt(jnp.concatenate([wide_ref[i] for i in picks], 0), spread[dx, 1])
        high = dot_nt(jnp.concatenate([wide_ref[i, :margin] for i in picks], 0), spread[dx, 2])
        for n in range(count):
            plane = jnp.concatenate(
                [
                    low[n * margin : (n + 1) * margin],
                    middle[n * fine_rows : (n + 1) * fine_rows],
                    high[n * margin : (n + 1) * margin],
                ],
                0,
            )
            up_ref[base + n] = three_lanes(plane)


def decode_kernel(cot_ref, low_ref, high_ref, edge_ref, conv_ref, up_ref, grad_ref, total_ref):
    fine_ch, planes, depth, width = cot_ref.shape
    main = fine_ch * depth
    rows = conv_ref.shape[0]
    taps = up_ref.shape[1]
    keep = []
    for x in range(planes + 2):
        fields = up_ref[x : x + 3].reshape(3 * taps, width)
        pre = dot(conv_ref[...], fields)
        if x == 0:
            inner = low_ref[...]
        elif x == planes + 1:
            inner = high_ref[...]
        else:
            inner = cot_ref[:, x - 1]
        cot = jnp.concatenate(
            [
                inner.astype(F32).reshape(main, width),
                edge_ref[x].astype(F32).reshape(rows - main, width),
            ],
            0,
        )
        grad = (cot * slope_of(pre)).astype(BF16)
        grad_ref[x] = three_lanes(grad.astype(F32))
        if 0 < x <= planes:
            keep.append(grad[:main])
    grads = jnp.concatenate(keep, 1)
    shape = (main, taps)
    span = RATIO + 4
    z_in = (iota(shape, 1) // fine_ch) % span
    z_out = iota(shape, 0) % RATIO
    shape = (taps, 3 * fine_ch)
    fold_row = iota(shape, 0)
    fold = jnp.where(
        (fold_row // (span * fine_ch) == iota(shape, 1) // fine_ch)
        & (fold_row % fine_ch == iota(shape, 1) % fine_ch),
        1.0,
        0.0,
    )
    for a in range(3):
        fields = jnp.concatenate([up_ref[x + a] for x in range(1, planes + 1)], 1)
        product = dot_nt(grads, fields)
        sums = []
        for b in range(3):
            kept = jnp.where(z_in - z_out - 1 == b, product, 0.0)
            sums.append(jnp.sum(kept.reshape(fine_ch, RATIO, taps), 1))
        total_ref[a] = jnp.dot(
            jnp.concatenate(sums, 0),
            fold,
            precision=lax.Precision.HIGHEST,
            preferred_element_type=F32,
        )


def spread_kernel(cot_ref, grad_ref, back_ref, wide_ref, send_ref):
    fine_ch, planes, depth, width = cot_ref.shape
    main = fine_ch * depth
    taps = grad_ref.shape[1]
    chans = wide_ref.shape[2] // RATIO
    owners, chunk, _ = send_ref.shape
    span = chunk - width // RATIO
    row = iota((main, main), 0)
    column = iota((main, main), 1)
    turn = one_hot((row % fine_ch == column // RATIO) & (row // fine_ch == column % RATIO))
    ups = []
    for x in range(planes):
        fields = grad_ref[x : x + 3].reshape(3 * taps, width)
        own = cot_ref[:, x].astype(F32).reshape(main, width).astype(BF16)
        ups.append((dot(back_ref[...], fields) + dot(turn, own)).astype(BF16))
    parts = dot_tn(
        jnp.concatenate(ups, 0), jnp.concatenate([wide_ref[x] for x in range(planes)], 0)
    )
    mask = iota(parts.shape, 0) % RATIO == iota(parts.shape, 1) // chans
    parts = jnp.where(mask, parts, 0.0)
    both = sum(parts[:, n : n + 2 * chans] for n in range(0, RATIO * chans, 2 * chans))
    cell_grad = jnp.sum((both + pltpu.roll(both, chans, 1)).reshape(-1, RATIO, 2 * chans), 1)
    cell_grad = cell_grad.astype(BF16)
    for owner in range(owners):
        first = (owner * RATIO * RATIO // owners) * fine_ch
        send_ref[owner, :span] = ups[first // main][first % main : first % main + span]
        send_ref[owner, span:] = cell_grad


def widen_kernel(encoded_ref, pre_ref, out_ref, slope_ref):
    cells = encoded_ref.shape[0]
    block = 32
    repeat = one_hot(
        iota((block * RATIO, block), 0) // RATIO == iota((block * RATIO, block), 1)
    )
    for first in range(0, cells, block):
        out_ref[first * RATIO : (first + block) * RATIO] = dot(
            repeat, encoded_ref[first : first + block]
        ).astype(BF16)
    slope_ref[...] = slope_of(pre_ref[...])


def finish_kernel(
    place_ref, got_ref, spread_ref, slope_ref, dark3_ref, enc_ref,
    dark_out, enc_out, up_out, pad_ref,
    *, scale,
):
    owners, chunk, fine_width = got_ref.shape
    padded_planes, padded_depth, width, chans3 = dark3_ref.shape
    planes = padded_planes - 2
    depth = padded_depth - 2
    chans = chans3 // 3
    cells = planes * depth * width
    span = chunk - width
    fine_ch = up_out.shape[1]
    arrived = got_ref[:, span:].astype(F32).reshape(cells, fine_width)[:, :chans]
    grad = (arrived * slope_ref[...]).astype(BF16)
    turned = grad.astype(F32).T.astype(BF16)
    for a in range(3):
        for b in range(3):
            window = dark3_ref[a : a + planes, b : b + depth].reshape(cells, chans3)
            product = dot(turned, window) * scale
            for e in range(3):
                enc_out[9 * a + 3 * b + e] = product[:, e * chans : (e + 1) * chans]
    pad_ref[...] = jnp.zeros(pad_ref.shape, BF16)
    pad_ref[1 : planes + 1, 1 : depth + 1] = shifted_rows(grad, width).reshape(
        planes, depth, width, chans3
    )
    own_z = place_ref[1]
    total = jnp.zeros((planes * width, chans), F32)
    for a in range(3):
        for b in range(3):
            window = pad_ref[a : a + planes, own_z + b].reshape(planes * width, chans3)
            first = 26 - (9 * a + 3 * b)
            taps = jnp.concatenate([enc_ref[first - e] for e in range(3)], 0)
            total = total + dot(window, taps)
    dark_out[...] = total.reshape(planes, width, chans)
    pairs = span // fine_ch
    lane = iota((RATIO * fine_ch, fine_width), 1) % RATIO
    masks = one_hot(lane == iota((RATIO * fine_ch, fine_width), 0) // fine_ch)
    step = 8

    def add(block, sums):
        pieces = []
        for n in range(step):
            rows = got_ref[block * step + n, :span]
            pieces.append(
                jnp.concatenate(
                    [
                        jnp.concatenate([rows[p * fine_ch : (p + 1) * fine_ch]] * RATIO, 0) * masks
                        for p in range(pairs)
                    ],
                    0,
                )
            )
        wide = step * fine_width
        field = spread_ref[pl.ds(pl.multiple_of(block * wide, wide), wide)]
        return sums + dot(jnp.concatenate(pieces, 1), field)

    sums = lax.fori_loop(
        0, owners // step, add, jnp.zeros((pairs * RATIO * fine_ch, chans), F32), unroll=True
    )
    up_out[...] = (sums * scale).reshape(pairs * RATIO, fine_ch, chans)


def call(kernel, out_shape, args, scratch=(), scalars=0, flops=1e8):
    specs = [pl.BlockSpec(memory_space=pltpu.SMEM)] * scalars
    specs += [pl.BlockSpec(memory_space=VMEM)] * (len(args) - scalars)
    return pl.pallas_call(
        kernel,
        out_shape=[jax.ShapeDtypeStruct(*s) for s in out_shape],
        in_specs=specs,
        out_specs=[pl.BlockSpec(memory_space=VMEM)] * len(out_shape),
        scratch_shapes=list(scratch),
        compiler_params=pltpu.CompilerParams(vmem_limit_bytes=VMEM_LIMIT),
        cost_estimate=pl.CostEstimate(
            flops=int(flops), bytes_accessed=2_000_000, transcendentals=0
        ),
    )(*args)


def shift(block, axis, by):
    count = lax.axis_size(axis)
    pairs = [(i, i + by) for i in range(count) if 0 <= i + by < count]
    return lax.ppermute(block, axis, pairs)


def sum_over_all(value):
    count = lax.axis_size(AXES)
    if count & (count - 1):
        return lax.psum(value, AXES)
    step = 1
    while step < count:
        value = value + lax.ppermute(value, AXES, [(i, i ^ step) for i in range(count)])
        step *= 2
    return value


def exchange_depth(dark_rows, faces):
    count = lax.axis_size("narrow")
    if count == 2:
        mine = lax.axis_index("narrow")
        swap = [(0, 1), (1, 0)]
        other = lax.ppermute(dark_rows, "narrow", swap)
        face = lax.ppermute(jnp.where(mine == 0, faces[1], faces[0]), "narrow", swap)
        none = jnp.zeros_like(face)
        first = mine == 0
        planes = jnp.stack(
            [jnp.where(first, dark_rows, other), jnp.where(first, other, dark_rows)], 0
        )
        return planes, jnp.where(first, none, face), jnp.where(first, face, none)
    planes = lax.all_gather(dark_rows, "narrow", axis=0)
    return planes, shift(faces[1], "narrow", 1), shift(faces[0], "narrow", -1)


def on_device(dark, w_enc, up_weight, w_dec, cotangent):
    chans, planes, own_depth, width = dark.shape
    fine_ch, own_fine, fine_depth, fine_width = cotangent.shape
    subs = up_weight.shape[0]
    wide_count = lax.axis_size("wide")
    depth = lax.axis_size("narrow")
    owners = wide_count * depth
    cells = planes * depth * width
    own_rows = subs // owners
    where = jnp.stack([lax.axis_index("wide"), lax.axis_index("narrow")]).astype(jnp.int32)

    dark_rows = dark[:, :, 0].transpose(1, 2, 0)
    faces = [cotangent[:, :, z].transpose(1, 0, 2) for z in (0, fine_depth - 1)]
    dark_planes, face_low, face_high = exchange_depth(dark_rows, faces)
    edges = jnp.stack([face_low, face_high], 1)
    x_low = shift(cotangent[:, -1], "wide", 1)
    x_high = shift(cotangent[:, 0], "wide", -1)
    edge_low = shift(edges[-1], "wide", 1)
    edge_high = shift(edges[0], "wide", -1)
    edges = jnp.concatenate([edge_low[None], edges, edge_high[None]], 0)

    rows = fine_ch * (RATIO + 2)
    taps = 3 * fine_ch * (RATIO + 4)
    main = fine_ch * RATIO
    wide_table, conv, back, enc3 = call(
        prepare_kernel,
        [
            ((RATIO, main, RATIO * chans), BF16),
            ((rows, 3 * taps), BF16),
            ((main, 9 * rows), BF16),
            ((9, chans, 3 * chans), BF16),
        ],
        (up_weight.reshape(RATIO, RATIO, RATIO, fine_ch, chans), w_dec, w_enc),
        flops=2e9,
    )
    enc_pre, encoded, dark3, upsampled = call(
        encode_kernel,
        [
            ((cells, chans), F32),
            ((cells, chans), BF16),
            ((planes + 2, depth + 2, width, 3 * chans), BF16),
            ((RATIO + 4, taps, fine_width), BF16),
        ],
        (where, dark_planes, enc3, wide_table),
        scratch=[VMEM((planes + 2, depth + 2, width, chans), BF16)],
        scalars=1,
        flops=2e9,
    )
    dec_grad, dec_part = call(
        decode_kernel,
        [((RATIO + 2, 3 * rows, fine_width), BF16), ((3, 3 * fine_ch, 3 * fine_ch), F32)],
        (cotangent, x_low, x_high, edges, conv, upsampled),
        flops=2e9,
    )
    dec_sum = sum_over_all(dec_part)
    chunk = max(1, RATIO * RATIO // owners) * fine_ch + width
    (send,) = call(
        spread_kernel,
        [((owners, chunk, fine_width), BF16)],
        (cotangent, dec_grad, back, wide_table),
        flops=2e9,
    )
    got = lax.all_to_all(send, AXES, 0, 0, tiled=True)
    enc_spread, enc_slope = call(
        widen_kernel,
        [((cells * RATIO, chans), BF16), ((cells, chans), F32)],
        (encoded, enc_pre),
        flops=1e9,
    )
    coarse_scale = 1.0 / math.sqrt(cells)
    fine_scale = 1.0 / math.sqrt(cells * subs)
    pairs = (chunk - width) // fine_ch
    grad_dark, grad_enc, grad_up = call(
        functools.partial(finish_kernel, scale=coarse_scale),
        [
            ((planes, width, chans), F32),
            ((27, chans, chans), F32),
            ((pairs * RATIO, fine_ch, chans), F32),
        ],
        (where, got, enc_spread, enc_slope, dark3, w_enc),
        scratch=[VMEM((planes + 2, depth + 2, width, 3 * chans), BF16)],
        scalars=1,
        flops=2e9,
    )
    if own_rows < pairs * RATIO:
        own = lax.axis_index(AXES) * own_rows % RATIO
        grad_up = lax.dynamic_slice_in_dim(grad_up, own, own_rows, 0)
    grad_dec = (
        dec_sum.reshape(3, 3, fine_ch, 3, fine_ch)
        .transpose(0, 1, 3, 2, 4)
        .reshape(27, fine_ch, fine_ch)
    ) * fine_scale
    return grad_dark.transpose(2, 0, 1)[:, :, None], grad_enc, grad_up, grad_dec


def solution(mesh):
    in_specs = (P(None, None, "narrow", None), P(), P(), P(), P(None, "wide", "narrow", None))
    out_specs = (P(None, None, "narrow", None), P(), P(("wide", "narrow"), None, None), P())
    return jax.shard_map(
        on_device, mesh=mesh, in_specs=in_specs, out_specs=out_specs, check_vma=False
    )
```

time: 330 us -> 70.2 us (0.21)
  waiting for transfers between devices: 146 us -> 15.6 us
  blocking collectives: 64.8 us -> 0 us
  local copies, waits for them, and re-layouts: 55.7 us -> 7 us
  Pallas kernels: 0 us -> 19.4 us
  between operations: 15.6 us -> 0.88 us
  matrix products: 11.8 us -> 0 us
  other arithmetic: 6.25 us -> 0.24 us
    psum x1 -> x0, waiting for transfers between devices: 140 us -> none  [on_device(): lax.psum((enc_total, dec_total, jnp.einsum('kn,cn->kc', grad_rows, enc_fl...]
    psum x1 -> x0, blocking collectives: 45.2 us -> none  [on_device(): lax.psum((enc_total, dec_total, jnp.einsum('kn,cn->kc', grad_rows, enc_fl...]
    all_gather x1 -> x0, blocking collectives: 19.6 us -> none  [on_device(): enc_grad = lax.all_gather(enc_grad_own, 'wide', axis=1, tiled=True)]
    pallas_call x0 -> x6, Pallas kernels: none -> 19.4 us  [call(): pl.pallas_call(kernel, out_shape=[jax.ShapeDtypeStruct(*s) for s in out_s...]
    dot_general x24 -> x0, matrix products: 11.8 us -> none  [the longest x12 3.08 us: convolve_blocks(): jnp.einsum('ok,kxzy->oxzy', flat, stacked, preferred_element_type=jnp.flo...]
    convert_element_type x4 -> x0, local copies, waits for them, and re-layouts: 9.89 us -> none  [the longest x3 8.13 us: upsample(): return up_rows.reshape(ratio, ratio, ratio, fine_ch, planes, depth, width...]
    ppermute x12 -> x11, starting transfers between devices: 28.3 us -> 18.7 us  [the longest x4 8.6 us: shift(): return lax.ppermute(block, axis, pairs)]
    transpose x5 -> x0, local copies, waits for them, and re-layouts: 9.34 us -> none  [the longest x2 7.63 us: on_device(): grad_rows = up_grad.reshape(fine_ch, own_planes, ratio, depth, ratio, wid...]
  transfers between devices with their start and end apart: 13 -> 12, of which waited for: 5 -> 5; matrix products, arithmetic and copies ran while one was open for 6% -> 9% of each run, Pallas kernels for 0% -> 15%
where the time goes in v1:
time: 70.2 us; the launch traced here: 69.8 us
  starting transfers between devices  26.6 us (38%)
  Pallas kernels  19.4 us (28%)
  waiting for transfers between devices  15.6 us (22%)
  local copies, waits for them, and re-layouts  7 us (10%)
  between operations  0.88 us (1%)
    pallas_call x6, Pallas kernels, call(): pl.pallas_call(kernel, out_shape=[jax.ShapeDtypeStruct(*s) for s in out_s...  19.4 us
    ppermute x5, waiting for transfers between devices, sum_over_all(): lax.ppermute(value, AXES, [(i, i ^ step) for i in range(count)])  15.6 us
    ppermute x4, starting transfers between devices, shift(): return lax.ppermute(block, axis, pairs)  8.6 us
    all_to_all x1, starting transfers between devices, on_device(): got = lax.all_to_all(send, AXES, 0, 0, tiled=True)  7.93 us
    ppermute x5, starting transfers between devices, sum_over_all(): lax.ppermute(value, AXES, [(i, i ^ step) for i in range(count)])  7 us
    unnamed x9, local copies, waits for them, and re-layouts  4.86 us
    ppermute x1, starting transfers between devices, exchange_depth(): other = lax.ppermute(dark_rows, 'narrow', swap)  3 us
  transfers between devices with their start and end apart: 12, of which 5 were waited for; matrix products, arithmetic and copies ran while one was open for 9% of the time, Pallas kernels for 15%

profile of v1, /device:TPU:0, one launch (start us, length us, event | category | flops | bytes accessed | tf_op | source)
XLA Modules:
  0.0 69.8 jit_solution(12286029383659745085)
XLA Ops:
  0.6 0.8 %slice_bitcast_fusion = (bf16[16,8,128]{2,1,0:T(8,128)(2,1)S(1)}, bf16[16,8,128]{2,1,0:T(8,128)(2,1)S(1)}) fusion(bf16[16,8,8,128]{3,2,1,0:T(8,128)(2,1)} %cot_ref.3), kind=kLoop, calls=%fused_computation.9 | loop fusion | bytes 131072 | tf_op jit(solution)/shard_map/squeeze | solution.py:421
  1.4 1.3 %collective-permute-start.1 = (bf16[16,8,128]{2,1,0:T(8,128)(2,1)S(1)}, bf16[16,8,128]{2,1,0:T(8,128)(2,1)S(1)}, u32[]{:S(2)}, u32[]{:S(2)}) collective-permute-start(bf16[16,8,128]{2,1,0:T(8,128)(2,1)S(1)} %get-tuple-element.44), channel_id=1, source_target_pairs={{2,0},{4,2},{6,4},{8,6},{10,8},{12,10},{14,12},{16,14},{18,16},{20... | collective-permute-start | bytes 98312 | tf_op jit(solution)/shard_map/ppermute | solution.py:374
  2.7 3.0 %collective-permute-start = (bf16[16,8,128]{2,1,0:T(8,128)(2,1)S(1)}, bf16[16,8,128]{2,1,0:T(8,128)(2,1)S(1)}, u32[]{:S(2)}, u32[]{:S(2)}) collective-permute-start(bf16[16,8,128]{2,1,0:T(8,128)(2,1)S(1)} %get-tuple-element.45), channel_id=1, source_target_pairs={{0,2},{2,4},{4,6},{6,8},{8,10},{10,12},{12,14},{14,16},{16,18},{18... | collective-permute-start | bytes 98312 | tf_op jit(solution)/shard_map/ppermute | solution.py:374
  5.7 3.0 %collective-permute-start.5 = (bf16[16,16,64]{2,1,0:T(8,128)(2,1)}, bf16[16,16,64]{2,1,0:T(8,128)(2,1)S(1)}, u32[]{:S(2)}, u32[]{:S(2)}) collective-permute-start(bf16[16,16,64]{2,1,0:T(8,128)(2,1)} %bitcast.46), channel_id=1, source_target_pairs={{0,1},{1,0},{2,3},{3,2},{4,5},{5,4},{6,7},{7,6},{8,9},{9,8},{10,11... | collective-permute-start | bytes 98312 | tf_op jit(solution)/shard_map/ppermute | solution.py:393
  8.7 1.2 %fusion.2 = (bf16[16,8,1,128]{3,2,1,0:T(2,128)(2,1)S(1)}, bf16[16,8,1,128]{3,2,1,0:T(2,128)(2,1)S(1)}) fusion(bf16[16,8,8,128]{3,2,1,0:T(8,128)(2,1)} %cot_ref.3), kind=kLoop, calls=%fused_computation.15 | loop fusion | bytes 131072 | tf_op jit(solution)/shard_map/slice | solution.py:417
  9.9 0.0 copy-start.1
  10.0 0.1 collective-permute-start.2
  10.1 1.0 %copy.24.dec_ref = bf16[27,16,16]{2,1,0:T(8,128)(2,1)S(1)} copy(bf16[27,16,16]{0,2,1:T(8,128)(2,1)} %param.8) | data formatting | bytes 27648 | tf_op args[3]
  11.1 3.0 %copy.23 = bf16[512,16,64]{2,1,0:T(8,128)(2,1)S(1)} copy(bf16[512,16,64]{0,2,1:T(8,128)(2,1)} %param.7) | data formatting | bytes 2097152 | tf_op args[2]
  14.1 0.0 copy-done.1
  14.1 0.0 copy-start.2
  14.1 4.7 %shard_map.84 = (bf16[8,128,512]{2,1,0:T(8,128)(2,1)S(1)}, bf16[160,1728]{1,0:T(8,128)(2,1)S(1)}, bf16[128,1440]{1,0:T(8,128)(2,1)S(1)}, bf16[9,64,192]{2,1,0:T(8,128)(2,1)S(1)}) custom-call(bf16[8,8,8,16,64]{4,3,2,1,0:T(8,128)(2,1)S(1)} %bitcast.43, bf16[27,16,16]{2,1,0:T(8,128)(2,1)S(1)} %copy.24.dec_ref, bf16[27,64,64]{2,1,0:T(8,128)(2,1)S(1)} %copy-done.1), custom_call_target="tpu_custom_call" | custom-call | flops 2000000000 | bytes 2000000 | tf_op jit(solution)/shard_map/pallas_call | solution.py:358
  18.9 0.1 pad_add_fusion.place_ref
  18.9 0.0 collective-permute-done.2
  19.0 3.0 %collective-permute-start.3 = (bf16[2,16,128]{2,1,0:T(8,128)(2,1)S(1)}, bf16[2,16,128]{2,1,0:T(8,128)(2,1)S(1)}, u32[]{:S(2)}, u32[]{:S(2)}) collective-permute-start(bf16[2,16,128]{2,1,0:T(8,128)(2,1)S(1)} %get-tuple-element.48), channel_id=1, source_target_pairs={{0,2},{2,4},{4,6},{6,8},{8,10},{10,12},{12,14},{14,16},{16,18},{18... | collective-permute-start | bytes 24584 | tf_op jit(solution)/shard_map/ppermute | solution.py:374
  22.0 1.3 %collective-permute-start.4 = (bf16[2,16,128]{2,1,0:T(8,128)(2,1)S(1)}, bf16[2,16,128]{2,1,0:T(8,128)(2,1)S(1)}, u32[]{:S(2)}, u32[]{:S(2)}) collective-permute-start(bf16[2,16,128]{2,1,0:T(8,128)(2,1)S(1)} %get-tuple-element.49), channel_id=1, source_target_pairs={{2,0},{4,2},{6,4},{8,6},{10,8},{12,10},{14,12},{16,14},{18,16},{20... | collective-permute-start | bytes 24584 | tf_op jit(solution)/shard_map/ppermute | solution.py:374
  23.3 0.0 collective-permute-done.5
  23.3 0.0 copy-done.2
  23.3 0.0 copy-start
  23.4 5.0 %shard_map.85 = (f32[512,64]{1,0:T(8,128)S(1)}, bf16[512,64]{1,0:T(8,128)(2,1)S(1)}, bf16[18,4,16,192]{3,2,1,0:T(8,128)(2,1)S(1)}, bf16[12,576,128]{2,1,0:T(8,128)(2,1)S(1)}) custom-call(s32[2]{0:T(128)S(1)} %pad_add_fusion.place_ref, bf16[2,16,16,64]{3,2,1,0:T(8,128)(2,1)S(1)} %pad_maximum_fusion.dark_ref, ...), custom_call_target="tpu_custom_call" | custom-call | flops 2000000000 | bytes 2000000 | tf_op jit(solution)/shard_map/pallas_call | solution.py:358
  28.4 0.0 collective-permute-done.3
  28.4 0.0 collective-permute-done.4
  28.4 0.0 collective-permute-done.1.high_ref
  28.4 0.0 collective-permute-done.low_ref
  28.4 0.0 copy-done
  28.5 4.0 %shard_map.86 = (bf16[10,480,128]{2,1,0:T(8,128)(2,1)S(1)}, f32[3,48,48]{2,1,0:T(8,128)S(1)}) custom-call(bf16[16,8,8,128]{3,2,1,0:T(8,128)(2,1)S(1)} %copy-done, bf16[16,8,128]{2,1,0:T(8,128)(2,1)S(1)} %collective-permute-done.low_ref, bf16[16,8,128]{2,1,0:T(8,128)(2,1)S(1)} %collective-permute-done.1.high_ref, ...), custom_call_target="tpu_custom_call" | custom-call | flops 2000000000 | bytes 2000000 | tf_op jit(solution)/shard_map/pallas_call | solution.py:358
  32.4 2.1 %shard_map.87 = bf16[32,48,128]{2,1,0:T(8,128)(2,1)} custom-call(bf16[16,8,8,128]{3,2,1,0:T(8,128)(2,1)S(1)} %copy-done, bf16[10,480,128]{2,1,0:T(8,128)(2,1)S(1)} %get-tuple-element.23.grad_ref, bf16[128,1440]{1,0:T(8,128)(2,1)S(1)} %get-tuple-element.24.back_ref, bf16[8,128,512]{2,1,0:T(8,128)(2,1)S(1)} %get-tuple-element.21.wide_ref), custom_call_target="tpu_custom_call" | custom-call | flops 2000000000 | bytes 2000000 | tf_op jit(solution)/shard_map/pallas_call | solution.py:358
  34.5 7.9 %all-to-all-start = ((bf16[32,48,128]{2,1,0:T(8,128)(2,1)}), bf16[32,48,128]{2,1,0:T(8,128)(2,1)S(1)}, u32[]{:S(2)}, u32[]{:S(2)}) async-start(bf16[32,48,128]{2,1,0:T(8,128)(2,1)} %shard_map.87), calls=%async_computation | async-start | bytes 786432 | tf_op jit(solution)/shard_map/all_to_all | solution.py:467
  42.5 1.8 %collective-permute-start.6 = (f32[3,48,48]{2,1,0:T(8,128)S(1)}, f32[3,48,48]{2,1,0:T(8,128)S(1)}, u32[]{:S(2)}, u32[]{:S(2)}) collective-permute-start(f32[3,48,48]{2,1,0:T(8,128)S(1)} %get-tuple-element.33), channel_id=1, source_target_pairs={{0,1},{1,0},{2,3},{3,2},{4,5},{5,4},{6,7},{7,6},{8,9},{9,8},{10,11... | collective-permute-start | bytes 82952 | tf_op jit(solution)/shard_map/ppermute | solution.py:383
  44.3 5.5 %collective-permute-done.6 = f32[3,48,48]{2,1,0:T(8,128)S(1)} collective-permute-done((f32[3,48,48]{2,1,0:T(8,128)S(1)}, f32[3,48,48]{2,1,0:T(8,128)S(1)}, u32[]{:S(2)}, u32[]{:S(2)}) %collective-permute-start.6) | collective-permute-done | bytes 27680 | tf_op jit(solution)/shard_map/ppermute | solution.py:383
  49.8 0.1 collective-permute-start.7
  49.9 1.3 %collective-permute-done.7 = f32[3,48,48]{2,1,0:T(8,128)S(1)} collective-permute-done((f32[3,48,48]{2,1,0:T(8,128)S(1)}, f32[3,48,48]{2,1,0:T(8,128)S(1)}, u32[]{:S(2)}, u32[]{:S(2)}) %collective-permute-start.7) | collective-permute-done | bytes 27680 | tf_op jit(solution)/shard_map/ppermute | solution.py:383
  51.2 1.3 %collective-permute-start.8 = (f32[3,48,48]{2,1,0:T(8,128)S(1)}, f32[3,48,48]{2,1,0:T(8,128)S(1)}, u32[]{:S(2)}, u32[]{:S(2)}) collective-permute-start(f32[3,48,48]{2,1,0:T(8,128)S(1)} %add.16), channel_id=1, source_target_pairs={{0,4},{1,5},{2,6},{3,7},{4,0},{5,1},{6,2},{7,3},{8,12},{9,13},{10,... | collective-permute-start | bytes 82952 | tf_op jit(solution)/shard_map/ppermute | solution.py:383
  52.4 3.4 %collective-permute-done.8 = f32[3,48,48]{2,1,0:T(8,128)S(1)} collective-permute-done((f32[3,48,48]{2,1,0:T(8,128)S(1)}, f32[3,48,48]{2,1,0:T(8,128)S(1)}, u32[]{:S(2)}, u32[]{:S(2)}) %collective-permute-start.8) | collective-permute-done | bytes 27680 | tf_op jit(solution)/shard_map/ppermute | solution.py:383
  55.8 1.4 %collective-permute-start.9 = (f32[3,48,48]{2,1,0:T(8,128)S(1)}, f32[3,48,48]{2,1,0:T(8,128)S(1)}, u32[]{:S(2)}, u32[]{:S(2)}) collective-permute-start(f32[3,48,48]{2,1,0:T(8,128)S(1)} %add.17), channel_id=1, source_target_pairs={{0,8},{1,9},{2,10},{3,11},{4,12},{5,13},{6,14},{7,15},{8,0},{9,1},... | collective-permute-start | bytes 82952 | tf_op jit(solution)/shard_map/ppermute | solution.py:383
  57.3 3.0 %collective-permute-done.9 = f32[3,48,48]{2,1,0:T(8,128)S(1)} collective-permute-done((f32[3,48,48]{2,1,0:T(8,128)S(1)}, f32[3,48,48]{2,1,0:T(8,128)S(1)}, u32[]{:S(2)}, u32[]{:S(2)}) %collective-permute-start.9) | collective-permute-done | bytes 27680 | tf_op jit(solution)/shard_map/ppermute | solution.py:383
  60.3 2.4 %collective-permute-start.10 = (f32[3,48,48]{2,1,0:T(8,128)S(1)}, f32[3,48,48]{2,1,0:T(8,128)S(1)}, u32[]{:S(2)}, u32[]{:S(2)}) collective-permute-start(f32[3,48,48]{2,1,0:T(8,128)S(1)} %add.18), channel_id=1, source_target_pairs={{0,16},{1,17},{2,18},{3,19},{4,20},{5,21},{6,22},{7,23},{8,24},{9,... | collective-permute-start | bytes 82952 | tf_op jit(solution)/shard_map/ppermute | solution.py:383
  62.7 0.5 shard_map.88
  63.1 2.5 %collective-permute-done.10 = f32[3,48,48]{2,1,0:T(8,128)S(1)} collective-permute-done((f32[3,48,48]{2,1,0:T(8,128)S(1)}, f32[3,48,48]{2,1,0:T(8,128)S(1)}, u32[]{:S(2)}, u32[]{:S(2)}) %collective-permute-start.10) | collective-permute-done | bytes 27680 | tf_op jit(solution)/shard_map/ppermute | solution.py:383
  65.6 0.2 mul.17
  65.8 0.8 %copy.27 = f32[27,16,16]{0,2,1:T(8,128)} copy(f32[27,16,16]{2,1,0:T(8,128)S(1)} %bitcast.45) | data formatting | bytes 55296
  66.6 0.0 all-to-all-done.got_ref
  66.6 3.2 %shard_map.89 = (f32[16,16,64]{2,1,0:T(8,128)}, f32[27,64,64]{2,1,0:T(8,128)}, f32[16,16,64]{2,1,0:T(8,128)}) custom-call(s32[2]{0:T(128)S(1)} %pad_add_fusion.place_ref, bf16[32,48,128]{2,1,0:T(8,128)(2,1)S(1)} %all-to-all-done.got_ref, bf16[4096,64]{1,0:T(8,128)(2,1)S(1)} %get-tuple-element.27.spread_ref, f32[512,64]{1,0:T(8,128)S(1)} %get-tuple-element.28.slope_ref, ...), custom_call_target="tpu_custom_call" | custom-call | flops 2000000000 | bytes 2000000 | tf_op jit(solution)/shard_map/pallas_call | solution.py:358
  (12 shorter events, 0.2 us)
Async XLA Ops:
  1.4 27.0 %collective-permute-start.1 = (bf16[16,8,128]{2,1,0:T(8,128)(2,1)S(1)}, bf16[16,8,128]{2,1,0:T(8,128)(2,1)S(1)}, u32[]{:S(2)}, u32[]{:S(2)}) collective-permute-start(bf16[16,8,128]{2,1,0:T(8,128)(2,1)S(1)} %get-tuple-element.44), channel_id=1, source_target_pairs={{2,0},{4,2},{6,4},{8,6},{10,8},{12,10},{14,12},{16,14},{18,16},{20... | collective-permute-start | bytes 98312 | tf_op jit(solution)/shard_map/ppermute | solution.py:374
  2.7 25.7 %collective-permute-start = (bf16[16,8,128]{2,1,0:T(8,128)(2,1)S(1)}, bf16[16,8,128]{2,1,0:T(8,128)(2,1)S(1)}, u32[]{:S(2)}, u32[]{:S(2)}) collective-permute-start(bf16[16,8,128]{2,1,0:T(8,128)(2,1)S(1)} %get-tuple-element.45), channel_id=1, source_target_pairs={{0,2},{2,4},{4,6},{6,8},{8,10},{10,12},{12,14},{14,16},{16,18},{18... | collective-permute-start | bytes 98312 | tf_op jit(solution)/shard_map/ppermute | solution.py:374
  5.7 17.5 %collective-permute-start.5 = (bf16[16,16,64]{2,1,0:T(8,128)(2,1)}, bf16[16,16,64]{2,1,0:T(8,128)(2,1)S(1)}, u32[]{:S(2)}, u32[]{:S(2)}) collective-permute-start(bf16[16,16,64]{2,1,0:T(8,128)(2,1)} %bitcast.46), channel_id=1, source_target_pairs={{0,1},{1,0},{2,3},{3,2},{4,5},{5,4},{6,7},{7,6},{8,9},{9,8},{10,11... | collective-permute-start | bytes 98312 | tf_op jit(solution)/shard_map/ppermute | solution.py:393
  9.9 4.2 %copy-start.1 = (bf16[27,64,64]{2,1,0:T(8,128)(2,1)S(1)}, bf16[27,64,64]{2,1,0:T(8,128)(2,1)}, u32[]{:S(2)}) copy-start(bf16[27,64,64]{2,1,0:T(8,128)(2,1)} %enc_ref.3) | copy-start | bytes 663556
  10.0 9.0 %collective-permute-start.2 = (bf16[8,16,128]{2,1,0:T(8,128)(2,1)S(1)}, bf16[8,16,128]{2,1,0:T(8,128)(2,1)S(1)}, u32[]{:S(2)}, u32[]{:S(2)}) collective-permute-start(bf16[8,16,128]{2,1,0:T(8,128)(2,1)S(1)} %fusion), channel_id=1, source_target_pairs={{0,1},{1,0},{2,3},{3,2},{4,5},{5,4},{6,7},{7,6},{8,9},{9,8},{10,11... | collective-permute-start | bytes 98312 | tf_op jit(solution)/shard_map/ppermute | solution.py:394
  14.1 9.2 %copy-start.2 = (bf16[64,16,1,16]{0,3,2,1:T(8,128)(2,1)S(1)}, bf16[64,16,1,16]{0,3,2,1:T(8,128)(2,1)}, u32[]{:S(2)}) copy-start(bf16[64,16,1,16]{0,3,2,1:T(8,128)(2,1)} %param.5) | copy-start | bytes 98308
  19.0 9.4 %collective-permute-start.3 = (bf16[2,16,128]{2,1,0:T(8,128)(2,1)S(1)}, bf16[2,16,128]{2,1,0:T(8,128)(2,1)S(1)}, u32[]{:S(2)}, u32[]{:S(2)}) collective-permute-start(bf16[2,16,128]{2,1,0:T(8,128)(2,1)S(1)} %get-tuple-element.48), channel_id=1, source_target_pairs={{0,2},{2,4},{4,6},{6,8},{8,10},{10,12},{12,14},{14,16},{16,18},{18... | collective-permute-start | bytes 24584 | tf_op jit(solution)/shard_map/ppermute | solution.py:374
  22.0 6.4 %collective-permute-start.4 = (bf16[2,16,128]{2,1,0:T(8,128)(2,1)S(1)}, bf16[2,16,128]{2,1,0:T(8,128)(2,1)S(1)}, u32[]{:S(2)}, u32[]{:S(2)}) collective-permute-start(bf16[2,16,128]{2,1,0:T(8,128)(2,1)S(1)} %get-tuple-element.49), channel_id=1, source_target_pairs={{2,0},{4,2},{6,4},{8,6},{10,8},{12,10},{14,12},{16,14},{18,16},{20... | collective-permute-start | bytes 24584 | tf_op jit(solution)/shard_map/ppermute | solution.py:374
  23.3 5.1 %copy-start = (bf16[16,8,8,128]{3,2,1,0:T(8,128)(2,1)S(1)}, bf16[16,8,8,128]{3,2,1,0:T(8,128)(2,1)}, u32[]{:S(2)}) copy-start(bf16[16,8,8,128]{3,2,1,0:T(8,128)(2,1)} %cot_ref.3) | copy-start | bytes 786436
  34.5 32.1 %all-to-all-start = ((bf16[32,48,128]{2,1,0:T(8,128)(2,1)}), bf16[32,48,128]{2,1,0:T(8,128)(2,1)S(1)}, u32[]{:S(2)}, u32[]{:S(2)}) async-start(bf16[32,48,128]{2,1,0:T(8,128)(2,1)} %shard_map.87), calls=%async_computation | async-start | bytes 786432 | tf_op jit(solution)/shard_map/all_to_all | solution.py:467
  42.5 7.3 %collective-permute-start.6 = (f32[3,48,48]{2,1,0:T(8,128)S(1)}, f32[3,48,48]{2,1,0:T(8,128)S(1)}, u32[]{:S(2)}, u32[]{:S(2)}) collective-permute-start(f32[3,48,48]{2,1,0:T(8,128)S(1)} %get-tuple-element.33), channel_id=1, source_target_pairs={{0,1},{1,0},{2,3},{3,2},{4,5},{5,4},{6,7},{7,6},{8,9},{9,8},{10,11... | collective-permute-start | bytes 82952 | tf_op jit(solution)/shard_map/ppermute | solution.py:383
  49.8 1.3 %collective-permute-start.7 = (f32[3,48,48]{2,1,0:T(8,128)S(1)}, f32[3,48,48]{2,1,0:T(8,128)S(1)}, u32[]{:S(2)}, u32[]{:S(2)}) collective-permute-start(f32[3,48,48]{2,1,0:T(8,128)S(1)} %add.15), channel_id=1, source_target_pairs={{0,2},{1,3},{2,0},{3,1},{4,6},{5,7},{6,4},{7,5},{8,10},{9,11},{10,... | collective-permute-start | bytes 82952 | tf_op jit(solution)/shard_map/ppermute | solution.py:383
  51.2 4.7 %collective-permute-start.8 = (f32[3,48,48]{2,1,0:T(8,128)S(1)}, f32[3,48,48]{2,1,0:T(8,128)S(1)}, u32[]{:S(2)}, u32[]{:S(2)}) collective-permute-start(f32[3,48,48]{2,1,0:T(8,128)S(1)} %add.16), channel_id=1, source_target_pairs={{0,4},{1,5},{2,6},{3,7},{4,0},{5,1},{6,2},{7,3},{8,12},{9,13},{10,... | collective-permute-start | bytes 82952 | tf_op jit(solution)/shard_map/ppermute | solution.py:383
  55.8 4.4 %collective-permute-start.9 = (f32[3,48,48]{2,1,0:T(8,128)S(1)}, f32[3,48,48]{2,1,0:T(8,128)S(1)}, u32[]{:S(2)}, u32[]{:S(2)}) collective-permute-start(f32[3,48,48]{2,1,0:T(8,128)S(1)} %add.17), channel_id=1, source_target_pairs={{0,8},{1,9},{2,10},{3,11},{4,12},{5,13},{6,14},{7,15},{8,0},{9,1},... | collective-permute-start | bytes 82952 | tf_op jit(solution)/shard_map/ppermute | solution.py:383
  60.3 5.3 %collective-permute-start.10 = (f32[3,48,48]{2,1,0:T(8,128)S(1)}, f32[3,48,48]{2,1,0:T(8,128)S(1)}, u32[]{:S(2)}, u32[]{:S(2)}) collective-permute-start(f32[3,48,48]{2,1,0:T(8,128)S(1)} %add.18), channel_id=1, source_target_pairs={{0,16},{1,17},{2,18},{3,19},{4,20},{5,21},{6,22},{7,23},{8,24},{9,... | collective-permute-start | bytes 82952 | tf_op jit(solution)/shard_map/ppermute | solution.py:383

commit v2 on v1

v2 whole, which is shorter than its diff:
```python
import functools
import math

import jax
import jax.numpy as jnp
from jax import lax
from jax.experimental import pallas as pl
from jax.experimental.pallas import tpu as pltpu
from jax.sharding import PartitionSpec as P

RATIO = 8
SPAN = 16
F32 = jnp.float32
BF16 = jnp.bfloat16
VMEM_LIMIT = 48 * 1024 * 1024
VMEM = pltpu.VMEM
AXES = ("wide", "narrow")


def slope_of(values):
    sigma = jax.nn.sigmoid(values)
    return sigma * (1.0 + values * (1.0 - sigma))


def dot(left, right):
    return jnp.dot(left, right, preferred_element_type=F32)


def dot_nt(left, right):
    return lax.dot_general(left, right, (((1,), (1,)), ((), ())), preferred_element_type=F32)


def dot_tn(left, right):
    return lax.dot_general(left, right, (((0,), (0,)), ((), ())), preferred_element_type=F32)


def iota(shape, dim):
    return lax.broadcasted_iota(jnp.int32, shape, dim)


def one_hot(condition):
    return jnp.where(condition, 1.0, 0.0).astype(BF16)


def place(index, fine_ch):
    main = fine_ch * RATIO
    over = index - main
    channel = jnp.where(index < main, index // RATIO, over % fine_ch)
    z = jnp.where(index < main, index % RATIO, jnp.where(over < fine_ch, -1, RATIO))
    return channel, z


def lane_shift(values, by):
    width = values.shape[1]
    lane = iota(values.shape, 1)
    if by > 0:
        return jnp.where(lane < by, 0.0, pltpu.roll(values, by, 1))
    return jnp.where(lane >= width + by, 0.0, pltpu.roll(values, width + by, 1))


def store_shifts(ref, block, values):
    rows, width = values.shape
    lanes = slice(block * width, (block + 1) * width)
    ref[0:rows, lanes] = lane_shift(values, 1).astype(BF16)
    ref[rows : 2 * rows, lanes] = values.astype(BF16)
    ref[2 * rows : 3 * rows, lanes] = lane_shift(values, -1).astype(BF16)


def prepare_kernel(table_ref, dec_ref, enc_ref, wide_ref, conv_ref, back_ref, encw_ref):
    fine_ch, chans, subs = table_ref.shape
    depth = encw_ref.shape[1] // chans
    pairs = RATIO * RATIO
    row = iota((subs, subs), 0)
    pick = one_hot(iota((subs, subs), 1) == (row % pairs) * RATIO + row // pairs)
    turned = dot_nt(pick, table_ref[...].reshape(fine_ch * chans, subs))
    two = 2 * chans
    low = iota((pairs, two), 1) < chans
    for p in range(fine_ch // 2):
        lanes = slice(p * two, (p + 1) * two)
        for q in range(RATIO // 2):
            even = turned[2 * q * pairs : (2 * q + 1) * pairs, lanes]
            odd = turned[(2 * q + 1) * pairs : (2 * q + 2) * pairs, lanes]
            first = jnp.where(low, even, pltpu.roll(odd, chans, 1))
            second = jnp.where(low, pltpu.roll(even, chans, 1), odd)
            both = jnp.concatenate(
                [first.reshape(RATIO, RATIO, two), second.reshape(RATIO, RATIO, two)], 1
            )
            wide_ref[:, p * SPAN : (p + 1) * SPAN, q * two : (q + 1) * two] = both.astype(BF16)
    blank = jnp.zeros((chans, chans), BF16)
    for a in range(3):
        for z_out in range(depth):
            blocks = []
            for e in range(3):
                for z_in in range(depth):
                    b = z_in - z_out + 1
                    blocks.append(enc_ref[9 * a + 3 * b + e] if 0 <= b < 3 else blank)
            encw_ref[a, z_out * chans : (z_out + 1) * chans] = jnp.concatenate(blocks, 1)
    taps = dec_ref[...].reshape(fine_ch * fine_ch, 27)
    group = 9 * fine_ch
    rows = fine_ch * (RATIO + 2)
    main = fine_ch * RATIO
    square = fine_ch * fine_ch
    tap_row = iota((27, group), 0)
    tap_ae = iota((27, group), 1) // fine_ch
    tap_base = 9 * (tap_ae // 3) + tap_ae % 3
    cell_row = iota((square, group), 0)
    cell_last = iota((square, group), 1) % fine_ch
    same_in = cell_last == cell_row % fine_ch
    same_out = cell_last == cell_row // fine_ch
    channel, _ = place(iota((rows, square), 0), fine_ch)
    pick = one_hot(channel == iota((rows, square), 1) // fine_ch)
    pick_back = one_hot(
        iota((main, square), 0) // RATIO == iota((main, square), 1) % fine_ch
    )
    _, z_out = place(iota((rows, 128), 0), fine_ch)
    offset = iota((rows, 128), 1) % SPAN - 2 - z_out + 1
    wide = group * SPAN
    spread = one_hot(iota((group, wide), 1) // SPAN == iota((group, wide), 0))
    offset = jnp.concatenate([offset] * (wide // 128), 1)
    piece = jnp.zeros((rows, wide), F32)
    backs = [jnp.zeros((main, 3 * rows), F32)] * 3
    spread_back = []
    for a in range(3):
        column = iota((group, 3 * rows), 1)
        channel, _ = place(column % rows, fine_ch)
        spread_back.append(
            one_hot(iota((group, 3 * rows), 0) == (3 * a + column // rows) * fine_ch + channel)
        )
    _, z_in = place(iota((main, 3 * rows), 1) % rows, fine_ch)
    offset_back = z_in - iota((main, 3 * rows), 0) % RATIO + 1
    for b in range(3):
        chosen = dot(taps, one_hot(tap_row == tap_base + 3 * b))
        chosen = dot(pick, jnp.where(same_in, chosen, 0.0).astype(BF16)).astype(BF16)
        piece = jnp.where(offset == b, dot(chosen, spread), piece)
        chosen = dot(taps, one_hot(tap_row == 26 - tap_base - 3 * b))
        chosen = dot(pick_back, jnp.where(same_out, chosen, 0.0).astype(BF16)).astype(BF16)
        backs = [
            jnp.where(offset_back == b, dot(chosen, spread_back[a]), backs[a]) for a in range(3)
        ]
    for a in range(3):
        conv_ref[a] = piece[:, a * (wide // 3) : (a + 1) * (wide // 3)].astype(BF16)
        back_ref[a] = backs[a].astype(BF16)


def shift_rows(values, width):
    count = values.shape[0]
    block = min(count, 256)
    row = iota((block, block), 0)
    column = iota((block, block), 1)
    down = one_hot((column == row - 1) & (row % width > 0))
    up = one_hot((column == row + 1) & (row % width < width - 1))
    pieces = []
    for first in range(0, count, block):
        part = values[first : first + block]
        pieces.append(
            jnp.concatenate([dot(down, part).astype(BF16), part, dot(up, part).astype(BF16)], 1)
        )
    return jnp.concatenate(pieces, 0)


def store_padded(ref, values, width):
    rows, lanes = ref.shape
    ref[0:width] = jnp.zeros((width, lanes), BF16)
    ref[rows - width : rows] = jnp.zeros((width, lanes), BF16)
    ref[width : rows - width] = shift_rows(values, width)


def encode_kernel(
    place_ref, dark_ref, encw_ref, wide_ref, pre_ref, encoded_ref, dark3_ref, up_ref, pad_ref
):
    depth, planes, width, chans = dark_ref.shape
    main = wide_ref.shape[1]
    fine_ch = main // RATIO
    cells = planes * width
    fine_width = width * RATIO
    dark = jnp.concatenate([dark_ref[z].reshape(cells, chans) for z in range(depth)], 1)
    store_padded(dark3_ref, dark, width)
    pre = sum(
        dot_nt(dark3_ref[a * width : a * width + cells], encw_ref[a]) for a in range(3)
    )
    pre_ref[...] = pre
    encoded = jax.nn.silu(pre).astype(BF16)
    encoded_ref[...] = encoded
    pad_ref[...] = jnp.zeros(pad_ref.shape, F32)
    for z in range(depth):
        part = encoded[:, z * chans : (z + 1) * chans].astype(F32)
        pad_ref[1 : planes + 1, z + 1] = jnp.concatenate([part, part], 1).reshape(
            planes, width, 2 * chans
        )
    first_x = place_ref[0]
    first_z = place_ref[1]
    repeat = one_hot(
        iota((fine_width, width), 0) // RATIO == iota((fine_width, width), 1)
    )
    two = 2 * chans
    cells = jnp.concatenate(
        [pad_ref[first_x + dx, first_z + dz] for dx in range(3) for dz in range(3)], 1
    )
    repeated = dot(repeat, cells.astype(BF16))
    lane = iota((fine_width, two), 1) // chans
    phase = iota((fine_width, two), 0) % RATIO
    plan = ((0, RATIO - 2, 2, 0), (1, 0, RATIO, 2), (2, 0, 2, RATIO + 2))
    low = iota((fine_ch, RATIO, fine_width), 1) < 2
    for dx, first, count, base in plan:
        rows = []
        for dz in range(3):
            n = 3 * dx + dz
            cell = repeated[:, n * two : (n + 1) * two]
            rows.append(
                jnp.concatenate(
                    [jnp.where(phase == 2 * q + lane, cell, 0.0) for q in range(RATIO // 2)], 1
                )
            )
        field = dot_nt(
            wide_ref[first : first + count].reshape(count * main, RATIO * chans),
            jnp.concatenate(rows, 0).astype(BF16),
        )
        for n in range(count):
            under, own, over = (
                pltpu.roll(
                    field[n * main : (n + 1) * main, m * fine_width : (m + 1) * fine_width].reshape(
                        fine_ch, RATIO, fine_width
                    ),
                    2,
                    1,
                )
                for m in range(3)
            )
            plane = jnp.concatenate([jnp.where(low, under, own), jnp.where(low, own, over)], 1)
            store_shifts(up_ref, base + n, plane.reshape(fine_ch * SPAN, fine_width))


def decode_kernel(
    cot_ref, low_ref, high_ref, face_ref, corner_ref, conv_ref, up_ref, grad_ref, total_ref
):
    fine_ch, planes, depth, width = cot_ref.shape
    main = fine_ch * depth
    rows = conv_ref.shape[1]
    wide = (planes + 2) * width
    own = planes * width
    pre = sum(dot(conv_ref[a], up_ref[:, a * width : a * width + wide]) for a in range(3))
    row = iota((main, main), 0)
    column = iota((main, main), 1)
    turn = one_hot((row % fine_ch == column // planes) & (row // fine_ch == column % planes))
    faces = [
        dot(turn, face_ref[side].astype(F32).reshape(main, width).astype(BF16))
        for side in range(2)
    ]
    for x in range(planes + 2):
        if x == 0:
            inner = low_ref[...]
            edge = [corner_ref[0, side].astype(F32) for side in range(2)]
        elif x == planes + 1:
            inner = high_ref[...]
            edge = [corner_ref[1, side].astype(F32) for side in range(2)]
        else:
            inner = cot_ref[:, x - 1]
            edge = [face[(x - 1) * fine_ch : x * fine_ch] for face in faces]
        cot = jnp.concatenate([inner.astype(F32).reshape(main, width)] + edge, 0)
        grad = (cot * slope_of(pre[:, x * width : (x + 1) * width])).astype(BF16)
        store_shifts(grad_ref, x, grad.astype(F32))
    grads = jnp.concatenate(
        [grad_ref[e * rows : e * rows + main, width : width + own] for e in range(3)], 0
    )
    taps = fine_ch * SPAN
    shape = (3 * main, taps)
    offset = iota(shape, 1) % SPAN - 2 - iota(shape, 0) % RATIO + 1
    sums = []
    for a in range(3):
        fields = up_ref[taps : 2 * taps, (a + 1) * width : (a + 1) * width + own]
        product = dot_nt(grads, fields)
        for b in range(3):
            kept = jnp.where(offset == b, product, 0.0)
            sums.append(jnp.sum(kept.reshape(3 * fine_ch, RATIO, taps), 1))
    fold = jnp.where(iota((fine_ch, taps), 1) // SPAN == iota((fine_ch, taps), 0), 1.0, 0.0)
    total_ref[...] = lax.dot_general(
        fold,
        jnp.concatenate(sums, 0),
        (((1,), (1,)), ((), ())),
        precision=lax.Precision.HIGHEST,
        preferred_element_type=F32,
    )


def spread_kernel(cot_ref, grad_ref, back_ref, wide_ref, send_ref):
    fine_ch, planes, depth, width = cot_ref.shape
    main = fine_ch * depth
    own = planes * width
    chans = wide_ref.shape[2] // RATIO
    owners, chunk, _ = send_ref.shape
    span = chunk - RATIO
    back = sum(dot(back_ref[a], grad_ref[:, a * width : a * width + own]) for a in range(3))
    cot = jnp.concatenate(
        [cot_ref[:, x].astype(F32).reshape(main, width) for x in range(planes)], 1
    )
    up = (cot + back).astype(BF16)
    row = iota((main, main), 0)
    column = iota((main, main), 1)
    turn = one_hot((row % fine_ch == column // RATIO) & (row // fine_ch == column % RATIO))
    turned = dot(turn, up).astype(BF16)
    parts = dot_tn(
        jnp.concatenate([up[:, x * width : (x + 1) * width] for x in range(planes)], 0),
        wide_ref[...].reshape(planes * main, RATIO * chans),
    )
    two = 2 * chans
    phase = iota((width, two), 0) % RATIO
    lane = iota((width, two), 1) // chans
    both = sum(
        jnp.where(phase == 2 * q + lane, parts[:, q * two : (q + 1) * two], 0.0)
        for q in range(RATIO // 2)
    )
    cells = jnp.sum((both + pltpu.roll(both, chans, 1)).reshape(-1, RATIO, two), 1)
    half = cells.shape[0] // 2
    cells = jnp.where(iota((half, two), 1) < chans, cells[:half], cells[half:]).astype(BF16)
    for owner in range(owners):
        first = owner * RATIO * RATIO // owners
        x = first // RATIO
        top = first % RATIO * fine_ch
        send_ref[owner, :span] = turned[top : top + span, x * width : (x + 1) * width]
        send_ref[owner, span:] = cells


def widen_kernel(place_ref, encoded_ref, pre_ref, enc_ref, out_ref, slope_ref, taps_ref):
    cells, lanes = encoded_ref.shape
    chans = enc_ref.shape[1]
    depth = lanes // chans
    block = 32
    repeat = one_hot(
        iota((block * RATIO, block), 0) // RATIO == iota((block * RATIO, block), 1)
    )
    for first in range(0, cells, block):
        out_ref[first * RATIO : (first + block) * RATIO] = dot(
            repeat, encoded_ref[first : first + block]
        ).astype(BF16)
    slope_ref[...] = slope_of(pre_ref[...])
    own_z = place_ref[1]
    for a in range(3):
        for e in range(3):
            for z in range(depth):
                b = z - own_z + 1
                tap = enc_ref[26 - (9 * a + 3 * jnp.clip(b, 0, 2) + e)]
                first = (3 * e * depth + 3 * z) * chans // 3
                taps_ref[a, first : first + chans] = jnp.where(
                    (b >= 0) & (b <= 2), tap.astype(F32), 0.0
                ).astype(BF16)


def finish_kernel(
    got_ref, spread_ref, slope_ref, dark3_ref, taps_ref, dark_out, enc_out, up_out, pad_ref, *, scale
):
    owners, chunk, fine_width = got_ref.shape
    cells, lanes = slope_ref.shape
    chans = taps_ref.shape[2]
    depth = lanes // chans
    planes = owners // depth
    width = cells // planes
    span = chunk - RATIO
    fine_ch = up_out.shape[1]
    rows = []
    for x in range(planes):
        parts = [got_ref[x * depth + z, span:].astype(F32) for z in range(depth)]
        for half in range(2):
            rows.append(
                jnp.concatenate([part[:, half * chans : (half + 1) * chans] for part in parts], 1)
            )
    grad = (jnp.concatenate(rows, 0) * slope_ref[...]).astype(BF16)
    store_padded(pad_ref, grad, width)
    dark_out[...] = sum(
        dot(pad_ref[a * width : a * width + cells], taps_ref[a]) for a in range(3)
    ).reshape(planes, width, chans)
    turned = grad.astype(F32).T.astype(BF16)
    for a in range(3):
        product = dot(turned, dark3_ref[a * width : a * width + cells]) * scale
        for b in range(3):
            for e in range(3):
                total = None
                for z in range(depth):
                    z_in = z + b - 1
                    if 0 <= z_in < depth:
                        first = (e * depth + z_in) * chans
                        part = product[z * chans : (z + 1) * chans, first : first + chans]
                        total = part if total is None else total + part
                enc_out[9 * a + 3 * b + e] = (
                    jnp.zeros((chans, chans), F32) if total is None else total
                )
    pairs = span // fine_ch
    lane = iota((RATIO * fine_ch, fine_width), 1) % RATIO
    masks = one_hot(lane == iota((RATIO * fine_ch, fine_width), 0) // fine_ch)
    sums = None
    for z in range(depth):
        pieces = []
        for x in range(planes):
            arrived = got_ref[x * depth + z, :span]
            pieces.append(
                jnp.concatenate(
                    [
                        jnp.concatenate([arrived[p * fine_ch : (p + 1) * fine_ch]] * RATIO, 0)
                        * masks
                        for p in range(pairs)
                    ],
                    0,
                )
            )
        part = dot(jnp.concatenate(pieces, 1), spread_ref[...])
        part = part[:, z * chans : (z + 1) * chans]
        sums = part if sums is None else sums + part
    up_out[...] = (sums * scale).reshape(pairs * RATIO, fine_ch, chans)


def call(kernel, out_shape, args, scratch=(), scalars=0, flops=1e8):
    specs = [pl.BlockSpec(memory_space=pltpu.SMEM)] * scalars
    specs += [pl.BlockSpec(memory_space=VMEM)] * (len(args) - scalars)
    return pl.pallas_call(
        kernel,
        out_shape=[jax.ShapeDtypeStruct(*s) for s in out_shape],
        in_specs=specs,
        out_specs=[pl.BlockSpec(memory_space=VMEM)] * len(out_shape),
        scratch_shapes=list(scratch),
        compiler_params=pltpu.CompilerParams(vmem_limit_bytes=VMEM_LIMIT),
        cost_estimate=pl.CostEstimate(
            flops=int(flops), bytes_accessed=2_000_000, transcendentals=0
        ),
    )(*args)


def shift(block, axis, by):
    count = lax.axis_size(axis)
    pairs = [(i, i + by) for i in range(count) if 0 <= i + by < count]
    return lax.ppermute(block, axis, pairs)


def sum_step(value, step):
    count = lax.axis_size(AXES)
    return value + lax.ppermute(value, AXES, [(i, i ^ step) for i in range(count)])


def exchange_depth(dark_rows, cotangent):
    count = lax.axis_size("narrow")
    last = cotangent.shape[2] - 1
    if count == 2:
        first = lax.axis_index("narrow") == 0
        swap = [(0, 1), (1, 0)]
        other = lax.ppermute(dark_rows, "narrow", swap)
        face = lax.dynamic_index_in_dim(cotangent, jnp.where(first, last, 0), 2, False)
        face = lax.ppermute(face, "narrow", swap)
        none = jnp.zeros_like(face)
        planes = jnp.stack(
            [jnp.where(first, dark_rows, other), jnp.where(first, other, dark_rows)], 0
        )
        low, high = jnp.where(first, none, face), jnp.where(first, face, none)
    else:
        planes = lax.all_gather(dark_rows, "narrow", axis=0)
        low = shift(cotangent[:, :, last], "narrow", 1)
        high = shift(cotangent[:, :, 0], "narrow", -1)
    return planes, jnp.stack([low, high], 0)


def exchange_width(cotangent, faces):
    count = lax.axis_size("wide")
    last = cotangent.shape[1] - 1
    even = lax.axis_index("wide") % 2 == 0
    got = []
    for odd, plane in ((0, jnp.where(even, last, 0)), (1, jnp.where(even, 0, last))):
        pairs = [(i, i + 1) for i in range(odd, count - 1, 2)]
        pairs += [(target, source) for source, target in pairs]
        send = (
            lax.dynamic_index_in_dim(cotangent, plane, 1, False),
            lax.dynamic_index_in_dim(faces, plane, 2, False),
        )
        got.append([lax.ppermute(part, "wide", pairs) for part in send])
    low = [jnp.where(even, second, first) for first, second in zip(*got)]
    high = [jnp.where(even, first, second) for first, second in zip(*got)]
    return low[0], high[0], jnp.stack([low[1], high[1]], 0)


def on_device(dark, w_enc, up_weight, w_dec, cotangent):
    chans, planes, own_depth, width = dark.shape
    fine_ch, own_fine, fine_depth, fine_width = cotangent.shape
    subs = up_weight.shape[0]
    depth = lax.axis_size("narrow")
    owners = lax.axis_size(AXES)
    cells = planes * width
    lanes = depth * chans
    own_rows = subs // owners
    where = jnp.stack([lax.axis_index("wide"), lax.axis_index("narrow")]).astype(jnp.int32)

    dark_planes, faces = exchange_depth(dark[:, :, 0].transpose(1, 2, 0), cotangent)
    x_low, x_high, corners = exchange_width(cotangent, faces)

    rows = fine_ch * (RATIO + 2)
    taps = fine_ch * SPAN
    main = fine_ch * RATIO
    wide_table, conv, back, enc_weights = call(
        prepare_kernel,
        [
            ((RATIO, main, RATIO * chans), BF16),
            ((3, rows, 3 * taps), BF16),
            ((3, main, 3 * rows), BF16),
            ((3, lanes, 3 * lanes), BF16),
        ],
        (up_weight.transpose(1, 2, 0), w_dec.transpose(1, 2, 0), w_enc),
        flops=2e9,
    )
    enc_pre, encoded, dark3, upsampled = call(
        encode_kernel,
        [
            ((cells, lanes), F32),
            ((cells, lanes), BF16),
            ((cells + 2 * width, 3 * lanes), BF16),
            ((3 * taps, (RATIO + 4) * fine_width), BF16),
        ],
        (where, dark_planes, enc_weights, wide_table),
        scratch=[VMEM((planes + 2, depth + 2, width, 2 * chans), F32)],
        scalars=1,
        flops=2e9,
    )
    dec_grad, dec_sum = call(
        decode_kernel,
        [((3 * rows, (RATIO + 2) * fine_width), BF16), ((fine_ch, 27 * fine_ch), F32)],
        (cotangent, x_low, x_high, faces, corners, conv, upsampled),
        flops=2e9,
    )
    chunk = max(1, RATIO * RATIO // owners) * fine_ch + RATIO
    (send,) = call(
        spread_kernel,
        [((owners, chunk, fine_width), BF16)],
        (cotangent, dec_grad, back, wide_table),
        flops=2e9,
    )
    steps = [1 << n for n in range(owners.bit_length() - 1)]
    if owners & (owners - 1):
        dec_sum = lax.psum(dec_sum, AXES)
        steps = []
    steps = sorted(steps, key=lambda step: (step != depth, step))
    for step in steps[:1]:
        dec_sum = sum_step(dec_sum, step)
    send, dec_sum = lax.optimization_barrier((send, dec_sum))
    got = lax.all_to_all(send, AXES, 0, 0, tiled=True)
    for step in steps[1:]:
        dec_sum = sum_step(dec_sum, step)
    enc_spread, enc_slope, enc_taps = call(
        widen_kernel,
        [
            ((cells * RATIO, lanes), BF16),
            ((cells, lanes), F32),
            ((3, 3 * lanes, chans), BF16),
        ],
        (where, encoded, enc_pre, w_enc),
        scalars=1,
        flops=1e9,
    )
    coarse_scale = 1.0 / math.sqrt(cells * depth)
    fine_scale = 1.0 / math.sqrt(cells * depth * subs)
    pairs = (chunk - RATIO) // fine_ch
    grad_dark, grad_enc, grad_up = call(
        functools.partial(finish_kernel, scale=coarse_scale),
        [
            ((planes, width, chans), F32),
            ((27, chans, chans), F32),
            ((pairs * RATIO, fine_ch, chans), F32),
        ],
        (got, enc_spread, enc_slope, dark3, enc_taps),
        scratch=[VMEM((cells + 2 * width, 3 * lanes), BF16)],
        flops=2e9,
    )
    if own_rows < pairs * RATIO:
        own = lax.axis_index(AXES) * own_rows % RATIO
        grad_up = lax.dynamic_slice_in_dim(grad_up, own, own_rows, 0)
    grad_dec = (
        dec_sum.reshape(fine_ch, 3, 3, 3, fine_ch)[:, :, :, ::-1]
        .transpose(1, 2, 3, 4, 0)
        .reshape(27, fine_ch, fine_ch)
    ) * fine_scale
    return grad_dark.transpose(2, 0, 1)[:, :, None], grad_enc, grad_up, grad_dec


def solution(mesh):
    in_specs = (P(None, None, "narrow", None), P(), P(), P(), P(None, "wide", "narrow", None))
    out_specs = (P(None, None, "narrow", None), P(), P(("wide", "narrow"), None, None), P())
    return jax.shard_map(
        on_device, mesh=mesh, in_specs=in_specs, out_specs=out_specs, check_vma=False
    )
```

time: 70.2 us -> 55.1 us (0.78)
  waiting for transfers between devices: 15.6 us -> 9.1 us
  Pallas kernels: 19.4 us -> 14.1 us
  starting transfers between devices: 26.6 us -> 23.6 us
    ppermute x10, waiting for transfers between devices: 15.6 us -> 9.1 us  [the longest x5 9.09 us: sum_step(): lax.ppermute(value, AXES, [(i, i ^ step) for i in range(count)])]
    pallas_call x6, Pallas kernels: 19.4 us -> 14.1 us  [call(): pl.pallas_call(kernel, out_shape=[jax.ShapeDtypeStruct(*s) for s in out_s...]
    ppermute x1, starting transfers between devices: 3 us -> 0.1 us  [exchange_depth(): other = lax.ppermute(dark_rows, 'narrow', swap)]
    all_to_all x1, starting transfers between devices: 7.93 us -> 5.1 us  [on_device(): got = lax.all_to_all(send, AXES, 0, 0, tiled=True)]
    ppermute x10, starting transfers between devices: 15.7 us -> 18.4 us  [the longest x5 11 us: sum_step(): lax.ppermute(value, AXES, [(i, i ^ step) for i in range(count)])]
    slice x1 -> x0, local copies, waits for them, and re-layouts: 1.18 us -> none  [on_device(): faces = [cotangent[:, :, z].transpose(1, 0, 2) for z in (0, fine_depth - 1)]]
    dynamic_slice x0 -> x1, local copies, waits for them, and re-layouts: none -> 1.03 us  [exchange_depth(): lax.dynamic_index_in_dim(cotangent, jnp.where(first, last, 0), 2, False)]
    unnamed x9 -> x16, local copies, waits for them, and re-layouts: 4.86 us -> 3.94 us
  transfers between devices with their start and end apart: 12 -> 12, of which waited for: 5 -> 4; matrix products, arithmetic and copies ran while one was open for 9% -> 5% of each run, Pallas kernels for 15% -> 16%
where the time goes in v2:
time: 55.1 us; the launch traced here: 54.7 us
  starting transfers between devices  23.6 us (43%)
  Pallas kernels  14.1 us (26%)
  waiting for transfers between devices  9.1 us (17%)
  local copies, waits for them, and re-layouts  6.62 us (12%)
  between operations  0.88 us (2%)
    pallas_call x6, Pallas kernels, call(): pl.pallas_call(kernel, out_shape=[jax.ShapeDtypeStruct(*s) for s in out_s...  14.1 us
    ppermute x5, starting transfers between devices, sum_step(): lax.ppermute(value, AXES, [(i, i ^ step) for i in range(count)])  11 us
    ppermute x5, waiting for transfers between devices, sum_step(): lax.ppermute(value, AXES, [(i, i ^ step) for i in range(count)])  9.09 us
    all_to_all x1, starting transfers between devices, on_device(): got = lax.all_to_all(send, AXES, 0, 0, tiled=True)  5.1 us
    ppermute x4, starting transfers between devices, exchange_width(): got.append([lax.ppermute(part, 'wide', pairs) for part in send])  4.48 us
    unnamed x16, local copies, waits for them, and re-layouts  3.94 us
    ppermute x1, starting transfers between devices, exchange_depth(): face = lax.ppermute(face, 'narrow', swap)  3 us
  transfers between devices with their start and end apart: 12, of which 4 were waited for; matrix products, arithmetic and copies ran while one was open for 5% of the time, Pallas kernels for 16%

profile of v2, /device:TPU:0, one launch (start us, length us, event | category | flops | bytes accessed | tf_op | source)
XLA Modules:
  0.0 54.7 jit_solution(9560290288631211821)
XLA Ops:
  0.6 1.0 %constant_dynamic-slice_fusion = bf16[16,8,1,128]{3,2,1,0:T(2,128)(2,1)S(1)} fusion(bf16[16,8,8,128]{3,2,1,0:T(8,128)(2,1)} %cot_ref.3, s32[]{:T(128)S(6)} %select_n.78), kind=kLoop, calls=%fused_computation.23 | loop fusion | bytes 65540 | tf_op jit(solution)/shard_map/jit(dynamic_index_in_dim)/dynamic_slice | solution.py:444
  1.7 3.0 %collective-permute-start.2 = (bf16[16,8,128]{2,1,0:T(8,128)(2,1)S(1)}, bf16[16,8,128]{2,1,0:T(8,128)(2,1)S(1)}, u32[]{:S(2)}, u32[]{:S(2)}) collective-permute-start(bf16[16,8,128]{2,1,0:T(8,128)(2,1)S(1)} %bitcast.46), channel_id=1, source_target_pairs={{0,1},{1,0},{2,3},{3,2},{4,5},{5,4},{6,7},{7,6},{8,9},{9,8},{10,11... | collective-permute-start | bytes 98312 | tf_op jit(solution)/shard_map/ppermute | solution.py:445
  4.7 0.8 %dynamic-slice_bitcast_fusion = (bf16[16,8,128]{2,1,0:T(8,128)(2,1)S(1)}, bf16[16,8,128]{2,1,0:T(8,128)(2,1)S(1)}) fusion(bf16[16,8,8,128]{3,2,1,0:T(8,128)(2,1)} %cot_ref.3, s32[]{:T(128)S(6)} %select_n.74, s32[]{:T(128)S(6)} %select_n.73), kind=kLoop, calls=%fused_computation.12 | loop fusion | bytes 131080 | tf_op jit(solution)/shard_map/jit(dynamic_index_in_dim)/squeeze | solution.py:467
  5.5 0.0 collective-permute-start.1
  5.5 0.7 %collective-permute-start = (bf16[16,8,128]{2,1,0:T(8,128)(2,1)S(1)}, bf16[16,8,128]{2,1,0:T(8,128)(2,1)S(1)}, u32[]{:S(2)}, u32[]{:S(2)}) collective-permute-start(bf16[16,8,128]{2,1,0:T(8,128)(2,1)S(1)} %get-tuple-element.49), channel_id=1, source_target_pairs={{2,4},{6,8},{10,12},{14,16},{18,20},{22,24},{26,28},{4,2},{8,6},{1... | collective-permute-start | bytes 98312 | tf_op jit(solution)/shard_map/ppermute | solution.py:470
  6.1 0.1 collective-permute-start.5
  6.2 0.0 copy-start.1
  6.3 1.2 %copy-done.1 = bf16[512,16,64]{0,2,1:T(8,128)(2,1)S(1)} copy-done((bf16[512,16,64]{0,2,1:T(8,128)(2,1)S(1)}, bf16[512,16,64]{0,2,1:T(8,128)(2,1)}, u32[]{:S(2)}) %copy-start.1) | copy-done | bytes 1048600
  7.5 0.0 copy-start.2
  7.5 1.0 %copy-done.2 = bf16[27,64,64]{2,1,0:T(8,128)(2,1)S(1)} copy-done((bf16[27,64,64]{2,1,0:T(8,128)(2,1)S(1)}, bf16[27,64,64]{2,1,0:T(8,128)(2,1)}, u32[]{:S(2)}) %copy-start.2) | copy-done | bytes 221208
  8.5 0.0 copy-start.4
  8.5 0.8 %copy-done.4 = bf16[27,16,16]{0,2,1:T(8,128)(2,1)S(1)} copy-done((bf16[27,16,16]{0,2,1:T(8,128)(2,1)S(1)}, bf16[27,16,16]{0,2,1:T(8,128)(2,1)}, u32[]{:S(2)}) %copy-start.4) | copy-done | bytes 13848
  9.3 3.6 %shard_map.84 = (bf16[8,128,512]{2,1,0:T(8,128)(2,1)S(1)}, bf16[3,160,768]{2,1,0:T(8,128)(2,1)S(1)}, bf16[3,128,480]{2,1,0:T(8,128)(2,1)S(1)}, bf16[3,128,384]{2,1,0:T(8,128)(2,1)S(1)}) custom-call(bf16[16,64,512]{2,1,0:T(8,128)(2,1)S(1)} %bitcast.42, bf16[16,16,27]{2,1,0:T(8,128)(2,1)S(1)} %bitcast.43, bf16[27,64,64]{2,1,0:T(8,128)(2,1)S(1)} %copy-done.2), custom_call_target="tpu_custom_call" | custom-call | flops 2000000000 | bytes 2000000 | tf_op jit(solution)/shard_map/pallas_call | solution.py:413
  12.9 0.1 pad_add_fusion.place_ref
  13.0 0.0 collective-permute-done.2
  13.1 3.2 %collective-permute-start.4 = (bf16[2,16,128]{2,1,0:T(8,128)(2,1)S(1)}, bf16[2,16,128]{2,1,0:T(8,128)(2,1)S(1)}, u32[]{:S(2)}, u32[]{:S(2)}) collective-permute-start(bf16[2,16,128]{2,1,0:T(8,128)(2,1)S(1)} %bitcast.48), channel_id=1, source_target_pairs={{0,2},{4,6},{8,10},{12,14},{16,18},{20,22},{24,26},{28,30},{2,0},{... | collective-permute-start | bytes 24584 | tf_op jit(solution)/shard_map/ppermute | solution.py:470
  16.2 0.6 %collective-permute-start.3 = (bf16[2,16,128]{2,1,0:T(8,128)(2,1)S(1)}, bf16[2,16,128]{2,1,0:T(8,128)(2,1)S(1)}, u32[]{:S(2)}, u32[]{:S(2)}) collective-permute-start(bf16[2,16,128]{2,1,0:T(8,128)(2,1)S(1)} %bitcast.47), channel_id=1, source_target_pairs={{2,4},{6,8},{10,12},{14,16},{18,20},{22,24},{26,28},{4,2},{8,6},{1... | collective-permute-start | bytes 24584 | tf_op jit(solution)/shard_map/ppermute | solution.py:470
  16.9 0.0 collective-permute-done.5
  16.9 0.0 copy-done.5
  17.0 0.0 copy-start
  17.0 2.5 %shard_map.85 = (f32[256,128]{1,0:T(8,128)S(1)}, bf16[256,128]{1,0:T(8,128)(2,1)S(1)}, bf16[288,384]{1,0:T(8,128)(2,1)S(1)}, bf16[768,1536]{1,0:T(8,128)(2,1)S(1)}) custom-call(s32[2]{0:T(128)S(1)} %pad_add_fusion.place_ref, bf16[2,16,16,64]{3,2,1,0:T(8,128)(2,1)S(1)} %pad_maximum_fusion.dark_ref, bf16[3,128,384]{2,1,0:T(8,128)(2,1)S(1)} %get-tuple-element.23.encw_ref, ...), custom_call_target="tpu_custom_call" | custom-call | flops 2000000000 | bytes 2000000 | tf_op jit(solution)/shard_map/pallas_call | solution.py:413
  19.5 0.0 collective-permute-done.1
  19.6 0.0 collective-permute-done
  19.6 0.0 collective-permute-done.4
  19.6 0.0 collective-permute-done.3
  19.6 0.0 copy-done
  19.7 3.2 %shard_map.86 = (bf16[480,1280]{1,0:T(8,128)(2,1)S(1)}, f32[16,432]{1,0:T(8,128)S(1)}) custom-call(bf16[16,8,8,128]{3,2,1,0:T(8,128)(2,1)S(1)} %copy-done, bf16[16,8,128]{2,1,0:T(8,128)(2,1)S(1)} %get-tuple-element.55.low_ref, bf16[16,8,128]{2,1,0:T(8,128)(2,1)S(1)} %get-tuple-element.54.high_ref, bf16[2,16,8,128]{3,2,1,0:T(8,128)(2,1)S(1)} %pad_maximum_fusion.1.face_ref, ...), custom_call_target="tpu_custom_call" | custom-call | flops 2000000000 | bytes 2000000 | tf_op jit(solution)/shard_map/pallas_call | solution.py:413
  22.9 2.9 %collective-permute-start.6 = (f32[16,432]{1,0:T(8,128)S(1)}, f32[16,432]{1,0:T(8,128)S(1)}, u32[]{:S(2)}, u32[]{:S(2)}) collective-permute-start(f32[16,432]{1,0:T(8,128)S(1)} %get-tuple-element.28), channel_id=1, source_target_pairs={{0,2},{1,3},{2,0},{3,1},{4,6},{5,7},{6,4},{7,5},{8,10},{9,11},{10,... | collective-permute-start | bytes 82952 | tf_op jit(solution)/shard_map/ppermute | solution.py:434
  25.8 1.7 %shard_map.87 = bf16[32,40,128]{2,1,0:T(8,128)(2,1)} custom-call(bf16[16,8,8,128]{3,2,1,0:T(8,128)(2,1)S(1)} %copy-done, bf16[480,1280]{1,0:T(8,128)(2,1)S(1)} %get-tuple-element.26.grad_ref, bf16[3,128,480]{2,1,0:T(8,128)(2,1)S(1)} %get-tuple-element.27.back_ref, bf16[8,128,512]{2,1,0:T(8,128)(2,1)S(1)} %get-tuple-element.24.wide_ref), custom_call_target="tpu_custom_call" | custom-call | flops 2000000000 | bytes 2000000 | tf_op jit(solution)/shard_map/pallas_call | solution.py:413
  27.5 0.0 collective-permute-done.6
  27.6 5.1 %all-to-all-start = ((bf16[32,40,128]{2,1,0:T(8,128)(2,1)}), bf16[32,40,128]{2,1,0:T(8,128)(2,1)S(1)}, u32[]{:S(2)}, u32[]{:S(2)}) async-start(bf16[32,40,128]{2,1,0:T(8,128)(2,1)} %shard_map.87), calls=%async_computation | async-start | bytes 655360 | tf_op jit(solution)/shard_map/all_to_all | solution.py:538
  32.7 1.8 %collective-permute-start.7 = (f32[16,432]{1,0:T(8,128)S(1)}, f32[16,432]{1,0:T(8,128)S(1)}, u32[]{:S(2)}, u32[]{:S(2)}) collective-permute-start(f32[16,432]{1,0:T(8,128)S(1)} %add.28), channel_id=1, source_target_pairs={{0,1},{1,0},{2,3},{3,2},{4,5},{5,4},{6,7},{7,6},{8,9},{9,8},{10,11... | collective-permute-start | bytes 82952 | tf_op jit(solution)/shard_map/ppermute | solution.py:434
  34.5 3.3 %collective-permute-done.7 = f32[16,432]{1,0:T(8,128)S(1)} collective-permute-done((f32[16,432]{1,0:T(8,128)S(1)}, f32[16,432]{1,0:T(8,128)S(1)}, u32[]{:S(2)}, u32[]{:S(2)}) %collective-permute-start.7) | collective-permute-done | bytes 27680 | tf_op jit(solution)/shard_map/ppermute | solution.py:434
  37.8 1.4 %collective-permute-start.8 = (f32[16,432]{1,0:T(8,128)S(1)}, f32[16,432]{1,0:T(8,128)S(1)}, u32[]{:S(2)}, u32[]{:S(2)}) collective-permute-start(f32[16,432]{1,0:T(8,128)S(1)} %add.29), channel_id=1, source_target_pairs={{0,4},{1,5},{2,6},{3,7},{4,0},{5,1},{6,2},{7,3},{8,12},{9,13},{10,... | collective-permute-start | bytes 82952 | tf_op jit(solution)/shard_map/ppermute | solution.py:434
  39.2 2.6 %collective-permute-done.8 = f32[16,432]{1,0:T(8,128)S(1)} collective-permute-done((f32[16,432]{1,0:T(8,128)S(1)}, f32[16,432]{1,0:T(8,128)S(1)}, u32[]{:S(2)}, u32[]{:S(2)}) %collective-permute-start.8) | collective-permute-done | bytes 27680 | tf_op jit(solution)/shard_map/ppermute | solution.py:434
  41.8 1.8 %collective-permute-start.9 = (f32[16,432]{1,0:T(8,128)S(1)}, f32[16,432]{1,0:T(8,128)S(1)}, u32[]{:S(2)}, u32[]{:S(2)}) collective-permute-start(f32[16,432]{1,0:T(8,128)S(1)} %add.30), channel_id=1, source_target_pairs={{0,8},{1,9},{2,10},{3,11},{4,12},{5,13},{6,14},{7,15},{8,0},{9,1},... | collective-permute-start | bytes 82952 | tf_op jit(solution)/shard_map/ppermute | solution.py:434
  43.5 2.1 %collective-permute-done.9 = f32[16,432]{1,0:T(8,128)S(1)} collective-permute-done((f32[16,432]{1,0:T(8,128)S(1)}, f32[16,432]{1,0:T(8,128)S(1)}, u32[]{:S(2)}, u32[]{:S(2)}) %collective-permute-start.9) | collective-permute-done | bytes 27680 | tf_op jit(solution)/shard_map/ppermute | solution.py:434
  45.7 3.1 %collective-permute-start.10 = (f32[16,432]{1,0:T(8,128)S(1)}, f32[16,432]{1,0:T(8,128)S(1)}, u32[]{:S(2)}, u32[]{:S(2)}) collective-permute-start(f32[16,432]{1,0:T(8,128)S(1)} %add.31), channel_id=1, source_target_pairs={{0,16},{1,17},{2,18},{3,19},{4,20},{5,21},{6,22},{7,23},{8,24},{9,... | collective-permute-start | bytes 82952 | tf_op jit(solution)/shard_map/ppermute | solution.py:434
  48.8 0.0 copy-done.3
  48.8 0.8 %shard_map.88 = (bf16[2048,128]{1,0:T(8,128)(2,1)S(1)}, f32[256,128]{1,0:T(8,128)S(1)}, bf16[3,384,64]{2,1,0:T(8,128)(2,1)S(1)}) custom-call(s32[2]{0:T(128)S(1)} %pad_add_fusion.place_ref, bf16[256,128]{1,0:T(8,128)(2,1)S(1)} %get-tuple-element.30.encoded_ref, f32[256,128]{1,0:T(8,128)S(1)} %get-tuple-element.31.pre_ref, bf16[27,64,64]{2,1,0:T(8,128)(2,1)S(1)} %copy-done.3), custom_call_target="tpu_custom_call" | custom-call | flops 1000000000 | bytes 2000000 | tf_op jit(solution)/shard_map/pallas_call | solution.py:413
  49.6 1.0 %collective-permute-done.10 = f32[16,432]{1,0:T(8,128)S(1)} collective-permute-done((f32[16,432]{1,0:T(8,128)S(1)}, f32[16,432]{1,0:T(8,128)S(1)}, u32[]{:S(2)}, u32[]{:S(2)}) %collective-permute-start.10) | collective-permute-done | bytes 27680 | tf_op jit(solution)/shard_map/ppermute | solution.py:434
  50.7 0.2 reshape.14
  50.8 0.6 %rev.3 = f32[16,3,3,3,16]{4,3,2,1,0:T(4,128)S(1)} reverse(f32[16,3,3,3,16]{4,3,2,1,0:T(4,128)S(1)} %reshape.14), dimensions={3} | reverse | bytes 55296 | tf_op jit(solution)/shard_map/rev | solution.py:570
  51.4 0.1 multiply_bitcast_fusion
  51.5 0.1 copy.12
  51.6 0.8 %copy.14 = f32[27,16,16]{0,2,1:T(8,128)} copy(f32[27,16,16]{2,1,0:T(8,128)S(1)} %bitcast.44) | data formatting | bytes 55296
  52.5 0.0 all-to-all-done.got_ref
  52.5 2.2 %shard_map.89 = (f32[16,16,64]{2,1,0:T(8,128)}, f32[27,64,64]{2,1,0:T(8,128)}, f32[16,16,64]{2,1,0:T(8,128)}) custom-call(bf16[32,40,128]{2,1,0:T(8,128)(2,1)S(1)} %all-to-all-done.got_ref, bf16[2048,128]{1,0:T(8,128)(2,1)S(1)} %get-tuple-element.32.spread_ref, f32[256,128]{1,0:T(8,128)S(1)} %get-tuple-element.33.slope_ref, ...), custom_call_target="tpu_custom_call" | custom-call | flops 2000000000 | bytes 2000000 | tf_op jit(solution)/shard_map/pallas_call | solution.py:413
  (18 shorter events, 0.2 us)
Async XLA Ops:
  1.7 11.3 %collective-permute-start.2 = (bf16[16,8,128]{2,1,0:T(8,128)(2,1)S(1)}, bf16[16,8,128]{2,1,0:T(8,128)(2,1)S(1)}, u32[]{:S(2)}, u32[]{:S(2)}) collective-permute-start(bf16[16,8,128]{2,1,0:T(8,128)(2,1)S(1)} %bitcast.46), channel_id=1, source_target_pairs={{0,1},{1,0},{2,3},{3,2},{4,5},{5,4},{6,7},{7,6},{8,9},{9,8},{10,11... | collective-permute-start | bytes 98312 | tf_op jit(solution)/shard_map/ppermute | solution.py:445
  5.5 14.1 %collective-permute-start.1 = (bf16[16,8,128]{2,1,0:T(8,128)(2,1)S(1)}, bf16[16,8,128]{2,1,0:T(8,128)(2,1)S(1)}, u32[]{:S(2)}, u32[]{:S(2)}) collective-permute-start(bf16[16,8,128]{2,1,0:T(8,128)(2,1)S(1)} %get-tuple-element.48), channel_id=1, source_target_pairs={{0,2},{4,6},{8,10},{12,14},{16,18},{20,22},{24,26},{28,30},{2,0},{... | collective-permute-start | bytes 98312 | tf_op jit(solution)/shard_map/ppermute | solution.py:470
  5.5 14.1 %collective-permute-start = (bf16[16,8,128]{2,1,0:T(8,128)(2,1)S(1)}, bf16[16,8,128]{2,1,0:T(8,128)(2,1)S(1)}, u32[]{:S(2)}, u32[]{:S(2)}) collective-permute-start(bf16[16,8,128]{2,1,0:T(8,128)(2,1)S(1)} %get-tuple-element.49), channel_id=1, source_target_pairs={{2,4},{6,8},{10,12},{14,16},{18,20},{22,24},{26,28},{4,2},{8,6},{1... | collective-permute-start | bytes 98312 | tf_op jit(solution)/shard_map/ppermute | solution.py:470
  6.1 10.8 %collective-permute-start.5 = (bf16[16,16,64]{2,1,0:T(8,128)(2,1)}, bf16[16,16,64]{2,1,0:T(8,128)(2,1)S(1)}, u32[]{:S(2)}, u32[]{:S(2)}) collective-permute-start(bf16[16,16,64]{2,1,0:T(8,128)(2,1)} %bitcast.45), channel_id=1, source_target_pairs={{0,1},{1,0},{2,3},{3,2},{4,5},{5,4},{6,7},{7,6},{8,9},{9,8},{10,11... | collective-permute-start | bytes 98312 | tf_op jit(solution)/shard_map/ppermute | solution.py:443
  6.2 1.2 %copy-start.1 = (bf16[512,16,64]{0,2,1:T(8,128)(2,1)S(1)}, bf16[512,16,64]{0,2,1:T(8,128)(2,1)}, u32[]{:S(2)}) copy-start(bf16[512,16,64]{0,2,1:T(8,128)(2,1)} %param.7) | copy-start | bytes 3145732
  7.5 1.0 %copy-start.2 = (bf16[27,64,64]{2,1,0:T(8,128)(2,1)S(1)}, bf16[27,64,64]{2,1,0:T(8,128)(2,1)}, u32[]{:S(2)}) copy-start(bf16[27,64,64]{2,1,0:T(8,128)(2,1)} %enc_ref.3) | copy-start | bytes 663556
  8.5 0.8 %copy-start.4 = (bf16[27,16,16]{0,2,1:T(8,128)(2,1)S(1)}, bf16[27,16,16]{0,2,1:T(8,128)(2,1)}, u32[]{:S(2)}) copy-start(bf16[27,16,16]{0,2,1:T(8,128)(2,1)} %param.8) | copy-start | bytes 41476
  9.3 7.6 %copy-start.5 = (bf16[64,16,1,16]{0,3,2,1:T(8,128)(2,1)S(1)}, bf16[64,16,1,16]{0,3,2,1:T(8,128)(2,1)}, u32[]{:S(2)}) copy-start(bf16[64,16,1,16]{0,3,2,1:T(8,128)(2,1)} %param.5) | copy-start | bytes 98308
  13.1 6.5 %collective-permute-start.4 = (bf16[2,16,128]{2,1,0:T(8,128)(2,1)S(1)}, bf16[2,16,128]{2,1,0:T(8,128)(2,1)S(1)}, u32[]{:S(2)}, u32[]{:S(2)}) collective-permute-start(bf16[2,16,128]{2,1,0:T(8,128)(2,1)S(1)} %bitcast.48), channel_id=1, source_target_pairs={{0,2},{4,6},{8,10},{12,14},{16,18},{20,22},{24,26},{28,30},{2,0},{... | collective-permute-start | bytes 24584 | tf_op jit(solution)/shard_map/ppermute | solution.py:470
  16.2 3.4 %collective-permute-start.3 = (bf16[2,16,128]{2,1,0:T(8,128)(2,1)S(1)}, bf16[2,16,128]{2,1,0:T(8,128)(2,1)S(1)}, u32[]{:S(2)}, u32[]{:S(2)}) collective-permute-start(bf16[2,16,128]{2,1,0:T(8,128)(2,1)S(1)} %bitcast.47), channel_id=1, source_target_pairs={{2,4},{6,8},{10,12},{14,16},{18,20},{22,24},{26,28},{4,2},{8,6},{1... | collective-permute-start | bytes 24584 | tf_op jit(solution)/shard_map/ppermute | solution.py:470
  17.0 2.7 %copy-start = (bf16[16,8,8,128]{3,2,1,0:T(8,128)(2,1)S(1)}, bf16[16,8,8,128]{3,2,1,0:T(8,128)(2,1)}, u32[]{:S(2)}) copy-start(bf16[16,8,8,128]{3,2,1,0:T(8,128)(2,1)} %cot_ref.3) | copy-start | bytes 786436
  22.9 4.6 %collective-permute-start.6 = (f32[16,432]{1,0:T(8,128)S(1)}, f32[16,432]{1,0:T(8,128)S(1)}, u32[]{:S(2)}, u32[]{:S(2)}) collective-permute-start(f32[16,432]{1,0:T(8,128)S(1)} %get-tuple-element.28), channel_id=1, source_target_pairs={{0,2},{1,3},{2,0},{3,1},{4,6},{5,7},{6,4},{7,5},{8,10},{9,11},{10,... | collective-permute-start | bytes 82952 | tf_op jit(solution)/shard_map/ppermute | solution.py:434
  25.8 22.9 %copy-start.3 = (bf16[27,64,64]{2,1,0:T(8,128)(2,1)S(1)}, bf16[27,64,64]{2,1,0:T(8,128)(2,1)}, u32[]{:S(2)}) copy-start(bf16[27,64,64]{2,1,0:T(8,128)(2,1)} %enc_ref.3) | copy-start | bytes 663556
  27.6 24.9 %all-to-all-start = ((bf16[32,40,128]{2,1,0:T(8,128)(2,1)}), bf16[32,40,128]{2,1,0:T(8,128)(2,1)S(1)}, u32[]{:S(2)}, u32[]{:S(2)}) async-start(bf16[32,40,128]{2,1,0:T(8,128)(2,1)} %shard_map.87), calls=%async_computation | async-start | bytes 655360 | tf_op jit(solution)/shard_map/all_to_all | solution.py:538
  32.7 5.1 %collective-permute-start.7 = (f32[16,432]{1,0:T(8,128)S(1)}, f32[16,432]{1,0:T(8,128)S(1)}, u32[]{:S(2)}, u32[]{:S(2)}) collective-permute-start(f32[16,432]{1,0:T(8,128)S(1)} %add.28), channel_id=1, source_target_pairs={{0,1},{1,0},{2,3},{3,2},{4,5},{5,4},{6,7},{7,6},{8,9},{9,8},{10,11... | collective-permute-start | bytes 82952 | tf_op jit(solution)/shard_map/ppermute | solution.py:434
  37.8 3.9 %collective-permute-start.8 = (f32[16,432]{1,0:T(8,128)S(1)}, f32[16,432]{1,0:T(8,128)S(1)}, u32[]{:S(2)}, u32[]{:S(2)}) collective-permute-start(f32[16,432]{1,0:T(8,128)S(1)} %add.29), channel_id=1, source_target_pairs={{0,4},{1,5},{2,6},{3,7},{4,0},{5,1},{6,2},{7,3},{8,12},{9,13},{10,... | collective-permute-start | bytes 82952 | tf_op jit(solution)/shard_map/ppermute | solution.py:434
  41.8 3.9 %collective-permute-start.9 = (f32[16,432]{1,0:T(8,128)S(1)}, f32[16,432]{1,0:T(8,128)S(1)}, u32[]{:S(2)}, u32[]{:S(2)}) collective-permute-start(f32[16,432]{1,0:T(8,128)S(1)} %add.30), channel_id=1, source_target_pairs={{0,8},{1,9},{2,10},{3,11},{4,12},{5,13},{6,14},{7,15},{8,0},{9,1},... | collective-permute-start | bytes 82952 | tf_op jit(solution)/shard_map/ppermute | solution.py:434
  45.7 5.0 %collective-permute-start.10 = (f32[16,432]{1,0:T(8,128)S(1)}, f32[16,432]{1,0:T(8,128)S(1)}, u32[]{:S(2)}, u32[]{:S(2)}) collective-permute-start(f32[16,432]{1,0:T(8,128)S(1)} %add.31), channel_id=1, source_target_pairs={{0,16},{1,17},{2,18},{3,19},{4,20},{5,21},{6,22},{7,23},{8,24},{9,... | collective-permute-start | bytes 82952 | tf_op jit(solution)/shard_map/ppermute | solution.py:434

commit v3 on v2

--- a/solution.py
+++ b/solution.py
@@ -38,6 +38,14 @@
     return lax.broadcasted_iota(jnp.int32, shape, dim)
 
 
+def row_index(count):
+    return iota((count, 1), 0)
+
+
+def lane_index(count):
+    return iota((1, count), 1)
+
+
 def one_hot(condition):
     return jnp.where(condition, 1.0, 0.0).astype(BF16)
 
@@ -66,12 +74,78 @@
     ref[2 * rows : 3 * rows, lanes] = lane_shift(values, -1).astype(BF16)
 
 
-def prepare_kernel(table_ref, dec_ref, enc_ref, wide_ref, conv_ref, back_ref, encw_ref):
+def taps_kernel(dec_ref, conv_ref, back_ref):
+    fine_ch = dec_ref.shape[0]
+    rows = fine_ch * (RATIO + 2)
+    square = fine_ch * fine_ch
+    group = 9 * fine_ch
+    block = 256
+    column = lane_index(6 * block)
+    rest = column % block
+    base = 9 * (rest // (3 * fine_ch)) + (rest // fine_ch) % 3 + 3 * (column // block % 3)
+    tap = jnp.where(column < 3 * block, base, 26 - base)
+    chosen_taps = one_hot(iota((27, 6 * block), 0) == jnp.where(rest < group, tap, -1))
+    cell = row_index(square)
+    last_index = iota((square, block), 1) % fine_ch
+    same_in = last_index == cell % fine_ch
+    same_out = last_index == cell // fine_ch
+    shape = (fine_ch, square)
+    pick_out = one_hot(iota(shape, 0) == lane_index(square) // fine_ch)
+    pick_in = one_hot(iota(shape, 0) == lane_index(square) % fine_ch)
+    wide = group * SPAN
+    spread = one_hot(iota((block, wide), 0) == lane_index(wide) // SPAN)
+    back_wide = 9 * rows
+    column = lane_index(back_wide)
+    channel, _ = place(column % rows, fine_ch)
+    spread_back = one_hot(iota((block, back_wide), 0) == column // rows * fine_ch + channel)
+    chosen = dot(dec_ref[...].reshape(square, 27), chosen_taps)
+    taps = []
+    for n in range(6):
+        part = chosen[:, n * block : (n + 1) * block]
+        part = jnp.where(same_in if n < 3 else same_out, part, 0.0).astype(BF16)
+        taps.append(dot(pick_out if n < 3 else pick_in, part).astype(BF16))
+    forward = dot(jnp.concatenate(taps[:3], 0), spread)
+    backward = dot(jnp.concatenate(taps[3:], 0), spread_back)
+
+    def banded(parts, offset):
+        total = jnp.zeros(offset.shape, F32)
+        for b in range(3):
+            total = jnp.where(offset == b, parts[b], total)
+        return total
+
+    def rows_of(field, channel):
+        shape = (RATIO, field.shape[1])
+        return [
+            jnp.broadcast_to(field[b * fine_ch + channel : b * fine_ch + channel + 1], shape)
+            for b in range(3)
+        ]
+
+    slot = iota((RATIO, 128), 1) % SPAN
+    offset = jnp.concatenate([10 - slot - iota((RATIO, 128), 0)] * (wide // 128), 1)
+    pieces = [banded(rows_of(forward, o), offset) for o in range(fine_ch)]
+    slot = jnp.concatenate([iota((fine_ch, 128), 1) % SPAN] * (wide // 128), 1)
+    parts = [forward[b * fine_ch : (b + 1) * fine_ch] for b in range(3)]
+    pieces += [banded(parts, 11 - slot), banded(parts, 2 - slot)]
+    field = jnp.concatenate(pieces, 0).astype(BF16)
+    for a in range(3):
+        conv_ref[a] = field[:, a * (wide // 3) : (a + 1) * (wide // 3)]
+    _, z_in = place(lane_index(back_wide) % rows, fine_ch)
+    offset = z_in - iota((RATIO, back_wide), 0) + 1
+    back_ref[...] = jnp.concatenate(
+        [banded(rows_of(backward, c), offset) for c in range(fine_ch)], 0
+    ).astype(BF16)
+
+
+def table_kernel(place_ref, table_ref, cot_ref, wide_ref, first_ref, second_ref):
+    last = cot_ref.shape[1] - 1
+    even = lax.rem(place_ref[0], 2) == 0
+    first_ref[...] = cot_ref[:, jnp.where(even, last, 0)]
+    second_ref[...] = cot_ref[:, jnp.where(even, 0, last)]
     fine_ch, chans, subs = table_ref.shape
-    depth = encw_ref.shape[1] // chans
     pairs = RATIO * RATIO
-    row = iota((subs, subs), 0)
-    pick = one_hot(iota((subs, subs), 1) == (row % pairs) * RATIO + row // pairs)
+    row = row_index(subs)
+    position = row % pairs // RATIO * pairs + (RATIO - 1 - row % RATIO) * RATIO + row // pairs
+    pick = one_hot(iota((subs, subs), 1) == position)
     turned = dot_nt(pick, table_ref[...].reshape(fine_ch * chans, subs))
     two = 2 * chans
     low = iota((pairs, two), 1) < chans
@@ -86,60 +160,6 @@
                 [first.reshape(RATIO, RATIO, two), second.reshape(RATIO, RATIO, two)], 1
             )
             wide_ref[:, p * SPAN : (p + 1) * SPAN, q * two : (q + 1) * two] = both.astype(BF16)
-    blank = jnp.zeros((chans, chans), BF16)
-    for a in range(3):
-        for z_out in range(depth):
-            blocks = []
-            for e in range(3):
-                for z_in in range(depth):
-                    b = z_in - z_out + 1
-                    blocks.append(enc_ref[9 * a + 3 * b + e] if 0 <= b < 3 else blank)
-            encw_ref[a, z_out * chans : (z_out + 1) * chans] = jnp.concatenate(blocks, 1)
-    taps = dec_ref[...].reshape(fine_ch * fine_ch, 27)
-    group = 9 * fine_ch
-    rows = fine_ch * (RATIO + 2)
-    main = fine_ch * RATIO
-    square = fine_ch * fine_ch
-    tap_row = iota((27, group), 0)
-    tap_ae = iota((27, group), 1) // fine_ch
-    tap_base = 9 * (tap_ae // 3) + tap_ae % 3
-    cell_row = iota((square, group), 0)
-    cell_last = iota((square, group), 1) % fine_ch
-    same_in = cell_last == cell_row % fine_ch
-    same_out = cell_last == cell_row // fine_ch
-    channel, _ = place(iota((rows, square), 0), fine_ch)
-    pick = one_hot(channel == iota((rows, square), 1) // fine_ch)
-    pick_back = one_hot(
-        iota((main, square), 0) // RATIO == iota((main, square), 1) % fine_ch
-    )
-    _, z_out = place(iota((rows, 128), 0), fine_ch)
-    offset = iota((rows, 128), 1) % SPAN - 2 - z_out + 1
-    wide = group * SPAN
-    spread = one_hot(iota((group, wide), 1) // SPAN == iota((group, wide), 0))
-    offset = jnp.concatenate([offset] * (wide // 128), 1)
-    piece = jnp.zeros((rows, wide), F32)
-    backs = [jnp.zeros((main, 3 * rows), F32)] * 3
-    spread_back = []
-    for a in range(3):
-        column = iota((group, 3 * rows), 1)
-        channel, _ = place(column % rows, fine_ch)
-        spread_back.append(
-            one_hot(iota((group, 3 * rows), 0) == (3 * a + column // rows) * fine_ch + channel)
-        )
-    _, z_in = place(iota((main, 3 * rows), 1) % rows, fine_ch)
-    offset_back = z_in - iota((main, 3 * rows), 0) % RATIO + 1
-    for b in range(3):
-        chosen = dot(taps, one_hot(tap_row == tap_base + 3 * b))
-        chosen = dot(pick, jnp.where(same_in, chosen, 0.0).astype(BF16)).astype(BF16)
-        piece = jnp.where(offset == b, dot(chosen, spread), piece)
-        chosen = dot(taps, one_hot(tap_row == 26 - tap_base - 3 * b))
-        chosen = dot(pick_back, jnp.where(same_out, chosen, 0.0).astype(BF16)).astype(BF16)
-        backs = [
-            jnp.where(offset_back == b, dot(chosen, spread_back[a]), backs[a]) for a in range(3)
-        ]
-    for a in range(3):
-        conv_ref[a] = piece[:, a * (wide // 3) : (a + 1) * (wide // 3)].astype(BF16)
-        back_ref[a] = backs[a].astype(BF16)
 
 
 def shift_rows(values, width):
@@ -166,17 +186,36 @@
 
 
 def encode_kernel(
-    place_ref, dark_ref, encw_ref, wide_ref, pre_ref, encoded_ref, dark3_ref, up_ref, pad_ref
+    place_ref, enc_ref, wide_ref, *refs, depth
 ):
-    depth, planes, width, chans = dark_ref.shape
+    *dark_refs, pre_ref, encoded_ref, dark3_ref, up_ref, pad_ref = refs
+    planes, width, chans = dark_refs[0].shape[-3:]
     main = wide_ref.shape[1]
     fine_ch = main // RATIO
     cells = planes * width
     fine_width = width * RATIO
-    dark = jnp.concatenate([dark_ref[z].reshape(cells, chans) for z in range(depth)], 1)
+    blank = jnp.zeros((chans, chans), BF16)
+    weights = []
+    for a in range(3):
+        rows = []
+        for z_out in range(depth):
+            blocks = []
+            for e in range(3):
+                for z_in in range(depth):
+                    b = z_in - z_out + 1
+                    blocks.append(enc_ref[9 * a + 3 * b + e] if 0 <= b < 3 else blank)
+            rows.append(jnp.concatenate(blocks, 1))
+        weights.append(jnp.concatenate(rows, 0))
+    if len(dark_refs) == 2:
+        own, other = (ref[...].reshape(cells, chans) for ref in dark_refs)
+        first = place_ref[1] == 0
+        parts = [jnp.where(first, own, other), jnp.where(first, other, own)]
+    else:
+        parts = [dark_refs[0][z].reshape(cells, chans) for z in range(depth)]
+    dark = jnp.concatenate(parts, 1)
     store_padded(dark3_ref, dark, width)
     pre = sum(
-        dot_nt(dark3_ref[a * width : a * width + cells], encw_ref[a]) for a in range(3)
+        dot_nt(dark3_ref[a * width : a * width + cells], weights[a]) for a in range(3)
     )
     pre_ref[...] = pre
     encoded = jax.nn.silu(pre).astype(BF16)
@@ -226,12 +265,13 @@
                 )
                 for m in range(3)
             )
-            plane = jnp.concatenate([jnp.where(low, under, own), jnp.where(low, own, over)], 1)
+            plane = jnp.concatenate([jnp.where(low, over, own), jnp.where(low, own, under)], 1)
             store_shifts(up_ref, base + n, plane.reshape(fine_ch * SPAN, fine_width))
 
 
 def decode_kernel(
-    cot_ref, low_ref, high_ref, face_ref, corner_ref, conv_ref, up_ref, grad_ref, total_ref
+    place_ref, cot_ref, x_low_ref, x_high_ref, z_low_ref, z_high_ref, conv_ref, up_ref,
+    grad_ref, total_ref, *, planes_z
 ):
     fine_ch, planes, depth, width = cot_ref.shape
     main = fine_ch * depth
@@ -239,40 +279,49 @@
     wide = (planes + 2) * width
     own = planes * width
     pre = sum(dot(conv_ref[a], up_ref[:, a * width : a * width + wide]) for a in range(3))
-    row = iota((main, main), 0)
-    column = iota((main, main), 1)
-    turn = one_hot((row % fine_ch == column // planes) & (row // fine_ch == column % planes))
-    faces = [
-        dot(turn, face_ref[side].astype(F32).reshape(main, width).astype(BF16))
-        for side in range(2)
+    own_z = place_ref[1]
+    valid = (own_z > 0, own_z < planes_z - 1)
+    shape = (main, main)
+    turn = iota(shape, 1) == row_index(main) % fine_ch * planes + row_index(main) // fine_ch
+    sides = [
+        dot(one_hot(turn & valid[side]), ref[...].astype(F32).reshape(main, width).astype(BF16))
+        for side, ref in enumerate((z_low_ref, z_high_ref))
     ]
     for x in range(planes + 2):
-        if x == 0:
-            inner = low_ref[...]
-            edge = [corner_ref[0, side].astype(F32) for side in range(2)]
-        elif x == planes + 1:
-            inner = high_ref[...]
-            edge = [corner_ref[1, side].astype(F32) for side in range(2)]
+        if 0 < x <= planes:
+            inner = cot_ref[:, x - 1].astype(F32).reshape(main, width)
+            edge = [side[(x - 1) * fine_ch : x * fine_ch] for side in sides]
         else:
-            inner = cot_ref[:, x - 1]
-            edge = [face[(x - 1) * fine_ch : x * fine_ch] for face in faces]
-        cot = jnp.concatenate([inner.astype(F32).reshape(main, width)] + edge, 0)
+            outer = x_low_ref if x == 0 else x_high_ref
+            inner = outer[:main].astype(F32)
+            edge = []
+            for side in range(2):
+                first = main + side * (outer.shape[0] - main - fine_ch)
+                corner = outer[first : first + fine_ch].astype(F32)
+                edge.append(jnp.where(valid[side], corner, 0.0))
+        cot = jnp.concatenate([inner] + edge, 0)
         grad = (cot * slope_of(pre[:, x * width : (x + 1) * width])).astype(BF16)
         store_shifts(grad_ref, x, grad.astype(F32))
     grads = jnp.concatenate(
-        [grad_ref[e * rows : e * rows + main, width : width + own] for e in range(3)], 0
+        [grad_ref[e * rows : e * rows + main, width : width + own] for e in (2, 1, 0)], 0
     )
     taps = fine_ch * SPAN
-    shape = (3 * main, taps)
-    offset = iota(shape, 1) % SPAN - 2 - iota(shape, 0) % RATIO + 1
     sums = []
     for a in range(3):
         fields = up_ref[taps : 2 * taps, (a + 1) * width : (a + 1) * width + own]
         product = dot_nt(grads, fields)
-        for b in range(3):
-            kept = jnp.where(offset == b, product, 0.0)
-            sums.append(jnp.sum(kept.reshape(3 * fine_ch, RATIO, taps), 1))
-    fold = jnp.where(iota((fine_ch, taps), 1) // SPAN == iota((fine_ch, taps), 0), 1.0, 0.0)
+        halves = []
+        for first in range(0, taps, 128):
+            part = product[:, first : first + 128].reshape(3 * fine_ch, RATIO, 128)
+            halves.append(jnp.sum(pltpu.roll(part, 0, 2, stride=1, stride_axis=1), 1))
+        sums.append(jnp.concatenate(halves, 1))
+    shape = (3 * fine_ch, taps)
+    fold = jnp.where(
+        (iota(shape, 1) // SPAN == iota(shape, 0) % fine_ch)
+        & (iota(shape, 1) % SPAN == 10 - iota(shape, 0) // fine_ch),
+        1.0,
+        0.0,
+    )
     total_ref[...] = lax.dot_general(
         fold,
         jnp.concatenate(sums, 0),
@@ -289,7 +338,11 @@
     chans = wide_ref.shape[2] // RATIO
     owners, chunk, _ = send_ref.shape
     span = chunk - RATIO
-    back = sum(dot(back_ref[a], grad_ref[:, a * width : a * width + own]) for a in range(3))
+    taps = grad_ref.shape[0]
+    back = sum(
+        dot(back_ref[:, a * taps : (a + 1) * taps], grad_ref[:, a * width : a * width + own])
+        for a in range(3)
+    )
     cot = jnp.concatenate(
         [cot_ref[:, x].astype(F32).reshape(main, width) for x in range(planes)], 1
     )
@@ -298,8 +351,12 @@
     column = iota((main, main), 1)
     turn = one_hot((row % fine_ch == column // RATIO) & (row // fine_ch == column % RATIO))
     turned = dot(turn, up).astype(BF16)
+    flip = one_hot(
+        (row // RATIO == column // RATIO) & (row % RATIO + column % RATIO == RATIO - 1)
+    )
+    flipped = dot(flip, up).astype(BF16)
     parts = dot_tn(
-        jnp.concatenate([up[:, x * width : (x + 1) * width] for x in range(planes)], 0),
+        jnp.concatenate([flipped[:, x * width : (x + 1) * width] for x in range(planes)], 0),
         wide_ref[...].reshape(planes * main, RATIO * chans),
     )
     two = 2 * chans
@@ -320,7 +377,9 @@
         send_ref[owner, span:] = cells
 
 
-def widen_kernel(place_ref, encoded_ref, pre_ref, enc_ref, out_ref, slope_ref, taps_ref):
+def widen_kernel(
+    place_ref, encoded_ref, pre_ref, enc_ref, out_ref, slope_ref, taps_ref, order_ref
+):
     cells, lanes = encoded_ref.shape
     chans = enc_ref.shape[1]
     depth = lanes // chans
@@ -343,11 +402,42 @@
                 taps_ref[a, first : first + chans] = jnp.where(
                     (b >= 0) & (b <= 2), tap.astype(F32), 0.0
                 ).astype(BF16)
+    shape = order_ref.shape[1:]
+    fine_ch = shape[0] // 9
+    step = shape[1] // fine_ch
+    row = row_index(shape[0])
+    column = iota(shape, 1)
+    tap = row // fine_ch // 3 * 9 + row // fine_ch % 3
+    for b in range(3):
+        order_ref[b] = one_hot(column == row % fine_ch * step + tap + 3 * b)
+
+
+def final_kernel(own_ref, other_ref, order_ref, done_ref, out_ref, *, scale):
+    total = (own_ref[...] + other_ref[...]) * scale
+    fine_ch = out_ref.shape[0]
+    high = total.astype(BF16)
+    rest = total - high.astype(F32)
+    middle = rest.astype(BF16)
+    low = (rest - middle.astype(F32)).astype(BF16)
+    field = 0.0
+    for b in range(3):
+        rows = slice(b * fine_ch, (b + 1) * fine_ch)
+        field = field + dot(jnp.concatenate([high[rows], middle[rows], low[rows]], 0), order_ref[b])
+    field = field[:fine_ch] + field[fine_ch : 2 * fine_ch] + field[2 * fine_ch :]
+    step = field.shape[1] // fine_ch
+    for o in range(fine_ch):
+        first = o * step // 128 * 128
+        part = field[:, first : first + 128]
+        if o * step > first:
+            part = pltpu.roll(part, 128 - (o * step - first), 1)
+        out_ref[o] = part[:, :27]
 
 
 def finish_kernel(
-    got_ref, spread_ref, slope_ref, dark3_ref, taps_ref, dark_out, enc_out, up_out, pad_ref, *, scale
+    got_ref, spread_ref, slope_ref, dark3_ref, taps_ref,
+    dark_out, enc_out, up_out, done_ref, pad_ref, *, scale
 ):
+    done_ref[...] = jnp.zeros(done_ref.shape, F32)
     owners, chunk, fine_width = got_ref.shape
     cells, lanes = slope_ref.shape
     chans = taps_ref.shape[2]
@@ -429,48 +519,38 @@
     return lax.ppermute(block, axis, pairs)
 
 
-def sum_step(value, step):
+def swapped(value, step):
     count = lax.axis_size(AXES)
-    return value + lax.ppermute(value, AXES, [(i, i ^ step) for i in range(count)])
+    return lax.ppermute(value, AXES, [(i, i ^ step) for i in range(count)])
 
 
 def exchange_depth(dark_rows, cotangent):
     count = lax.axis_size("narrow")
     last = cotangent.shape[2] - 1
     if count == 2:
-        first = lax.axis_index("narrow") == 0
         swap = [(0, 1), (1, 0)]
-        other = lax.ppermute(dark_rows, "narrow", swap)
-        face = lax.dynamic_index_in_dim(cotangent, jnp.where(first, last, 0), 2, False)
-        face = lax.ppermute(face, "narrow", swap)
-        none = jnp.zeros_like(face)
-        planes = jnp.stack(
-            [jnp.where(first, dark_rows, other), jnp.where(first, other, dark_rows)], 0
-        )
-        low, high = jnp.where(first, none, face), jnp.where(first, face, none)
-    else:
-        planes = lax.all_gather(dark_rows, "narrow", axis=0)
-        low = shift(cotangent[:, :, last], "narrow", 1)
-        high = shift(cotangent[:, :, 0], "narrow", -1)
-    return planes, jnp.stack([low, high], 0)
-
-
-def exchange_width(cotangent, faces):
+        dark = lax.ppermute(dark_rows, "narrow", swap)
+        z = jnp.where(lax.axis_index("narrow") == 0, last, 0)
+        face = lax.ppermute(lax.dynamic_index_in_dim(cotangent, z, 2, False), "narrow", swap)
+        return (dark_rows, dark), (face,)
+    planes = lax.all_gather(dark_rows, "narrow", axis=0)
+    low = shift(cotangent[:, :, last], "narrow", 1)
+    return (planes,), (low, shift(cotangent[:, :, 0], "narrow", -1))
+
+
+def exchange_width(planes, faces):
     count = lax.axis_size("wide")
-    last = cotangent.shape[1] - 1
+    last = faces[0].shape[1] - 1
     even = lax.axis_index("wide") % 2 == 0
     got = []
-    for odd, plane in ((0, jnp.where(even, last, 0)), (1, jnp.where(even, 0, last))):
+    for odd in range(2):
         pairs = [(i, i + 1) for i in range(odd, count - 1, 2)]
         pairs += [(target, source) for source, target in pairs]
-        send = (
-            lax.dynamic_index_in_dim(cotangent, plane, 1, False),
-            lax.dynamic_index_in_dim(faces, plane, 2, False),
-        )
-        got.append([lax.ppermute(part, "wide", pairs) for part in send])
-    low = [jnp.where(even, second, first) for first, second in zip(*got)]
-    high = [jnp.where(even, first, second) for first, second in zip(*got)]
-    return low[0], high[0], jnp.stack([low[1], high[1]], 0)
+        plane = jnp.where(even, 0, last) if odd else jnp.where(even, last, 0)
+        edges = [lax.dynamic_index_in_dim(face, plane, 1, False) for face in faces]
+        send = jnp.concatenate([planes[odd], *edges], 0)
+        got.append(lax.ppermute(send, "wide", pairs))
+    return jnp.where(even, got[1], got[0]), jnp.where(even, got[0], got[1])
 
 
 def on_device(dark, w_enc, up_weight, w_dec, cotangent):
@@ -485,39 +565,45 @@
     where = jnp.stack([lax.axis_index("wide"), lax.axis_index("narrow")]).astype(jnp.int32)
 
     dark_planes, faces = exchange_depth(dark[:, :, 0].transpose(1, 2, 0), cotangent)
-    x_low, x_high, corners = exchange_width(cotangent, faces)
 
     rows = fine_ch * (RATIO + 2)
     taps = fine_ch * SPAN
     main = fine_ch * RATIO
-    wide_table, conv, back, enc_weights = call(
-        prepare_kernel,
-        [
-            ((RATIO, main, RATIO * chans), BF16),
-            ((3, rows, 3 * taps), BF16),
-            ((3, main, 3 * rows), BF16),
-            ((3, lanes, 3 * lanes), BF16),
-        ],
-        (up_weight.transpose(1, 2, 0), w_dec.transpose(1, 2, 0), w_enc),
-        flops=2e9,
-    )
+    face = (fine_ch * fine_depth, fine_width)
+    conv, back = call(
+        taps_kernel,
+        [((3, rows, 3 * taps), BF16), ((main, 9 * rows), BF16)],
+        (w_dec.transpose(1, 2, 0),),
+        flops=1e9,
+    )
+    outer = (fine_ch, fine_depth, fine_width)
+    wide_table, first_plane, second_plane = call(
+        table_kernel,
+        [((RATIO, main, RATIO * chans), BF16), (outer, BF16), (outer, BF16)],
+        (where, up_weight.transpose(1, 2, 0), cotangent),
+        scalars=1,
+        flops=1e9,
+    )
+    outer_planes = [plane.reshape(face) for plane in (first_plane, second_plane)]
+    x_low, x_high = exchange_width(outer_planes, faces)
     enc_pre, encoded, dark3, upsampled = call(
-        encode_kernel,
+        functools.partial(encode_kernel, depth=depth),
         [
             ((cells, lanes), F32),
             ((cells, lanes), BF16),
             ((cells + 2 * width, 3 * lanes), BF16),
             ((3 * taps, (RATIO + 4) * fine_width), BF16),
         ],
-        (where, dark_planes, enc_weights, wide_table),
+        (where, w_enc, wide_table, *dark_planes),
         scratch=[VMEM((planes + 2, depth + 2, width, 2 * chans), F32)],
         scalars=1,
         flops=2e9,
     )
     dec_grad, dec_sum = call(
-        decode_kernel,
-        [((3 * rows, (RATIO + 2) * fine_width), BF16), ((fine_ch, 27 * fine_ch), F32)],
-        (cotangent, x_low, x_high, faces, corners, conv, upsampled),
+        functools.partial(decode_kernel, planes_z=depth),
+        [((3 * rows, (RATIO + 2) * fine_width), BF16), ((3 * fine_ch, 9 * fine_ch), F32)],
+        (where, cotangent, x_low, x_high, faces[0], faces[-1], conv, upsampled),
+        scalars=1,
         flops=2e9,
     )
     chunk = max(1, RATIO * RATIO // owners) * fine_ch + RATIO
@@ -531,19 +617,22 @@
     if owners & (owners - 1):
         dec_sum = lax.psum(dec_sum, AXES)
         steps = []
-    steps = sorted(steps, key=lambda step: (step != depth, step))
-    for step in steps[:1]:
-        dec_sum = sum_step(dec_sum, step)
-    send, dec_sum = lax.optimization_barrier((send, dec_sum))
+    steps = sorted(steps)
+    received = jnp.zeros_like(dec_sum)
+    for n, step in enumerate(steps):
+        received = swapped(dec_sum, step)
+        if n < len(steps) - 1:
+            dec_sum = dec_sum + received
+        if n == 0:
+            send, dec_sum = lax.optimization_barrier((send, dec_sum))
     got = lax.all_to_all(send, AXES, 0, 0, tiled=True)
-    for step in steps[1:]:
-        dec_sum = sum_step(dec_sum, step)
-    enc_spread, enc_slope, enc_taps = call(
+    enc_spread, enc_slope, enc_taps, order = call(
         widen_kernel,
         [
             ((cells * RATIO, lanes), BF16),
             ((cells, lanes), F32),
             ((3, 3 * lanes, chans), BF16),
+            ((3, 9 * fine_ch, 32 * fine_ch), BF16),
         ],
         (where, encoded, enc_pre, w_enc),
         scalars=1,
@@ -552,12 +641,13 @@
     coarse_scale = 1.0 / math.sqrt(cells * depth)
     fine_scale = 1.0 / math.sqrt(cells * depth * subs)
     pairs = (chunk - RATIO) // fine_ch
-    grad_dark, grad_enc, grad_up = call(
+    grad_dark, grad_enc, grad_up, done = call(
         functools.partial(finish_kernel, scale=coarse_scale),
         [
             ((planes, width, chans), F32),
             ((27, chans, chans), F32),
             ((pairs * RATIO, fine_ch, chans), F32),
+            ((8, 128), F32),
         ],
         (got, enc_spread, enc_slope, dark3, enc_taps),
         scratch=[VMEM((cells + 2 * width, 3 * lanes), BF16)],
@@ -566,12 +656,13 @@
     if own_rows < pairs * RATIO:
         own = lax.axis_index(AXES) * own_rows % RATIO
         grad_up = lax.dynamic_slice_in_dim(grad_up, own, own_rows, 0)
-    grad_dec = (
-        dec_sum.reshape(fine_ch, 3, 3, 3, fine_ch)[:, :, :, ::-1]
-        .transpose(1, 2, 3, 4, 0)
-        .reshape(27, fine_ch, fine_ch)
-    ) * fine_scale
-    return grad_dark.transpose(2, 0, 1)[:, :, None], grad_enc, grad_up, grad_dec
+    (grad_dec,) = call(
+        functools.partial(final_kernel, scale=fine_scale),
+        [((fine_ch, fine_ch, 27), F32)],
+        (dec_sum, received, order, done),
+        flops=1e8,
+    )
+    return grad_dark.transpose(2, 0, 1)[:, :, None], grad_enc, grad_up, grad_dec.transpose(2, 0, 1)
 
 
 def solution(mesh):

time: 55.1 us -> 46.2 us (0.84)
  starting transfers between devices: 23.6 us -> 19.8 us
  local copies, waits for them, and re-layouts: 6.62 us -> 2.9 us
  waiting for transfers between devices: 9.1 us -> 7.78 us
    ppermute x11 -> x9, starting transfers between devices: 18.5 us -> 11.5 us  [the longest x5 7.67 us: swapped(): return lax.ppermute(value, AXES, [(i, i ^ step) for i in range(count)])]
    all_to_all x1, starting transfers between devices: 5.1 us -> 8.31 us  [on_device(): got = lax.all_to_all(send, AXES, 0, 0, tiled=True)]
    unnamed x16 -> x25, local copies, waits for them, and re-layouts: 3.94 us -> 1.75 us
    ppermute x11 -> x9, waiting for transfers between devices: 9.1 us -> 7.77 us  [the longest x5 7.76 us: swapped(): return lax.ppermute(value, AXES, [(i, i ^ step) for i in range(count)])]
    squeeze x1 -> x0, local copies, waits for them, and re-layouts: 0.78 us -> none  [exchange_width(): lax.dynamic_index_in_dim(cotangent, plane, 1, False)]
    rev x1 -> x0, local copies, waits for them, and re-layouts: 0.57 us -> none  [on_device(): dec_sum.reshape(fine_ch, 3, 3, 3, fine_ch)[:, :, :, ::-1]]
    pallas_call x6 -> x8, Pallas kernels: 14.1 us -> 14.4 us  [call(): pl.pallas_call(kernel, out_shape=[jax.ShapeDtypeStruct(*s) for s in out_s...]
    dynamic_slice x1 -> x2, local copies, waits for them, and re-layouts: 1.03 us -> 1.15 us  [the longest x1 1.12 us: exchange_depth(): lax.dynamic_index_in_dim(cotangent, z, 2, False)]
  transfers between devices with their start and end apart: 12 -> 10, of which waited for: 4 -> 5; matrix products, arithmetic and copies ran while one was open for 5% -> 0% of each run, Pallas kernels for 16% -> 22%
where the time goes in v3:
time: 46.2 us; the launch traced here: 46 us
  starting transfers between devices  19.8 us (43%)
  Pallas kernels  14.4 us (31%)
  waiting for transfers between devices  7.78 us (17%)
  local copies, waits for them, and re-layouts  2.9 us (6%)
  between operations  0.92 us (2%)
    pallas_call x8, Pallas kernels, call(): pl.pallas_call(kernel, out_shape=[jax.ShapeDtypeStruct(*s) for s in out_s...  14.4 us
    all_to_all x1, starting transfers between devices, on_device(): got = lax.all_to_all(send, AXES, 0, 0, tiled=True)  8.31 us
    ppermute x5, waiting for transfers between devices, swapped(): return lax.ppermute(value, AXES, [(i, i ^ step) for i in range(count)])  7.76 us
    ppermute x5, starting transfers between devices, swapped(): return lax.ppermute(value, AXES, [(i, i ^ step) for i in range(count)])  7.67 us
    ppermute x1, starting transfers between devices, exchange_depth(): lax.ppermute(lax.dynamic_index_in_dim(cotangent, z, 2, False), 'narrow',...  3 us
    unnamed x25, local copies, waits for them, and re-layouts  1.75 us
    dynamic_slice x1, local copies, waits for them, and re-layouts, exchange_depth(): lax.dynamic_index_in_dim(cotangent, z, 2, False)  1.12 us
  transfers between devices with their start and end apart: 10, of which 5 were waited for; matrix products, arithmetic and copies ran while one was open for 0% of the time, Pallas kernels for 22%

profile of v3, /device:TPU:0, one launch (start us, length us, event | category | flops | bytes accessed | tf_op | source)
XLA Modules:
  0.0 46.0 jit_solution(13484840943727811393)
XLA Ops:
  0.6 0.0 copy-start
  0.6 0.0 copy-start.1
  0.7 1.1 %constant_dynamic-slice_fusion.2 = bf16[16,8,1,128]{3,2,1,0:T(2,128)(2,1)S(1)} fusion(bf16[16,8,8,128]{3,2,1,0:T(8,128)(2,1)} %cot_ref.5, s32[]{:T(128)S(6)} %select_n.36), kind=kLoop, calls=%fused_computation.9 | loop fusion | bytes 65540 | tf_op jit(solution)/shard_map/jit(dynamic_index_in_dim)/dynamic_slice | solution.py:534
  1.8 3.0 %collective-permute-start = (bf16[16,8,128]{2,1,0:T(8,128)(2,1)S(1)}, bf16[16,8,128]{2,1,0:T(8,128)(2,1)S(1)}, u32[]{:S(2)}, u32[]{:S(2)}) collective-permute-start(bf16[16,8,128]{2,1,0:T(8,128)(2,1)S(1)} %bitcast.31), channel_id=1, source_target_pairs={{0,1},{1,0},{2,3},{3,2},{4,5},{5,4},{6,7},{7,6},{8,9},{9,8},{10,11... | collective-permute-start | bytes 98312 | tf_op jit(solution)/shard_map/ppermute | solution.py:534
  4.8 0.1 collective-permute-start.3
  4.9 0.8 %copy-done.3 = bf16[27,16,16]{0,2,1:T(8,128)(2,1)S(1)} copy-done((bf16[27,16,16]{0,2,1:T(8,128)(2,1)S(1)}, bf16[27,16,16]{0,2,1:T(8,128)(2,1)}, u32[]{:S(2)}) %copy-start.3) | copy-done | bytes 13848
  5.7 1.2 %shard_map.85 = (bf16[3,160,768]{2,1,0:T(8,128)(2,1)S(1)}, bf16[128,1440]{1,0:T(8,128)(2,1)S(1)}) custom-call(bf16[16,16,27]{2,1,0:T(8,128)(2,1)S(1)} %bitcast.27), custom_call_target="tpu_custom_call" | custom-call | flops 1000000000 | bytes 2000000 | tf_op jit(solution)/shard_map/pallas_call | solution.py:503
  7.0 0.0 copy-start.5
  7.0 0.9 %copy-done.5 = bf16[3,160,768]{2,1,0:T(8,128)(2,1)} copy-done((bf16[3,160,768]{2,1,0:T(8,128)(2,1)}, bf16[3,160,768]{2,1,0:T(8,128)(2,1)S(1)}, u32[]{:S(2)}) %copy-start.5) | copy-done | bytes 737304
  7.8 0.1 pad_add_fusion.place_ref
  7.9 0.0 copy-done
  7.9 0.0 copy-done.1
  7.9 1.4 %shard_map.84 = (bf16[8,128,512]{2,1,0:T(8,128)(2,1)S(1)}, bf16[16,8,128]{2,1,0:T(8,128)(2,1)S(1)}, bf16[16,8,128]{2,1,0:T(8,128)(2,1)S(1)}) custom-call(s32[2]{0:T(128)S(1)} %pad_add_fusion.place_ref, bf16[16,64,512]{2,1,0:T(8,128)(2,1)S(1)} %bitcast.26, bf16[16,8,8,128]{3,2,1,0:T(8,128)(2,1)S(1)} %copy-done), custom_call_target="tpu_custom_call" | custom-call | flops 1000000000 | bytes 2000000 | tf_op jit(solution)/shard_map/pallas_call | solution.py:503
  9.4 0.0 collective-permute-done.z_low_ref.z_high_ref
  9.4 0.1 collective-permute-start.2
  9.5 0.7 %collective-permute-start.1 = (bf16[144,128]{1,0:T(8,128)(2,1)S(1)}, bf16[144,128]{1,0:T(8,128)(2,1)S(1)}, u32[]{:S(2)}, u32[]{:S(2)}) collective-permute-start(bf16[144,128]{1,0:T(8,128)(2,1)S(1)} %pad_maximum_fusion), channel_id=1, source_target_pairs={{2,4},{6,8},{10,12},{14,16},{18,20},{22,24},{26,28},{4,2},{8,6},{1... | collective-permute-start | bytes 110600 | tf_op jit(solution)/shard_map/ppermute | solution.py:552
  10.2 0.0 collective-permute-done.3.refs_1_
  10.2 0.0 copy-done.2
  10.2 0.0 copy-done.4
  10.2 0.0 copy-start.6
  10.2 2.6 %shard_map.86 = (f32[256,128]{1,0:T(8,128)S(1)}, bf16[256,128]{1,0:T(8,128)(2,1)S(1)}, bf16[288,384]{1,0:T(8,128)(2,1)S(1)}, bf16[768,1536]{1,0:T(8,128)(2,1)S(1)}) custom-call(s32[2]{0:T(128)S(1)} %pad_add_fusion.place_ref, bf16[27,64,64]{2,1,0:T(8,128)(2,1)S(1)} %copy-done.2, bf16[8,128,512]{2,1,0:T(8,128)(2,1)S(1)} %get-tuple-element.28.wide_ref, ...), custom_call_target="tpu_custom_call" | custom-call | flops 2000000000 | bytes 2000000 | tf_op jit(solution)/shard_map/pallas_call | solution.py:503
  12.8 0.0 copy-start.7
  12.8 0.0 copy-start.9
  12.8 0.0 collective-permute-done.2
  12.8 0.0 collective-permute-done.1
  12.9 0.0 copy-done.6
  12.9 3.1 %shard_map.87 = (bf16[480,1280]{1,0:T(8,128)(2,1)S(1)}, f32[48,144]{1,0:T(8,128)S(1)}) custom-call(s32[2]{0:T(128)S(1)} %pad_add_fusion.place_ref, bf16[16,8,8,128]{3,2,1,0:T(8,128)(2,1)S(1)} %copy-done, bf16[144,128]{1,0:T(8,128)(2,1)S(1)} %get-tuple-element.55.x_low_ref, bf16[144,128]{1,0:T(8,128)(2,1)S(1)} %get-tuple-element.54.x_high_ref, ...), custom_call_target="tpu_custom_call" | custom-call | flops 2000000000 | bytes 2000000 | tf_op jit(solution)/shard_map/pallas_call | solution.py:503
  16.0 0.0 copy-done.7
  16.0 0.0 copy-done.9
  16.1 2.0 %collective-permute-start.4 = (f32[48,144]{1,0:T(8,128)S(1)}, f32[48,144]{1,0:T(8,128)S(1)}, u32[]{:S(2)}, u32[]{:S(2)}) collective-permute-start(f32[48,144]{1,0:T(8,128)S(1)} %get-tuple-element.32), channel_id=1, source_target_pairs={{0,1},{1,0},{2,3},{3,2},{4,5},{5,4},{6,7},{7,6},{8,9},{9,8},{10,11... | collective-permute-start | bytes 82952 | tf_op jit(solution)/shard_map/ppermute | solution.py:524
  18.1 2.0 %shard_map.88 = bf16[32,40,128]{2,1,0:T(8,128)(2,1)} custom-call(bf16[16,8,8,128]{3,2,1,0:T(8,128)(2,1)S(1)} %copy-done, bf16[480,1280]{1,0:T(8,128)(2,1)S(1)} %get-tuple-element.30.grad_ref, bf16[128,1440]{1,0:T(8,128)(2,1)S(1)} %get-tuple-element.31.back_ref, bf16[8,128,512]{2,1,0:T(8,128)(2,1)S(1)} %get-tuple-element.28.wide_ref), custom_call_target="tpu_custom_call" | custom-call | flops 2000000000 | bytes 2000000 | tf_op jit(solution)/shard_map/pallas_call | solution.py:503
  20.0 0.2 collective-permute-done.4
  20.2 0.0 copy-start.10
  20.2 8.3 %all-to-all-start = ((bf16[32,40,128]{2,1,0:T(8,128)(2,1)}), bf16[32,40,128]{2,1,0:T(8,128)(2,1)S(1)}, u32[]{:S(2)}, u32[]{:S(2)}) async-start(bf16[32,40,128]{2,1,0:T(8,128)(2,1)} %shard_map.88), calls=%async_computation | async-start | bytes 655360 | tf_op jit(solution)/shard_map/all_to_all | solution.py:628
  28.5 0.3 collective-permute-start.5
  28.9 1.0 %collective-permute-done.5 = f32[48,144]{1,0:T(8,128)S(1)} collective-permute-done((f32[48,144]{1,0:T(8,128)S(1)}, f32[48,144]{1,0:T(8,128)S(1)}, u32[]{:S(2)}, u32[]{:S(2)}) %collective-permute-start.5) | collective-permute-done | bytes 27680 | tf_op jit(solution)/shard_map/ppermute | solution.py:524
  29.9 1.8 %collective-permute-start.6 = (f32[48,144]{1,0:T(8,128)S(1)}, f32[48,144]{1,0:T(8,128)S(1)}, u32[]{:S(2)}, u32[]{:S(2)}) collective-permute-start(f32[48,144]{1,0:T(8,128)S(1)} %add.23), channel_id=1, source_target_pairs={{0,4},{1,5},{2,6},{3,7},{4,0},{5,1},{6,2},{7,3},{8,12},{9,13},{10,... | collective-permute-start | bytes 82952 | tf_op jit(solution)/shard_map/ppermute | solution.py:524
  31.7 4.1 %collective-permute-done.6 = f32[48,144]{1,0:T(8,128)S(1)} collective-permute-done((f32[48,144]{1,0:T(8,128)S(1)}, f32[48,144]{1,0:T(8,128)S(1)}, u32[]{:S(2)}, u32[]{:S(2)}) %collective-permute-start.6) | collective-permute-done | bytes 27680 | tf_op jit(solution)/shard_map/ppermute | solution.py:524
  35.8 1.3 %collective-permute-start.7 = (f32[48,144]{1,0:T(8,128)S(1)}, f32[48,144]{1,0:T(8,128)S(1)}, u32[]{:S(2)}, u32[]{:S(2)}) collective-permute-start(f32[48,144]{1,0:T(8,128)S(1)} %add.24), channel_id=1, source_target_pairs={{0,8},{1,9},{2,10},{3,11},{4,12},{5,13},{6,14},{7,15},{8,0},{9,1},... | collective-permute-start | bytes 82952 | tf_op jit(solution)/shard_map/ppermute | solution.py:524
  37.0 0.0 copy-done.8
  37.0 0.9 %shard_map.89 = (bf16[2048,128]{1,0:T(8,128)(2,1)S(1)}, f32[256,128]{1,0:T(8,128)S(1)}, bf16[3,384,64]{2,1,0:T(8,128)(2,1)S(1)}, bf16[3,144,512]{2,1,0:T(8,128)(2,1)S(1)}) custom-call(s32[2]{0:T(128)S(1)} %pad_add_fusion.place_ref, bf16[256,128]{1,0:T(8,128)(2,1)S(1)} %get-tuple-element.34.encoded_ref, f32[256,128]{1,0:T(8,128)S(1)} %copy-done.8, ...), custom_call_target="tpu_custom_call" | custom-call | flops 1000000000 | bytes 2000000 | tf_op jit(solution)/shard_map/pallas_call | solution.py:503
  38.0 2.0 %collective-permute-done.7 = f32[48,144]{1,0:T(8,128)S(1)} collective-permute-done((f32[48,144]{1,0:T(8,128)S(1)}, f32[48,144]{1,0:T(8,128)S(1)}, u32[]{:S(2)}, u32[]{:S(2)}) %collective-permute-start.7) | collective-permute-done | bytes 27680 | tf_op jit(solution)/shard_map/ppermute | solution.py:524
  40.0 2.3 %collective-permute-start.8 = (f32[48,144]{1,0:T(8,128)S(1)}, f32[48,144]{1,0:T(8,128)S(1)}, u32[]{:S(2)}, u32[]{:S(2)}) collective-permute-start(f32[48,144]{1,0:T(8,128)S(1)} %add.25.own_ref), channel_id=1, source_target_pairs={{0,16},{1,17},{2,18},{3,19},{4,20},{5,21},{6,22},{7,23},{8,24},{9,... | collective-permute-start | bytes 82952 | tf_op jit(solution)/shard_map/ppermute | solution.py:524
  42.2 0.0 all-to-all-done.got_ref
  42.2 0.0 copy-done.10
  42.2 2.2 %shard_map.90 = (f32[16,16,64]{2,1,0:T(8,128)}, f32[27,64,64]{2,1,0:T(8,128)}, f32[16,16,64]{2,1,0:T(8,128)}, f32[8,128]{1,0:T(8,128)S(1)}) custom-call(bf16[32,40,128]{2,1,0:T(8,128)(2,1)S(1)} %all-to-all-done.got_ref, bf16[2048,128]{1,0:T(8,128)(2,1)S(1)} %get-tuple-element.36.spread_ref, f32[256,128]{1,0:T(8,128)S(1)} %get-tuple-element.37.slope_ref, ...), custom_call_target="tpu_custom_call" | custom-call | flops 2000000000 | bytes 2000000 | tf_op jit(solution)/shard_map/pallas_call | solution.py:503
  44.5 0.6 %collective-permute-done.8.other_ref = f32[48,144]{1,0:T(8,128)S(1)} collective-permute-done((f32[48,144]{1,0:T(8,128)S(1)}, f32[48,144]{1,0:T(8,128)S(1)}, u32[]{:S(2)}, u32[]{:S(2)}) %collective-permute-start.8) | collective-permute-done | bytes 27680 | tf_op jit(solution)/shard_map/ppermute | solution.py:524
  45.0 0.9 %shard_map.91 = f32[16,16,27]{2,1,0:T(8,128)} custom-call(f32[48,144]{1,0:T(8,128)S(1)} %add.25.own_ref, f32[48,144]{1,0:T(8,128)S(1)} %collective-permute-done.8.other_ref, bf16[3,144,512]{2,1,0:T(8,128)(2,1)S(1)} %get-tuple-element.44.order_ref, f32[8,128]{1,0:T(8,128)S(1)} %get-tuple-element.45.done_ref), custom_call_target="tpu_custom_call" | custom-call | flops 100000000 | bytes 2000000 | tf_op jit(solution)/shard_map/pallas_call | solution.py:503
  (15 shorter events, 0.1 us)
Async XLA Ops:
  0.6 7.3 %copy-start = (bf16[16,8,8,128]{3,2,1,0:T(8,128)(2,1)S(1)}, bf16[16,8,8,128]{3,2,1,0:T(8,128)(2,1)}, u32[]{:S(2)}) copy-start(bf16[16,8,8,128]{3,2,1,0:T(8,128)(2,1)} %cot_ref.5) | copy-start | bytes 786436
  0.6 7.3 %copy-start.1 = (bf16[512,16,64]{0,2,1:T(8,128)(2,1)S(1)}, bf16[512,16,64]{0,2,1:T(8,128)(2,1)}, u32[]{:S(2)}) copy-start(bf16[512,16,64]{0,2,1:T(8,128)(2,1)} %param.7) | copy-start | bytes 3145732
  1.8 7.6 %collective-permute-start = (bf16[16,8,128]{2,1,0:T(8,128)(2,1)S(1)}, bf16[16,8,128]{2,1,0:T(8,128)(2,1)S(1)}, u32[]{:S(2)}, u32[]{:S(2)}) collective-permute-start(bf16[16,8,128]{2,1,0:T(8,128)(2,1)S(1)} %bitcast.31), channel_id=1, source_target_pairs={{0,1},{1,0},{2,3},{3,2},{4,5},{5,4},{6,7},{7,6},{8,9},{9,8},{10,11... | collective-permute-start | bytes 98312 | tf_op jit(solution)/shard_map/ppermute | solution.py:534
  4.8 5.4 %collective-permute-start.3 = (bf16[16,16,64]{2,1,0:T(8,128)(2,1)}, bf16[16,16,64]{2,1,0:T(8,128)(2,1)S(1)}, u32[]{:S(2)}, u32[]{:S(2)}) collective-permute-start(bf16[16,16,64]{2,1,0:T(8,128)(2,1)} %bitcast.28), channel_id=1, source_target_pairs={{0,1},{1,0},{2,3},{3,2},{4,5},{5,4},{6,7},{7,6},{8,9},{9,8},{10,11... | collective-permute-start | bytes 98312 | tf_op jit(solution)/shard_map/ppermute | solution.py:532
  4.9 0.8 %copy-start.3 = (bf16[27,16,16]{0,2,1:T(8,128)(2,1)S(1)}, bf16[27,16,16]{0,2,1:T(8,128)(2,1)}, u32[]{:S(2)}) copy-start(bf16[27,16,16]{0,2,1:T(8,128)(2,1)} %param.8) | copy-start | bytes 41476
  7.0 0.9 %copy-start.5 = (bf16[3,160,768]{2,1,0:T(8,128)(2,1)}, bf16[3,160,768]{2,1,0:T(8,128)(2,1)S(1)}, u32[]{:S(2)}) copy-start(bf16[3,160,768]{2,1,0:T(8,128)(2,1)S(1)} %get-tuple-element.27.conv_ref) | copy-start | bytes 2211844
  7.8 2.4 %copy-start.2 = (bf16[27,64,64]{2,1,0:T(8,128)(2,1)S(1)}, bf16[27,64,64]{2,1,0:T(8,128)(2,1)}, u32[]{:S(2)}) copy-start(bf16[27,64,64]{2,1,0:T(8,128)(2,1)} %enc_ref.3) | copy-start | bytes 663556
  7.8 2.4 %copy-start.4 = (bf16[64,16,1,16]{0,3,2,1:T(8,128)(2,1)S(1)}, bf16[64,16,1,16]{0,3,2,1:T(8,128)(2,1)}, u32[]{:S(2)}) copy-start(bf16[64,16,1,16]{0,3,2,1:T(8,128)(2,1)} %param.5) | copy-start | bytes 98308
  9.4 3.4 %collective-permute-start.2 = (bf16[144,128]{1,0:T(8,128)(2,1)S(1)}, bf16[144,128]{1,0:T(8,128)(2,1)S(1)}, u32[]{:S(2)}, u32[]{:S(2)}) collective-permute-start(bf16[144,128]{1,0:T(8,128)(2,1)S(1)} %pad_maximum_fusion.1), channel_id=1, source_target_pairs={{0,2},{4,6},{8,10},{12,14},{16,18},{20,22},{24,26},{28,30},{2,0},{... | collective-permute-start | bytes 110600 | tf_op jit(solution)/shard_map/ppermute | solution.py:552
  9.5 3.3 %collective-permute-start.1 = (bf16[144,128]{1,0:T(8,128)(2,1)S(1)}, bf16[144,128]{1,0:T(8,128)(2,1)S(1)}, u32[]{:S(2)}, u32[]{:S(2)}) collective-permute-start(bf16[144,128]{1,0:T(8,128)(2,1)S(1)} %pad_maximum_fusion), channel_id=1, source_target_pairs={{2,4},{6,8},{10,12},{14,16},{18,20},{22,24},{26,28},{4,2},{8,6},{1... | collective-permute-start | bytes 110600 | tf_op jit(solution)/shard_map/ppermute | solution.py:552
  10.2 2.6 %copy-start.6 = (bf16[3,160,768]{2,1,0:T(8,128)(2,1)S(1)}, bf16[3,160,768]{2,1,0:T(8,128)(2,1)}, u32[]{:S(2)}) copy-start(bf16[3,160,768]{2,1,0:T(8,128)(2,1)} %copy-done.5) | copy-start | bytes 2211844
  12.8 3.2 %copy-start.7 = (f32[256,128]{1,0:T(8,128)}, f32[256,128]{1,0:T(8,128)S(1)}, u32[]{:S(2)}) copy-start(f32[256,128]{1,0:T(8,128)S(1)} %get-tuple-element.35.pre_ref) | copy-start | bytes 393220
  12.8 3.2 %copy-start.9 = (bf16[288,384]{1,0:T(8,128)(2,1)}, bf16[288,384]{1,0:T(8,128)(2,1)S(1)}, u32[]{:S(2)}) copy-start(bf16[288,384]{1,0:T(8,128)(2,1)S(1)} %get-tuple-element.38.dark3_ref) | copy-start | bytes 663556
  16.1 4.2 %collective-permute-start.4 = (f32[48,144]{1,0:T(8,128)S(1)}, f32[48,144]{1,0:T(8,128)S(1)}, u32[]{:S(2)}, u32[]{:S(2)}) collective-permute-start(f32[48,144]{1,0:T(8,128)S(1)} %get-tuple-element.32), channel_id=1, source_target_pairs={{0,1},{1,0},{2,3},{3,2},{4,5},{5,4},{6,7},{7,6},{8,9},{9,8},{10,11... | collective-permute-start | bytes 82952 | tf_op jit(solution)/shard_map/ppermute | solution.py:524
  18.1 19.0 %copy-start.8 = (f32[256,128]{1,0:T(8,128)S(1)}, f32[256,128]{1,0:T(8,128)}, u32[]{:S(2)}) copy-start(f32[256,128]{1,0:T(8,128)} %copy-done.7) | copy-start | bytes 393220
  20.2 22.0 %copy-start.10 = (bf16[288,384]{1,0:T(8,128)(2,1)S(1)}, bf16[288,384]{1,0:T(8,128)(2,1)}, u32[]{:S(2)}) copy-start(bf16[288,384]{1,0:T(8,128)(2,1)} %copy-done.9) | copy-start | bytes 663556
  20.2 22.0 %all-to-all-start = ((bf16[32,40,128]{2,1,0:T(8,128)(2,1)}), bf16[32,40,128]{2,1,0:T(8,128)(2,1)S(1)}, u32[]{:S(2)}, u32[]{:S(2)}) async-start(bf16[32,40,128]{2,1,0:T(8,128)(2,1)} %shard_map.88), calls=%async_computation | async-start | bytes 655360 | tf_op jit(solution)/shard_map/all_to_all | solution.py:628
  28.5 1.3 %collective-permute-start.5 = (f32[48,144]{1,0:T(8,128)S(1)}, f32[48,144]{1,0:T(8,128)S(1)}, u32[]{:S(2)}, u32[]{:S(2)}) collective-permute-start(f32[48,144]{1,0:T(8,128)S(1)} %add.22), channel_id=1, source_target_pairs={{0,2},{1,3},{2,0},{3,1},{4,6},{5,7},{6,4},{7,5},{8,10},{9,11},{10,... | collective-permute-start | bytes 82952 | tf_op jit(solution)/shard_map/ppermute | solution.py:524
  29.9 5.9 %collective-permute-start.6 = (f32[48,144]{1,0:T(8,128)S(1)}, f32[48,144]{1,0:T(8,128)S(1)}, u32[]{:S(2)}, u32[]{:S(2)}) collective-permute-start(f32[48,144]{1,0:T(8,128)S(1)} %add.23), channel_id=1, source_target_pairs={{0,4},{1,5},{2,6},{3,7},{4,0},{5,1},{6,2},{7,3},{8,12},{9,13},{10,... | collective-permute-start | bytes 82952 | tf_op jit(solution)/shard_map/ppermute | solution.py:524
  35.8 4.2 %collective-permute-start.7 = (f32[48,144]{1,0:T(8,128)S(1)}, f32[48,144]{1,0:T(8,128)S(1)}, u32[]{:S(2)}, u32[]{:S(2)}) collective-permute-start(f32[48,144]{1,0:T(8,128)S(1)} %add.24), channel_id=1, source_target_pairs={{0,8},{1,9},{2,10},{3,11},{4,12},{5,13},{6,14},{7,15},{8,0},{9,1},... | collective-permute-start | bytes 82952 | tf_op jit(solution)/shard_map/ppermute | solution.py:524
  40.0 5.1 %collective-permute-start.8 = (f32[48,144]{1,0:T(8,128)S(1)}, f32[48,144]{1,0:T(8,128)S(1)}, u32[]{:S(2)}, u32[]{:S(2)}) collective-permute-start(f32[48,144]{1,0:T(8,128)S(1)} %add.25.own_ref), channel_id=1, source_target_pairs={{0,16},{1,17},{2,18},{3,19},{4,20},{5,21},{6,22},{7,23},{8,24},{9,... | collective-permute-start | bytes 82952 | tf_op jit(solution)/shard_map/ppermute | solution.py:524

commit v4 on v3

--- a/solution.py
+++ b/solution.py
@@ -10,6 +10,7 @@
 
 RATIO = 8
 SPAN = 16
+LAST_STEPS = 2
 F32 = jnp.float32
 BF16 = jnp.bfloat16
 VMEM_LIMIT = 48 * 1024 * 1024
@@ -32,6 +33,13 @@
 
 def dot_tn(left, right):
     return lax.dot_general(left, right, (((0,), (0,)), ((), ())), preferred_element_type=F32)
+
+
+def split(values):
+    high = values.astype(BF16)
+    rest = values - high.astype(F32)
+    middle = rest.astype(BF16)
+    return high, middle, (rest - middle.astype(F32)).astype(BF16)
 
 
 def iota(shape, dim):
@@ -74,7 +82,7 @@
     ref[2 * rows : 3 * rows, lanes] = lane_shift(values, -1).astype(BF16)
 
 
-def taps_kernel(dec_ref, conv_ref, back_ref):
+def band_taps(dec_ref, conv_ref, back_ref):
     fine_ch = dec_ref.shape[0]
     rows = fine_ch * (RATIO + 2)
     square = fine_ch * fine_ch
@@ -136,30 +144,51 @@
     ).astype(BF16)
 
 
-def table_kernel(place_ref, table_ref, cot_ref, wide_ref, first_ref, second_ref):
-    last = cot_ref.shape[1] - 1
+def table_kernel(
+    place_ref, table_hbm, cot_hbm, wide_ref, first_ref, second_ref, table_ref, sems
+):
+    last = cot_hbm.shape[1] - 1
     even = lax.rem(place_ref[0], 2) == 0
-    first_ref[...] = cot_ref[:, jnp.where(even, last, 0)]
-    second_ref[...] = cot_ref[:, jnp.where(even, 0, last)]
     fine_ch, chans, subs = table_ref.shape
+    half = fine_ch // 2
+    loads = [
+        pltpu.make_async_copy(
+            table_hbm.at[n * half : (n + 1) * half],
+            table_ref.at[n * half : (n + 1) * half],
+            sems.at[n],
+        )
+        for n in range(2)
+    ]
+    planes = [
+        pltpu.make_async_copy(cot_hbm.at[:, jnp.where(even, last, 0)], first_ref, sems.at[2]),
+        pltpu.make_async_copy(cot_hbm.at[:, jnp.where(even, 0, last)], second_ref, sems.at[3]),
+    ]
+    for copy in loads + planes:
+        copy.start()
     pairs = RATIO * RATIO
     row = row_index(subs)
     position = row % pairs // RATIO * pairs + (RATIO - 1 - row % RATIO) * RATIO + row // pairs
     pick = one_hot(iota((subs, subs), 1) == position)
-    turned = dot_nt(pick, table_ref[...].reshape(fine_ch * chans, subs))
     two = 2 * chans
     low = iota((pairs, two), 1) < chans
-    for p in range(fine_ch // 2):
-        lanes = slice(p * two, (p + 1) * two)
-        for q in range(RATIO // 2):
-            even = turned[2 * q * pairs : (2 * q + 1) * pairs, lanes]
-            odd = turned[(2 * q + 1) * pairs : (2 * q + 2) * pairs, lanes]
-            first = jnp.where(low, even, pltpu.roll(odd, chans, 1))
-            second = jnp.where(low, pltpu.roll(even, chans, 1), odd)
-            both = jnp.concatenate(
-                [first.reshape(RATIO, RATIO, two), second.reshape(RATIO, RATIO, two)], 1
-            )
-            wide_ref[:, p * SPAN : (p + 1) * SPAN, q * two : (q + 1) * two] = both.astype(BF16)
+    for n in range(2):
+        loads[n].wait()
+        part = table_ref[n * half : (n + 1) * half].reshape(half * chans, subs)
+        turned = dot_nt(pick, part)
+        for p in range(half // 2):
+            lanes = slice(p * two, (p + 1) * two)
+            top = (n * half // 2 + p) * SPAN
+            for q in range(RATIO // 2):
+                even = turned[2 * q * pairs : (2 * q + 1) * pairs, lanes]
+                odd = turned[(2 * q + 1) * pairs : (2 * q + 2) * pairs, lanes]
+                first = jnp.where(low, even, pltpu.roll(odd, chans, 1))
+                second = jnp.where(low, pltpu.roll(even, chans, 1), odd)
+                both = jnp.concatenate(
+                    [first.reshape(RATIO, RATIO, two), second.reshape(RATIO, RATIO, two)], 1
+                )
+                wide_ref[:, top : top + SPAN, q * two : (q + 1) * two] = both.astype(BF16)
+    for copy in planes:
+        copy.wait()
 
 
 def shift_rows(values, width):
@@ -186,9 +215,9 @@
 
 
 def encode_kernel(
-    place_ref, enc_ref, wide_ref, *refs, depth
+    place_ref, dec_ref, enc_ref, wide_ref, *refs, depth
 ):
-    *dark_refs, pre_ref, encoded_ref, dark3_ref, up_ref, pad_ref = refs
+    *dark_refs, conv_ref, back_ref, pre_ref, encoded_ref, dark3_ref, up_ref, pad_ref = refs
     planes, width, chans = dark_refs[0].shape[-3:]
     main = wide_ref.shape[1]
     fine_ch = main // RATIO
@@ -218,6 +247,7 @@
         dot_nt(dark3_ref[a * width : a * width + cells], weights[a]) for a in range(3)
     )
     pre_ref[...] = pre
+    band_taps(dec_ref, conv_ref, back_ref)
     encoded = jax.nn.silu(pre).astype(BF16)
     encoded_ref[...] = encoded
     pad_ref[...] = jnp.zeros(pad_ref.shape, F32)
@@ -271,16 +301,25 @@
 
 def decode_kernel(
     place_ref, cot_ref, x_low_ref, x_high_ref, z_low_ref, z_high_ref, conv_ref, up_ref,
-    grad_ref, total_ref, *, planes_z
+    grad_ref, total_ref, *, planes_x, planes_z
 ):
     fine_ch, planes, depth, width = cot_ref.shape
     main = fine_ch * depth
     rows = conv_ref.shape[1]
     wide = (planes + 2) * width
     own = planes * width
-    pre = sum(dot(conv_ref[a], up_ref[:, a * width : a * width + wide]) for a in range(3))
+
+    def convolve(first, count):
+        low, high = first * width, (first + count) * width
+        return sum(
+            dot(conv_ref[a], up_ref[:, a * width + low : a * width + high]) for a in range(3)
+        )
+
+    step = 2
+    ahead = convolve(0, step)
     own_z = place_ref[1]
     valid = (own_z > 0, own_z < planes_z - 1)
+    own_x = place_ref[0]
     shape = (main, main)
     turn = iota(shape, 1) == row_index(main) % fine_ch * planes + row_index(main) // fine_ch
     sides = [
@@ -288,19 +327,24 @@
         for side, ref in enumerate((z_low_ref, z_high_ref))
     ]
     for x in range(planes + 2):
+        if x % step == 0:
+            pre = ahead
+            if x + step < planes + 2:
+                ahead = convolve(x + step, step)
         if 0 < x <= planes:
             inner = cot_ref[:, x - 1].astype(F32).reshape(main, width)
             edge = [side[(x - 1) * fine_ch : x * fine_ch] for side in sides]
         else:
             outer = x_low_ref if x == 0 else x_high_ref
-            inner = outer[:main].astype(F32)
+            inside = own_x > 0 if x == 0 else own_x < planes_x - 1
+            inner = jnp.where(inside, outer[:main].astype(F32), 0.0)
             edge = []
             for side in range(2):
                 first = main + side * (outer.shape[0] - main - fine_ch)
                 corner = outer[first : first + fine_ch].astype(F32)
-                edge.append(jnp.where(valid[side], corner, 0.0))
+                edge.append(jnp.where(valid[side] & inside, corner, 0.0))
         cot = jnp.concatenate([inner] + edge, 0)
-        grad = (cot * slope_of(pre[:, x * width : (x + 1) * width])).astype(BF16)
+        grad = (cot * slope_of(pre[:, x % step * width : (x % step + 1) * width])).astype(BF16)
         store_shifts(grad_ref, x, grad.astype(F32))
     grads = jnp.concatenate(
         [grad_ref[e * rows : e * rows + main, width : width + own] for e in (2, 1, 0)], 0
@@ -316,27 +360,19 @@
             halves.append(jnp.sum(pltpu.roll(part, 0, 2, stride=1, stride_axis=1), 1))
         sums.append(jnp.concatenate(halves, 1))
     shape = (3 * fine_ch, taps)
-    fold = jnp.where(
-        (iota(shape, 1) // SPAN == iota(shape, 0) % fine_ch)
-        & (iota(shape, 1) % SPAN == 10 - iota(shape, 0) // fine_ch),
-        1.0,
-        0.0,
-    )
-    total_ref[...] = lax.dot_general(
-        fold,
-        jnp.concatenate(sums, 0),
-        (((1,), (1,)), ((), ())),
-        precision=lax.Precision.HIGHEST,
-        preferred_element_type=F32,
-    )
-
-
-def spread_kernel(cot_ref, grad_ref, back_ref, wide_ref, send_ref):
+    fold = one_hot(
+        iota(shape, 1)
+        == row_index(shape[0]) % fine_ch * SPAN + 10 - row_index(shape[0]) // fine_ch
+    )
+    total_ref[...] = sum(dot_nt(fold, part) for part in split(jnp.concatenate(sums, 0)))
+
+
+def spread_kernel(cot_ref, grad_ref, back_ref, wide_ref, send_hbm, send_ref, cells_ref, sems):
     fine_ch, planes, depth, width = cot_ref.shape
     main = fine_ch * depth
     own = planes * width
     chans = wide_ref.shape[2] // RATIO
-    owners, chunk, _ = send_ref.shape
+    owners, chunk, _ = send_hbm.shape
     span = chunk - RATIO
     taps = grad_ref.shape[0]
     back = sum(
@@ -351,6 +387,13 @@
     column = iota((main, main), 1)
     turn = one_hot((row % fine_ch == column // RATIO) & (row // fine_ch == column % RATIO))
     turned = dot(turn, up).astype(BF16)
+    for owner in range(owners):
+        first = owner * RATIO * RATIO // owners
+        x = first // RATIO
+        top = first % RATIO * fine_ch
+        send_ref[owner] = turned[top : top + span, x * width : (x + 1) * width]
+    store = pltpu.make_async_copy(send_ref, send_hbm.at[:, :span], sems.at[0])
+    store.start()
     flip = one_hot(
         (row // RATIO == column // RATIO) & (row % RATIO + column % RATIO == RATIO - 1)
     )
@@ -370,11 +413,11 @@
     half = cells.shape[0] // 2
     cells = jnp.where(iota((half, two), 1) < chans, cells[:half], cells[half:]).astype(BF16)
     for owner in range(owners):
-        first = owner * RATIO * RATIO // owners
-        x = first // RATIO
-        top = first % RATIO * fine_ch
-        send_ref[owner, :span] = turned[top : top + span, x * width : (x + 1) * width]
-        send_ref[owner, span:] = cells
+        cells_ref[owner] = cells
+    last = pltpu.make_async_copy(cells_ref, send_hbm.at[:, span:], sems.at[1])
+    last.start()
+    store.wait()
+    last.wait()
 
 
 def widen_kernel(
@@ -412,17 +455,15 @@
         order_ref[b] = one_hot(column == row % fine_ch * step + tap + 3 * b)
 
 
-def final_kernel(own_ref, other_ref, order_ref, done_ref, out_ref, *, scale):
-    total = (own_ref[...] + other_ref[...]) * scale
+def final_kernel(order_ref, done_ref, *refs, scale):
+    *parts, out_ref = refs
+    total = sum(part[...] for part in parts) * scale
     fine_ch = out_ref.shape[0]
-    high = total.astype(BF16)
-    rest = total - high.astype(F32)
-    middle = rest.astype(BF16)
-    low = (rest - middle.astype(F32)).astype(BF16)
+    parts = split(total)
     field = 0.0
     for b in range(3):
         rows = slice(b * fine_ch, (b + 1) * fine_ch)
-        field = field + dot(jnp.concatenate([high[rows], middle[rows], low[rows]], 0), order_ref[b])
+        field = field + dot(jnp.concatenate([part[rows] for part in parts], 0), order_ref[b])
     field = field[:fine_ch] + field[fine_ch : 2 * fine_ch] + field[2 * fine_ch :]
     step = field.shape[1] // fine_ch
     for o in range(fine_ch):
@@ -497,14 +538,24 @@
     up_out[...] = (sums * scale).reshape(pairs * RATIO, fine_ch, chans)
 
 
-def call(kernel, out_shape, args, scratch=(), scalars=0, flops=1e8):
+def call(kernel, out_shape, args, scratch=(), scalars=0, flops=1e8, hbm=(), hbm_out=()):
     specs = [pl.BlockSpec(memory_space=pltpu.SMEM)] * scalars
-    specs += [pl.BlockSpec(memory_space=VMEM)] * (len(args) - scalars)
+    specs += [
+        pl.BlockSpec(memory_space=pltpu.HBM if n in hbm else VMEM)
+        for n in range(scalars, len(args))
+    ]
+    args = [
+        pltpu.with_memory_space_constraint(arg, pltpu.HBM) if n in hbm else arg
+        for n, arg in enumerate(args)
+    ]
     return pl.pallas_call(
         kernel,
         out_shape=[jax.ShapeDtypeStruct(*s) for s in out_shape],
         in_specs=specs,
-        out_specs=[pl.BlockSpec(memory_space=VMEM)] * len(out_shape),
+        out_specs=[
+            pl.BlockSpec(memory_space=pltpu.HBM if n in hbm_out else VMEM)
+            for n in range(len(out_shape))
+        ],
         scratch_shapes=list(scratch),
         compiler_params=pltpu.CompilerParams(vmem_limit_bytes=VMEM_LIMIT),
         cost_estimate=pl.CostEstimate(
@@ -540,16 +591,23 @@
 
 def exchange_width(planes, faces):
     count = lax.axis_size("wide")
+    depth = lax.axis_size("narrow")
     last = faces[0].shape[1] - 1
     even = lax.axis_index("wide") % 2 == 0
     got = []
     for odd in range(2):
-        pairs = [(i, i + 1) for i in range(odd, count - 1, 2)]
-        pairs += [(target, source) for source, target in pairs]
+        partner = {}
+        for x in range(count):
+            other = x + 1 if x % 2 == odd else x - 1
+            for z in range(depth):
+                if 0 <= other < count:
+                    partner[x * depth + z] = other * depth + z
+                elif depth % 2 == 0:
+                    partner[x * depth + z] = x * depth + (z ^ 1)
         plane = jnp.where(even, 0, last) if odd else jnp.where(even, last, 0)
         edges = [lax.dynamic_index_in_dim(face, plane, 1, False) for face in faces]
         send = jnp.concatenate([planes[odd], *edges], 0)
-        got.append(lax.ppermute(send, "wide", pairs))
+        got.append(lax.ppermute(send, AXES, list(partner.items())))
     return jnp.where(even, got[1], got[0]), jnp.where(even, got[0], got[1])
 
 
@@ -570,37 +628,35 @@
     taps = fine_ch * SPAN
     main = fine_ch * RATIO
     face = (fine_ch * fine_depth, fine_width)
-    conv, back = call(
-        taps_kernel,
-        [((3, rows, 3 * taps), BF16), ((main, 9 * rows), BF16)],
-        (w_dec.transpose(1, 2, 0),),
-        flops=1e9,
-    )
     outer = (fine_ch, fine_depth, fine_width)
     wide_table, first_plane, second_plane = call(
         table_kernel,
         [((RATIO, main, RATIO * chans), BF16), (outer, BF16), (outer, BF16)],
         (where, up_weight.transpose(1, 2, 0), cotangent),
+        scratch=[VMEM((fine_ch, chans, subs), BF16), pltpu.SemaphoreType.DMA((4,))],
         scalars=1,
+        hbm=(1, 2),
         flops=1e9,
     )
     outer_planes = [plane.reshape(face) for plane in (first_plane, second_plane)]
     x_low, x_high = exchange_width(outer_planes, faces)
-    enc_pre, encoded, dark3, upsampled = call(
+    conv, back, enc_pre, encoded, dark3, upsampled = call(
         functools.partial(encode_kernel, depth=depth),
         [
+            ((3, rows, 3 * taps), BF16),
+            ((main, 9 * rows), BF16),
             ((cells, lanes), F32),
             ((cells, lanes), BF16),
             ((cells + 2 * width, 3 * lanes), BF16),
             ((3 * taps, (RATIO + 4) * fine_width), BF16),
         ],
-        (where, w_enc, wide_table, *dark_planes),
+        (where, w_dec.transpose(1, 2, 0), w_enc, wide_table, *dark_planes),
         scratch=[VMEM((planes + 2, depth + 2, width, 2 * chans), F32)],
         scalars=1,
         flops=2e9,
     )
     dec_grad, dec_sum = call(
-        functools.partial(decode_kernel, planes_z=depth),
+        functools.partial(decode_kernel, planes_x=planes, planes_z=depth),
         [((3 * rows, (RATIO + 2) * fine_width), BF16), ((3 * fine_ch, 9 * fine_ch), F32)],
         (where, cotangent, x_low, x_high, faces[0], faces[-1], conv, upsampled),
         scalars=1,
@@ -611,20 +667,28 @@
         spread_kernel,
         [((owners, chunk, fine_width), BF16)],
         (cotangent, dec_grad, back, wide_table),
+        scratch=[
+            VMEM((owners, chunk - RATIO, fine_width), BF16),
+            VMEM((owners, RATIO, fine_width), BF16),
+            pltpu.SemaphoreType.DMA((2,)),
+        ],
         flops=2e9,
+        hbm_out=(0,),
     )
     steps = [1 << n for n in range(owners.bit_length() - 1)]
     if owners & (owners - 1):
         dec_sum = lax.psum(dec_sum, AXES)
         steps = []
     steps = sorted(steps)
-    received = jnp.zeros_like(dec_sum)
-    for n, step in enumerate(steps):
-        received = swapped(dec_sum, step)
-        if n < len(steps) - 1:
-            dec_sum = dec_sum + received
-        if n == 0:
+    one_by_one = steps[: max(1, len(steps) - LAST_STEPS)]
+    for step in one_by_one:
+        dec_sum = dec_sum + swapped(dec_sum, step)
+        if step == steps[0]:
             send, dec_sum = lax.optimization_barrier((send, dec_sum))
+    sums = [0]
+    for step in steps[len(one_by_one) :]:
+        sums += [step + other for other in sums]
+    received = [swapped(dec_sum, step) for step in sums[1:]]
     got = lax.all_to_all(send, AXES, 0, 0, tiled=True)
     enc_spread, enc_slope, enc_taps, order = call(
         widen_kernel,
@@ -659,7 +723,7 @@
     (grad_dec,) = call(
         functools.partial(final_kernel, scale=fine_scale),
         [((fine_ch, fine_ch, 27), F32)],
-        (dec_sum, received, order, done),
+        (order, done, dec_sum, *received),
         flops=1e8,
     )
     return grad_dark.transpose(2, 0, 1)[:, :, None], grad_enc, grad_up, grad_dec.transpose(2, 0, 1)

time: 46.2 us -> 42.6 us (0.922)
  starting transfers between devices: 19.8 us -> 17.1 us
  local copies, waits for them, and re-layouts: 2.9 us -> 1.14 us
  Pallas kernels: 14.4 us -> 15.1 us
    all_to_all x1, starting transfers between devices: 8.31 us -> 4.91 us  [on_device(): got = lax.all_to_all(send, AXES, 0, 0, tiled=True)]
    unnamed x25 -> x11, local copies, waits for them, and re-layouts: 1.75 us -> 0.04 us
    ppermute x2, starting transfers between devices: 0.73 us -> 2.07 us  [exchange_width(): got.append(lax.ppermute(send, AXES, list(partner.items())))]
    pallas_call x8 -> x7, Pallas kernels: 14.4 us -> 15.1 us  [call(): pl.pallas_call(kernel, out_shape=[jax.ShapeDtypeStruct(*s) for s in out_s...]
    ppermute x5 -> x6, starting transfers between devices: 7.67 us -> 7.05 us  [swapped(): return lax.ppermute(value, AXES, [(i, i ^ step) for i in range(count)])]
    ppermute x5 -> x6, waiting for transfers between devices: 7.76 us -> 8.01 us  [swapped(): return lax.ppermute(value, AXES, [(i, i ^ step) for i in range(count)])]
  transfers between devices with their start and end apart: 10 -> 11, of which waited for: 5 -> 5; matrix products, arithmetic and copies ran while one was open for 0% -> 0% of each run, Pallas kernels for 22% -> 27%
where the time goes in v4:
time: 42.6 us; the launch traced here: 42.4 us
  starting transfers between devices  17.1 us (40%)
  Pallas kernels  15.1 us (35%)
  waiting for transfers between devices  8.04 us (19%)
  local copies, waits for them, and re-layouts  1.14 us (3%)
  between operations  0.86 us (2%)
    pallas_call x7, Pallas kernels, call(): pl.pallas_call(kernel, out_shape=[jax.ShapeDtypeStruct(*s) for s in out_s...  15.1 us
    ppermute x6, waiting for transfers between devices, swapped(): return lax.ppermute(value, AXES, [(i, i ^ step) for i in range(count)])  8.01 us
    ppermute x6, starting transfers between devices, swapped(): return lax.ppermute(value, AXES, [(i, i ^ step) for i in range(count)])  7.05 us
    all_to_all x1, starting transfers between devices, on_device(): got = lax.all_to_all(send, AXES, 0, 0, tiled=True)  4.91 us
    ppermute x1, starting transfers between devices, exchange_depth(): lax.ppermute(lax.dynamic_index_in_dim(cotangent, z, 2, False), 'narrow',...  3 us
    ppermute x2, starting transfers between devices, exchange_width(): got.append(lax.ppermute(send, AXES, list(partner.items())))  2.07 us
    dynamic_slice x1, local copies, waits for them, and re-layouts, exchange_depth(): lax.dynamic_index_in_dim(cotangent, z, 2, False)  1.08 us
  transfers between devices with their start and end apart: 11, of which 5 were waited for; matrix products, arithmetic and copies ran while one was open for 0% of the time, Pallas kernels for 27%

profile of v4, /device:TPU:0, one launch (start us, length us, event | category | flops | bytes accessed | tf_op | source)
XLA Modules:
  0.0 42.4 jit_solution(17352001643574829174)
XLA Ops:
  0.6 0.0 copy-start.3
  0.6 0.0 copy-start.1
  0.7 0.0 copy-start.2
  0.7 1.1 %constant_dynamic-slice_fusion.2 = bf16[16,8,1,128]{3,2,1,0:T(2,128)(2,1)S(1)} fusion(bf16[16,8,8,128]{3,2,1,0:T(8,128)(2,1)} %cot_ref.3, s32[]{:T(128)S(6)} %select_n.36), kind=kLoop, calls=%fused_computation.9 | loop fusion | bytes 65540 | tf_op jit(solution)/shard_map/jit(dynamic_index_in_dim)/dynamic_slice | solution.py:585
  1.8 3.0 %collective-permute-start = (bf16[16,8,128]{2,1,0:T(8,128)(2,1)S(1)}, bf16[16,8,128]{2,1,0:T(8,128)(2,1)S(1)}, u32[]{:S(2)}, u32[]{:S(2)}) collective-permute-start(bf16[16,8,128]{2,1,0:T(8,128)(2,1)S(1)} %bitcast.30), channel_id=1, source_target_pairs={{0,1},{1,0},{2,3},{3,2},{4,5},{5,4},{6,7},{7,6},{8,9},{9,8},{10,11... | collective-permute-start | bytes 98312 | tf_op jit(solution)/shard_map/ppermute | solution.py:585
  4.8 0.1 collective-permute-start.3
  4.9 0.1 pad_add_fusion.place_ref
  4.9 2.8 %shard_map.84 = (bf16[8,128,512]{2,1,0:T(8,128)(2,1)S(1)}, bf16[16,8,128]{2,1,0:T(8,128)(2,1)S(1)}, bf16[16,8,128]{2,1,0:T(8,128)(2,1)S(1)}) custom-call(s32[2]{0:T(128)S(1)} %pad_add_fusion.place_ref, bf16[16,64,512]{2,1,0:T(8,128)(2,1)} %bitcast.33, bf16[16,8,8,128]{3,2,1,0:T(8,128)(2,1)} %cot_ref.3), custom_call_target="tpu_custom_call" | custom-call | flops 1000000000 | bytes 2000000 | tf_op jit(solution)/shard_map/pallas_call | solution.py:551
  7.7 0.0 collective-permute-done.z_low_ref.z_high_ref
  7.8 0.1 collective-permute-start.2
  7.9 2.0 %collective-permute-start.1 = (bf16[144,128]{1,0:T(8,128)(2,1)S(1)}, bf16[144,128]{1,0:T(8,128)(2,1)S(1)}, u32[]{:S(2)}, u32[]{:S(2)}) collective-permute-start(bf16[144,128]{1,0:T(8,128)(2,1)S(1)} %pad_maximum_fusion), channel_id=1, source_target_pairs={{0,1},{1,0},{2,4},{3,5},{4,2},{5,3},{6,8},{7,9},{8,6},{9,7},{10,12... | collective-permute-start | bytes 110600 | tf_op jit(solution)/shard_map/ppermute | solution.py:610
  9.9 0.0 collective-permute-done.3.refs_1_
  9.9 0.0 copy-done.3
  9.9 0.0 copy-done.1
  9.9 0.0 copy-done.2
  9.9 0.0 copy-start
  9.9 3.5 %shard_map.85 = (bf16[3,160,768]{2,1,0:T(8,128)(2,1)S(1)}, bf16[128,1440]{1,0:T(8,128)(2,1)S(1)}, f32[256,128]{1,0:T(8,128)S(1)}, bf16[256,128]{1,0:T(8,128)(2,1...) custom-call(s32[2]{0:T(128)S(1)} %pad_add_fusion.place_ref, bf16[16,16,27]{2,1,0:T(8,128)(2,1)S(1)} %bitcast.26, ...), custom_call_target="tpu_custom_call" | custom-call | flops 2000000000 | bytes 2000000 | tf_op jit(solution)/shard_map/pallas_call | solution.py:551
  13.5 0.0 collective-permute-done.2
  13.5 0.0 collective-permute-done.1
  13.5 0.0 copy-done
  13.5 2.8 %shard_map.86 = (bf16[480,1280]{1,0:T(8,128)(2,1)S(1)}, f32[48,144]{1,0:T(8,128)S(1)}) custom-call(s32[2]{0:T(128)S(1)} %pad_add_fusion.place_ref, bf16[16,8,8,128]{3,2,1,0:T(8,128)(2,1)S(1)} %copy-done, bf16[144,128]{1,0:T(8,128)(2,1)S(1)} %get-tuple-element.55.x_low_ref, bf16[144,128]{1,0:T(8,128)(2,1)S(1)} %get-tuple-element.54.x_high_ref, ...), custom_call_target="tpu_custom_call" | custom-call | flops 2000000000 | bytes 2000000 | tf_op jit(solution)/shard_map/pallas_call | solution.py:551
  16.4 0.4 %collective-permute-start.4 = (f32[48,144]{1,0:T(8,128)S(1)}, f32[48,144]{1,0:T(8,128)S(1)}, u32[]{:S(2)}, u32[]{:S(2)}) collective-permute-start(f32[48,144]{1,0:T(8,128)S(1)} %get-tuple-element.32), channel_id=1, source_target_pairs={{0,1},{1,0},{2,3},{3,2},{4,5},{5,4},{6,7},{7,6},{8,9},{9,8},{10,11... | collective-permute-start | bytes 82952 | tf_op jit(solution)/shard_map/ppermute | solution.py:575
  16.8 1.9 %shard_map.87 = bf16[32,40,128]{2,1,0:T(8,128)(2,1)} custom-call(bf16[16,8,8,128]{3,2,1,0:T(8,128)(2,1)S(1)} %copy-done, bf16[480,1280]{1,0:T(8,128)(2,1)S(1)} %get-tuple-element.30.grad_ref, bf16[128,1440]{1,0:T(8,128)(2,1)S(1)} %get-tuple-element.31.back_ref, bf16[8,128,512]{2,1,0:T(8,128)(2,1)S(1)} %get-tuple-element.27.wide_ref), custom_call_target="tpu_custom_call" | custom-call | flops 2000000000 | bytes 2000000 | tf_op jit(solution)/shard_map/pallas_call | solution.py:551
  18.7 1.8 %collective-permute-done.4 = f32[48,144]{1,0:T(8,128)S(1)} collective-permute-done((f32[48,144]{1,0:T(8,128)S(1)}, f32[48,144]{1,0:T(8,128)S(1)}, u32[]{:S(2)}, u32[]{:S(2)}) %collective-permute-start.4) | collective-permute-done | bytes 27680 | tf_op jit(solution)/shard_map/ppermute | solution.py:575
  20.5 4.9 %all-to-all-start = ((bf16[32,40,128]{2,1,0:T(8,128)(2,1)}), bf16[32,40,128]{2,1,0:T(8,128)(2,1)S(1)}, u32[]{:S(2)}, u32[]{:S(2)}) async-start(bf16[32,40,128]{2,1,0:T(8,128)(2,1)} %shard_map.87), calls=%async_computation | async-start | bytes 655360 | tf_op jit(solution)/shard_map/all_to_all | solution.py:692
  25.4 0.3 collective-permute-start.5
  25.8 1.0 %collective-permute-done.5 = f32[48,144]{1,0:T(8,128)S(1)} collective-permute-done((f32[48,144]{1,0:T(8,128)S(1)}, f32[48,144]{1,0:T(8,128)S(1)}, u32[]{:S(2)}, u32[]{:S(2)}) %collective-permute-start.5) | collective-permute-done | bytes 27680 | tf_op jit(solution)/shard_map/ppermute | solution.py:575
  26.8 1.8 %collective-permute-start.6 = (f32[48,144]{1,0:T(8,128)S(1)}, f32[48,144]{1,0:T(8,128)S(1)}, u32[]{:S(2)}, u32[]{:S(2)}) collective-permute-start(f32[48,144]{1,0:T(8,128)S(1)} %add.20), channel_id=1, source_target_pairs={{0,4},{1,5},{2,6},{3,7},{4,0},{5,1},{6,2},{7,3},{8,12},{9,13},{10,... | collective-permute-start | bytes 82952 | tf_op jit(solution)/shard_map/ppermute | solution.py:575
  28.6 0.9 %shard_map.88 = (bf16[2048,128]{1,0:T(8,128)(2,1)S(1)}, f32[256,128]{1,0:T(8,128)S(1)}, bf16[3,384,64]{2,1,0:T(8,128)(2,1)S(1)}, bf16[3,144,512]{2,1,0:T(8,128)(2,1)S(1)}) custom-call(s32[2]{0:T(128)S(1)} %pad_add_fusion.place_ref, bf16[256,128]{1,0:T(8,128)(2,1)S(1)} %get-tuple-element.34.encoded_ref, f32[256,128]{1,0:T(8,128)S(1)} %get-tuple-element.35.pre_ref, ...), custom_call_target="tpu_custom_call" | custom-call | flops 1000000000 | bytes 2000000 | tf_op jit(solution)/shard_map/pallas_call | solution.py:551
  29.5 3.2 %collective-permute-done.6 = f32[48,144]{1,0:T(8,128)S(1)} collective-permute-done((f32[48,144]{1,0:T(8,128)S(1)}, f32[48,144]{1,0:T(8,128)S(1)}, u32[]{:S(2)}, u32[]{:S(2)}) %collective-permute-start.6) | collective-permute-done | bytes 27680 | tf_op jit(solution)/shard_map/ppermute | solution.py:575
  32.7 3.6 %collective-permute-start.9 = (f32[48,144]{1,0:T(8,128)S(1)}, f32[48,144]{1,0:T(8,128)S(1)}, u32[]{:S(2)}, u32[]{:S(2)}) collective-permute-start(f32[48,144]{1,0:T(8,128)S(1)} %add.21.refs_0_), channel_id=1, source_target_pairs={{0,24},{1,25},{2,26},{3,27},{4,28},{5,29},{6,30},{7,31},{8,16},{9,... | collective-permute-start | bytes 82952 | tf_op jit(solution)/shard_map/ppermute | solution.py:575
  36.3 0.0 collective-permute-start.8
  36.3 0.8 %collective-permute-start.7 = (f32[48,144]{1,0:T(8,128)S(1)}, f32[48,144]{1,0:T(8,128)S(1)}, u32[]{:S(2)}, u32[]{:S(2)}) collective-permute-start(f32[48,144]{1,0:T(8,128)S(1)} %add.21.refs_0_), channel_id=1, source_target_pairs={{0,8},{1,9},{2,10},{3,11},{4,12},{5,13},{6,14},{7,15},{8,0},{9,1},... | collective-permute-start | bytes 82952 | tf_op jit(solution)/shard_map/ppermute | solution.py:575
  37.1 0.0 all-to-all-done.got_ref
  37.2 2.2 %shard_map.89 = (f32[16,16,64]{2,1,0:T(8,128)}, f32[27,64,64]{2,1,0:T(8,128)}, f32[16,16,64]{2,1,0:T(8,128)}, f32[8,128]{1,0:T(8,128)S(1)}) custom-call(bf16[32,40,128]{2,1,0:T(8,128)(2,1)S(1)} %all-to-all-done.got_ref, bf16[2048,128]{1,0:T(8,128)(2,1)S(1)} %get-tuple-element.36.spread_ref, f32[256,128]{1,0:T(8,128)S(1)} %get-tuple-element.37.slope_ref, ...), custom_call_target="tpu_custom_call" | custom-call | flops 2000000000 | bytes 2000000 | tf_op jit(solution)/shard_map/pallas_call | solution.py:551
  39.4 0.0 collective-permute-done.9.refs_3_
  39.4 1.9 %collective-permute-done.8.refs_2_ = f32[48,144]{1,0:T(8,128)S(1)} collective-permute-done((f32[48,144]{1,0:T(8,128)S(1)}, f32[48,144]{1,0:T(8,128)S(1)}, u32[]{:S(2)}, u32[]{:S(2)}) %collective-permute-start.8) | collective-permute-done | bytes 27680 | tf_op jit(solution)/shard_map/ppermute | solution.py:575
  41.3 0.1 collective-permute-done.7.refs_1_
  41.4 0.9 %shard_map.90 = f32[16,16,27]{2,1,0:T(8,128)} custom-call(bf16[3,144,512]{2,1,0:T(8,128)(2,1)S(1)} %get-tuple-element.43.order_ref, f32[8,128]{1,0:T(8,128)S(1)} %get-tuple-element.44.done_ref, f32[48,144]{1,0:T(8,128)S(1)} %add.21.refs_0_, f32[48,144]{1,0:T(8,128)S(1)} %collective-permute-done.7.refs_1_, f32[48,144]{1,0:T(8,128)S(1)} %collective-permute-done.8.refs_2_, ...), custom_call_target="tpu_custom_call" | custom-call | flops 100000000 | bytes 2000000 | tf_op jit(solution)/shard_map/pallas_call | solution.py:551
  (10 shorter events, 0.1 us)
Async XLA Ops:
  0.6 9.3 %copy-start.3 = (bf16[64,16,1,16]{0,3,2,1:T(8,128)(2,1)S(1)}, bf16[64,16,1,16]{0,3,2,1:T(8,128)(2,1)}, u32[]{:S(2)}) copy-start(bf16[64,16,1,16]{0,3,2,1:T(8,128)(2,1)} %param.5) | copy-start | bytes 98308
  0.6 9.3 %copy-start.1 = (bf16[27,64,64]{2,1,0:T(8,128)(2,1)S(1)}, bf16[27,64,64]{2,1,0:T(8,128)(2,1)}, u32[]{:S(2)}) copy-start(bf16[27,64,64]{2,1,0:T(8,128)(2,1)} %enc_ref.3) | copy-start | bytes 663556
  0.7 9.3 %copy-start.2 = (bf16[27,16,16]{0,2,1:T(8,128)(2,1)S(1)}, bf16[27,16,16]{0,2,1:T(8,128)(2,1)}, u32[]{:S(2)}) copy-start(bf16[27,16,16]{0,2,1:T(8,128)(2,1)} %param.8) | copy-start | bytes 41476
  1.8 6.0 %collective-permute-start = (bf16[16,8,128]{2,1,0:T(8,128)(2,1)S(1)}, bf16[16,8,128]{2,1,0:T(8,128)(2,1)S(1)}, u32[]{:S(2)}, u32[]{:S(2)}) collective-permute-start(bf16[16,8,128]{2,1,0:T(8,128)(2,1)S(1)} %bitcast.30), channel_id=1, source_target_pairs={{0,1},{1,0},{2,3},{3,2},{4,5},{5,4},{6,7},{7,6},{8,9},{9,8},{10,11... | collective-permute-start | bytes 98312 | tf_op jit(solution)/shard_map/ppermute | solution.py:585
  4.8 5.1 %collective-permute-start.3 = (bf16[16,16,64]{2,1,0:T(8,128)(2,1)}, bf16[16,16,64]{2,1,0:T(8,128)(2,1)S(1)}, u32[]{:S(2)}, u32[]{:S(2)}) collective-permute-start(bf16[16,16,64]{2,1,0:T(8,128)(2,1)} %bitcast.27), channel_id=1, source_target_pairs={{0,1},{1,0},{2,3},{3,2},{4,5},{5,4},{6,7},{7,6},{8,9},{9,8},{10,11... | collective-permute-start | bytes 98312 | tf_op jit(solution)/shard_map/ppermute | solution.py:583
  7.8 5.7 %collective-permute-start.2 = (bf16[144,128]{1,0:T(8,128)(2,1)S(1)}, bf16[144,128]{1,0:T(8,128)(2,1)S(1)}, u32[]{:S(2)}, u32[]{:S(2)}) collective-permute-start(bf16[144,128]{1,0:T(8,128)(2,1)S(1)} %pad_maximum_fusion.1), channel_id=1, source_target_pairs={{0,2},{1,3},{2,0},{3,1},{4,6},{5,7},{6,4},{7,5},{8,10},{9,11},{10,... | collective-permute-start | bytes 110600 | tf_op jit(solution)/shard_map/ppermute | solution.py:610
  7.9 5.6 %collective-permute-start.1 = (bf16[144,128]{1,0:T(8,128)(2,1)S(1)}, bf16[144,128]{1,0:T(8,128)(2,1)S(1)}, u32[]{:S(2)}, u32[]{:S(2)}) collective-permute-start(bf16[144,128]{1,0:T(8,128)(2,1)S(1)} %pad_maximum_fusion), channel_id=1, source_target_pairs={{0,1},{1,0},{2,4},{3,5},{4,2},{5,3},{6,8},{7,9},{8,6},{9,7},{10,12... | collective-permute-start | bytes 110600 | tf_op jit(solution)/shard_map/ppermute | solution.py:610
  9.9 3.6 %copy-start = (bf16[16,8,8,128]{3,2,1,0:T(8,128)(2,1)S(1)}, bf16[16,8,8,128]{3,2,1,0:T(8,128)(2,1)}, u32[]{:S(2)}) copy-start(bf16[16,8,8,128]{3,2,1,0:T(8,128)(2,1)} %cot_ref.3) | copy-start | bytes 786436
  16.4 4.2 %collective-permute-start.4 = (f32[48,144]{1,0:T(8,128)S(1)}, f32[48,144]{1,0:T(8,128)S(1)}, u32[]{:S(2)}, u32[]{:S(2)}) collective-permute-start(f32[48,144]{1,0:T(8,128)S(1)} %get-tuple-element.32), channel_id=1, source_target_pairs={{0,1},{1,0},{2,3},{3,2},{4,5},{5,4},{6,7},{7,6},{8,9},{9,8},{10,11... | collective-permute-start | bytes 82952 | tf_op jit(solution)/shard_map/ppermute | solution.py:575
  20.5 16.6 %all-to-all-start = ((bf16[32,40,128]{2,1,0:T(8,128)(2,1)}), bf16[32,40,128]{2,1,0:T(8,128)(2,1)S(1)}, u32[]{:S(2)}, u32[]{:S(2)}) async-start(bf16[32,40,128]{2,1,0:T(8,128)(2,1)} %shard_map.87), calls=%async_computation | async-start | bytes 655360 | tf_op jit(solution)/shard_map/all_to_all | solution.py:692
  25.4 1.3 %collective-permute-start.5 = (f32[48,144]{1,0:T(8,128)S(1)}, f32[48,144]{1,0:T(8,128)S(1)}, u32[]{:S(2)}, u32[]{:S(2)}) collective-permute-start(f32[48,144]{1,0:T(8,128)S(1)} %add.19), channel_id=1, source_target_pairs={{0,2},{1,3},{2,0},{3,1},{4,6},{5,7},{6,4},{7,5},{8,10},{9,11},{10,... | collective-permute-start | bytes 82952 | tf_op jit(solution)/shard_map/ppermute | solution.py:575
  26.8 5.9 %collective-permute-start.6 = (f32[48,144]{1,0:T(8,128)S(1)}, f32[48,144]{1,0:T(8,128)S(1)}, u32[]{:S(2)}, u32[]{:S(2)}) collective-permute-start(f32[48,144]{1,0:T(8,128)S(1)} %add.20), channel_id=1, source_target_pairs={{0,4},{1,5},{2,6},{3,7},{4,0},{5,1},{6,2},{7,3},{8,12},{9,13},{10,... | collective-permute-start | bytes 82952 | tf_op jit(solution)/shard_map/ppermute | solution.py:575
  32.7 6.7 %collective-permute-start.9 = (f32[48,144]{1,0:T(8,128)S(1)}, f32[48,144]{1,0:T(8,128)S(1)}, u32[]{:S(2)}, u32[]{:S(2)}) collective-permute-start(f32[48,144]{1,0:T(8,128)S(1)} %add.21.refs_0_), channel_id=1, source_target_pairs={{0,24},{1,25},{2,26},{3,27},{4,28},{5,29},{6,30},{7,31},{8,16},{9,... | collective-permute-start | bytes 82952 | tf_op jit(solution)/shard_map/ppermute | solution.py:575
  36.3 5.0 %collective-permute-start.8 = (f32[48,144]{1,0:T(8,128)S(1)}, f32[48,144]{1,0:T(8,128)S(1)}, u32[]{:S(2)}, u32[]{:S(2)}) collective-permute-start(f32[48,144]{1,0:T(8,128)S(1)} %add.21.refs_0_), channel_id=1, source_target_pairs={{0,16},{1,17},{2,18},{3,19},{4,20},{5,21},{6,22},{7,23},{8,24},{9,... | collective-permute-start | bytes 82952 | tf_op jit(solution)/shard_map/ppermute | solution.py:575
  36.3 5.1 %collective-permute-start.7 = (f32[48,144]{1,0:T(8,128)S(1)}, f32[48,144]{1,0:T(8,128)S(1)}, u32[]{:S(2)}, u32[]{:S(2)}) collective-permute-start(f32[48,144]{1,0:T(8,128)S(1)} %add.21.refs_0_), channel_id=1, source_target_pairs={{0,8},{1,9},{2,10},{3,11},{4,12},{5,13},{6,14},{7,15},{8,0},{9,1},... | collective-permute-start | bytes 82952 | tf_op jit(solution)/shard_map/ppermute | solution.py:575

commit v5 on v4

--- a/solution.py
+++ b/solution.py
@@ -74,12 +74,13 @@
     return jnp.where(lane >= width + by, 0.0, pltpu.roll(values, width + by, 1))
 
 
-def store_shifts(ref, block, values):
+def store_shifts(ref, block, values, top=0, stride=None):
     rows, width = values.shape
+    stride = stride or rows
     lanes = slice(block * width, (block + 1) * width)
-    ref[0:rows, lanes] = lane_shift(values, 1).astype(BF16)
-    ref[rows : 2 * rows, lanes] = values.astype(BF16)
-    ref[2 * rows : 3 * rows, lanes] = lane_shift(values, -1).astype(BF16)
+    parts = (lane_shift(values, 1), values, lane_shift(values, -1))
+    for e, part in enumerate(parts):
+        ref[top + e * stride : top + e * stride + rows, lanes] = part.astype(BF16)
 
 
 def band_taps(dec_ref, conv_ref, back_ref):
@@ -101,11 +102,13 @@
     pick_out = one_hot(iota(shape, 0) == lane_index(square) // fine_ch)
     pick_in = one_hot(iota(shape, 0) == lane_index(square) % fine_ch)
     wide = group * SPAN
-    spread = one_hot(iota((block, wide), 0) == lane_index(wide) // SPAN)
+    spread = one_hot(iota((group, wide), 0) == lane_index(wide) // SPAN)
+    spread = jnp.concatenate([spread, jnp.zeros((block - group, wide), BF16)], 0)
     back_wide = 9 * rows
     column = lane_index(back_wide)
     channel, _ = place(column % rows, fine_ch)
-    spread_back = one_hot(iota((block, back_wide), 0) == column // rows * fine_ch + channel)
+    spread_back = one_hot(iota((group, back_wide), 0) == column // rows * fine_ch + channel)
+    spread_back = jnp.concatenate([spread_back, jnp.zeros((block - group, back_wide), BF16)], 0)
     chosen = dot(dec_ref[...].reshape(square, 27), chosen_taps)
     taps = []
     for n in range(6):
@@ -115,33 +118,40 @@
     forward = dot(jnp.concatenate(taps[:3], 0), spread)
     backward = dot(jnp.concatenate(taps[3:], 0), spread_back)
 
-    def banded(parts, offset):
-        total = jnp.zeros(offset.shape, F32)
-        for b in range(3):
-            total = jnp.where(offset == b, parts[b], total)
-        return total
+    def banded(parts, masks):
+        blocks = []
+        for first in range(0, parts[0].shape[1], 128):
+            total = jnp.zeros(masks[0].shape, F32)
+            for part, mask in zip(parts, masks):
+                part = jnp.broadcast_to(part[:, first : first + 128], mask.shape)
+                total = jnp.where(mask, part, total)
+            blocks.append(total)
+        return jnp.concatenate(blocks, 1)
 
     def rows_of(field, channel):
-        shape = (RATIO, field.shape[1])
         return [
-            jnp.broadcast_to(field[b * fine_ch + channel : b * fine_ch + channel + 1], shape)
-            for b in range(3)
+            field[b * fine_ch + channel : b * fine_ch + channel + 1] for b in range(3)
         ]
 
     slot = iota((RATIO, 128), 1) % SPAN
-    offset = jnp.concatenate([10 - slot - iota((RATIO, 128), 0)] * (wide // 128), 1)
-    pieces = [banded(rows_of(forward, o), offset) for o in range(fine_ch)]
-    slot = jnp.concatenate([iota((fine_ch, 128), 1) % SPAN] * (wide // 128), 1)
+    masks = [10 - slot - iota((RATIO, 128), 0) == b for b in range(3)]
+    pieces = [banded(rows_of(forward, o), masks) for o in range(fine_ch)]
+    slot = iota((fine_ch, 128), 1) % SPAN
     parts = [forward[b * fine_ch : (b + 1) * fine_ch] for b in range(3)]
-    pieces += [banded(parts, 11 - slot), banded(parts, 2 - slot)]
+    pieces += [banded(parts, [base - slot == b for b in range(3)]) for base in (11, 2)]
     field = jnp.concatenate(pieces, 0).astype(BF16)
     for a in range(3):
         conv_ref[a] = field[:, a * (wide // 3) : (a + 1) * (wide // 3)]
     _, z_in = place(lane_index(back_wide) % rows, fine_ch)
     offset = z_in - iota((RATIO, back_wide), 0) + 1
-    back_ref[...] = jnp.concatenate(
-        [banded(rows_of(backward, c), offset) for c in range(fine_ch)], 0
-    ).astype(BF16)
+    masks = [offset == b for b in range(3)]
+    pieces = []
+    for c in range(fine_ch):
+        total = jnp.zeros(offset.shape, F32)
+        for part, mask in zip(rows_of(backward, c), masks):
+            total = jnp.where(mask, jnp.broadcast_to(part, offset.shape), total)
+        pieces.append(total)
+    back_ref[...] = jnp.concatenate(pieces, 0).astype(BF16)
 
 
 def table_kernel(
@@ -268,45 +278,45 @@
     repeated = dot(repeat, cells.astype(BF16))
     lane = iota((fine_width, two), 1) // chans
     phase = iota((fine_width, two), 0) % RATIO
-    plan = ((0, RATIO - 2, 2, 0), (1, 0, RATIO, 2), (2, 0, 2, RATIO + 2))
     low = iota((fine_ch, RATIO, fine_width), 1) < 2
-    for dx, first, count, base in plan:
-        rows = []
-        for dz in range(3):
-            n = 3 * dx + dz
-            cell = repeated[:, n * two : (n + 1) * two]
-            rows.append(
-                jnp.concatenate(
-                    [jnp.where(phase == 2 * q + lane, cell, 0.0) for q in range(RATIO // 2)], 1
-                )
-            )
+    columns = []
+    for n in range(9):
+        cell = repeated[:, n * two : (n + 1) * two]
+        columns.append(
+            jnp.concatenate(
+                [jnp.where(phase == 2 * q + lane, cell, 0.0) for q in range(RATIO // 2)], 1
+            ).astype(BF16)
+        )
+    plan = (
+        (0, 2, ((1, 2), (2, RATIO + 2))),
+        (2, RATIO - 4, ((1, 2),)),
+        (RATIO - 2, 2, ((0, 2 - RATIO), (1, 2))),
+    )
+    for first, count, needed in plan:
         field = dot_nt(
             wide_ref[first : first + count].reshape(count * main, RATIO * chans),
-            jnp.concatenate(rows, 0).astype(BF16),
+            jnp.concatenate([columns[3 * dx + dz] for dx, _ in needed for dz in range(3)], 0),
         )
         for n in range(count):
-            under, own, over = (
-                pltpu.roll(
-                    field[n * main : (n + 1) * main, m * fine_width : (m + 1) * fine_width].reshape(
-                        fine_ch, RATIO, fine_width
-                    ),
-                    2,
-                    1,
+            for m, (_, base) in enumerate(needed):
+                under, own, over = (
+                    pltpu.roll(
+                        field[
+                            n * main : (n + 1) * main,
+                            (3 * m + dz) * fine_width : (3 * m + dz + 1) * fine_width,
+                        ].reshape(fine_ch, RATIO, fine_width),
+                        2,
+                        1,
+                    )
+                    for dz in range(3)
                 )
-                for m in range(3)
-            )
-            plane = jnp.concatenate([jnp.where(low, over, own), jnp.where(low, own, under)], 1)
-            store_shifts(up_ref, base + n, plane.reshape(fine_ch * SPAN, fine_width))
-
-
-def decode_kernel(
-    place_ref, cot_ref, x_low_ref, x_high_ref, z_low_ref, z_high_ref, conv_ref, up_ref,
-    grad_ref, total_ref, *, planes_x, planes_z
-):
+                plane = jnp.concatenate([jnp.where(low, over, own), jnp.where(low, own, under)], 1)
+                store_shifts(up_ref, base + first + n, plane.reshape(fine_ch * SPAN, fine_width))
+
+
+def decode_kernel(cot_ref, conv_ref, up_ref, grad_ref, outer_ref, edge_ref, total_ref):
     fine_ch, planes, depth, width = cot_ref.shape
     main = fine_ch * depth
-    rows = conv_ref.shape[1]
-    wide = (planes + 2) * width
     own = planes * width
 
     def convolve(first, count):
@@ -317,38 +327,20 @@
 
     step = 2
     ahead = convolve(0, step)
-    own_z = place_ref[1]
-    valid = (own_z > 0, own_z < planes_z - 1)
-    own_x = place_ref[0]
-    shape = (main, main)
-    turn = iota(shape, 1) == row_index(main) % fine_ch * planes + row_index(main) // fine_ch
-    sides = [
-        dot(one_hot(turn & valid[side]), ref[...].astype(F32).reshape(main, width).astype(BF16))
-        for side, ref in enumerate((z_low_ref, z_high_ref))
-    ]
     for x in range(planes + 2):
         if x % step == 0:
             pre = ahead
             if x + step < planes + 2:
                 ahead = convolve(x + step, step)
+        here = pre[:, x % step * width : (x % step + 1) * width]
         if 0 < x <= planes:
-            inner = cot_ref[:, x - 1].astype(F32).reshape(main, width)
-            edge = [side[(x - 1) * fine_ch : x * fine_ch] for side in sides]
+            cot = cot_ref[:, x - 1].astype(F32).reshape(main, width)
+            grad = (cot * slope_of(here[:main])).astype(BF16)
+            store_shifts(grad_ref, x - 1, grad.astype(F32))
+            edge_ref[:, (x - 1) * width : x * width] = here[main:]
         else:
-            outer = x_low_ref if x == 0 else x_high_ref
-            inside = own_x > 0 if x == 0 else own_x < planes_x - 1
-            inner = jnp.where(inside, outer[:main].astype(F32), 0.0)
-            edge = []
-            for side in range(2):
-                first = main + side * (outer.shape[0] - main - fine_ch)
-                corner = outer[first : first + fine_ch].astype(F32)
-                edge.append(jnp.where(valid[side] & inside, corner, 0.0))
-        cot = jnp.concatenate([inner] + edge, 0)
-        grad = (cot * slope_of(pre[:, x % step * width : (x % step + 1) * width])).astype(BF16)
-        store_shifts(grad_ref, x, grad.astype(F32))
-    grads = jnp.concatenate(
-        [grad_ref[e * rows : e * rows + main, width : width + own] for e in (2, 1, 0)], 0
-    )
+            outer_ref[0 if x == 0 else 1] = here
+    grads = jnp.concatenate([grad_ref[e * main : (e + 1) * main] for e in (2, 1, 0)], 0)
     taps = fine_ch * SPAN
     sums = []
     for a in range(3):
@@ -367,13 +359,44 @@
     total_ref[...] = sum(dot_nt(fold, part) for part in split(jnp.concatenate(sums, 0)))
 
 
-def spread_kernel(cot_ref, grad_ref, back_ref, wide_ref, send_hbm, send_ref, cells_ref, sems):
+def spread_kernel(
+    place_ref, cot_ref, x_low_ref, x_high_ref, z_low_ref, z_high_ref, own_ref, outer_ref, edge_ref,
+    back_ref, wide_ref, send_hbm, grad_ref, send_ref, cells_ref, sems, *, planes_x, planes_z
+):
     fine_ch, planes, depth, width = cot_ref.shape
     main = fine_ch * depth
     own = planes * width
+    rows = outer_ref.shape[1]
     chans = wide_ref.shape[2] // RATIO
     owners, chunk, _ = send_hbm.shape
     span = chunk - RATIO
+    own_x = place_ref[0]
+    own_z = place_ref[1]
+    valid = (own_z > 0, own_z < planes_z - 1)
+    for e in range(3):
+        grad_ref[e * rows : e * rows + main, width : width + own] = own_ref[
+            e * main : (e + 1) * main
+        ]
+    for x, outer in ((0, x_low_ref), (planes + 1, x_high_ref)):
+        inside = own_x > 0 if x == 0 else own_x < planes_x - 1
+        cot = [jnp.where(inside, outer[:main].astype(F32), 0.0)]
+        for side in range(2):
+            first = main + side * (outer.shape[0] - main - fine_ch)
+            corner = outer[first : first + fine_ch].astype(F32)
+            cot.append(jnp.where(valid[side] & inside, corner, 0.0))
+        pre = outer_ref[0 if x == 0 else 1]
+        grad = (jnp.concatenate(cot, 0) * slope_of(pre)).astype(BF16)
+        store_shifts(grad_ref, x, grad.astype(F32))
+    shape = (main, main)
+    turn = iota(shape, 1) == row_index(main) % fine_ch * planes + row_index(main) // fine_ch
+    sides = [
+        dot(one_hot(turn & valid[side]), ref[...].astype(F32).reshape(main, width).astype(BF16))
+        for side, ref in enumerate((z_low_ref, z_high_ref))
+    ]
+    for x in range(planes):
+        cot = jnp.concatenate([side[x * fine_ch : (x + 1) * fine_ch] for side in sides], 0)
+        grad = (cot * slope_of(edge_ref[:, x * width : (x + 1) * width])).astype(BF16)
+        store_shifts(grad_ref, x + 1, grad.astype(F32), main, rows)
     taps = grad_ref.shape[0]
     back = sum(
         dot(back_ref[:, a * taps : (a + 1) * taps], grad_ref[:, a * width : a * width + own])
@@ -383,10 +406,12 @@
         [cot_ref[:, x].astype(F32).reshape(main, width) for x in range(planes)], 1
     )
     up = (cot + back).astype(BF16)
-    row = iota((main, main), 0)
-    column = iota((main, main), 1)
-    turn = one_hot((row % fine_ch == column // RATIO) & (row // fine_ch == column % RATIO))
-    turned = dot(turn, up).astype(BF16)
+    row = row_index(main)
+    order = jnp.concatenate(
+        [row % fine_ch * RATIO + row // fine_ch, row // RATIO * RATIO + RATIO - 1 - row % RATIO], 0
+    )
+    both = dot(one_hot(iota((2 * main, main), 1) == order), up).astype(BF16)
+    turned, flipped = both[:main], both[main:]
     for owner in range(owners):
         first = owner * RATIO * RATIO // owners
         x = first // RATIO
@@ -394,10 +419,6 @@
         send_ref[owner] = turned[top : top + span, x * width : (x + 1) * width]
     store = pltpu.make_async_copy(send_ref, send_hbm.at[:, :span], sems.at[0])
     store.start()
-    flip = one_hot(
-        (row // RATIO == column // RATIO) & (row % RATIO + column % RATIO == RATIO - 1)
-    )
-    flipped = dot(flip, up).astype(BF16)
     parts = dot_tn(
         jnp.concatenate([flipped[:, x * width : (x + 1) * width] for x in range(planes)], 0),
         wide_ref[...].reshape(planes * main, RATIO * chans),
@@ -655,23 +676,33 @@
         scalars=1,
         flops=2e9,
     )
-    dec_grad, dec_sum = call(
-        functools.partial(decode_kernel, planes_x=planes, planes_z=depth),
-        [((3 * rows, (RATIO + 2) * fine_width), BF16), ((3 * fine_ch, 9 * fine_ch), F32)],
-        (where, cotangent, x_low, x_high, faces[0], faces[-1], conv, upsampled),
-        scalars=1,
+    own = own_fine * fine_width
+    dec_grad, outer_pre, edge_pre, dec_sum = call(
+        decode_kernel,
+        [
+            ((3 * main, own), BF16),
+            ((2, rows, fine_width), F32),
+            ((rows - main, own), F32),
+            ((3 * fine_ch, 9 * fine_ch), F32),
+        ],
+        (cotangent, conv, upsampled),
         flops=2e9,
     )
     chunk = max(1, RATIO * RATIO // owners) * fine_ch + RATIO
     (send,) = call(
-        spread_kernel,
+        functools.partial(spread_kernel, planes_x=planes, planes_z=depth),
         [((owners, chunk, fine_width), BF16)],
-        (cotangent, dec_grad, back, wide_table),
+        (
+            where, cotangent, x_low, x_high, faces[0], faces[-1], dec_grad, outer_pre, edge_pre,
+            back, wide_table,
+        ),
         scratch=[
+            VMEM((3 * rows, own + 2 * fine_width), BF16),
             VMEM((owners, chunk - RATIO, fine_width), BF16),
             VMEM((owners, RATIO, fine_width), BF16),
             pltpu.SemaphoreType.DMA((2,)),
         ],
+        scalars=1,
         flops=2e9,
         hbm_out=(0,),
     )
@@ -682,9 +713,10 @@
     steps = sorted(steps)
     one_by_one = steps[: max(1, len(steps) - LAST_STEPS)]
     for step in one_by_one:
-        dec_sum = dec_sum + swapped(dec_sum, step)
+        other = swapped(dec_sum, step)
         if step == steps[0]:
-            send, dec_sum = lax.optimization_barrier((send, dec_sum))
+            send, other, dec_sum = lax.optimization_barrier((send, other, dec_sum))
+        dec_sum = dec_sum + other
     sums = [0]
     for step in steps[len(one_by_one) :]:
         sums += [step + other for other in sums]

time: 42.6 us -> 41.8 us (0.981)
  transfers between devices with their start and end apart: 11 -> 11, of which waited for: 5 -> 5; matrix products, arithmetic and copies ran while one was open for 0% -> 0% of each run, Pallas kernels for 27% -> 34%
where the time goes in v5:
time: 41.8 us; the launch traced here: 41.6 us
  starting transfers between devices  16.8 us (40%)
  Pallas kernels  15 us (36%)
  waiting for transfers between devices  7.65 us (18%)
  local copies, waits for them, and re-layouts  1.14 us (3%)
  between operations  0.85 us (2%)
    pallas_call x7, Pallas kernels, call(): pl.pallas_call(kernel, out_shape=[jax.ShapeDtypeStruct(*s) for s in out_s...  15 us
    ppermute x6, waiting for transfers between devices, swapped(): return lax.ppermute(value, AXES, [(i, i ^ step) for i in range(count)])  7.61 us
    ppermute x6, starting transfers between devices, swapped(): return lax.ppermute(value, AXES, [(i, i ^ step) for i in range(count)])  6.75 us
    all_to_all x1, starting transfers between devices, on_device(): got = lax.all_to_all(send, AXES, 0, 0, tiled=True)  4.9 us
    ppermute x1, starting transfers between devices, exchange_depth(): lax.ppermute(lax.dynamic_index_in_dim(cotangent, z, 2, False), 'narrow',...  3 us
    ppermute x2, starting transfers between devices, exchange_width(): got.append(lax.ppermute(send, AXES, list(partner.items())))  2.07 us
    dynamic_slice x1, local copies, waits for them, and re-layouts, exchange_depth(): lax.dynamic_index_in_dim(cotangent, z, 2, False)  1.08 us
  transfers between devices with their start and end apart: 11, of which 5 were waited for; matrix products, arithmetic and copies ran while one was open for 0% of the time, Pallas kernels for 34%

profile of v5, /device:TPU:0, one launch (start us, length us, event | category | flops | bytes accessed | tf_op | source)
XLA Modules:
  0.0 41.6 jit_solution(14984361682282473814)
XLA Ops:
  0.6 0.0 copy-start.3
  0.6 0.0 copy-start.1
  0.7 0.0 copy-start.2
  0.7 1.1 %constant_dynamic-slice_fusion.2 = bf16[16,8,1,128]{3,2,1,0:T(2,128)(2,1)S(1)} fusion(bf16[16,8,8,128]{3,2,1,0:T(8,128)(2,1)} %cot_ref.3, s32[]{:T(128)S(6)} %select_n.36), kind=kLoop, calls=%fused_computation.9 | loop fusion | bytes 65540 | tf_op jit(solution)/shard_map/jit(dynamic_index_in_dim)/dynamic_slice | solution.py:606
  1.8 3.0 %collective-permute-start = (bf16[16,8,128]{2,1,0:T(8,128)(2,1)S(1)}, bf16[16,8,128]{2,1,0:T(8,128)(2,1)S(1)}, u32[]{:S(2)}, u32[]{:S(2)}) collective-permute-start(bf16[16,8,128]{2,1,0:T(8,128)(2,1)S(1)} %bitcast.30), channel_id=1, source_target_pairs={{0,1},{1,0},{2,3},{3,2},{4,5},{5,4},{6,7},{7,6},{8,9},{9,8},{10,11... | collective-permute-start | bytes 98312 | tf_op jit(solution)/shard_map/ppermute | solution.py:606
  4.8 0.1 collective-permute-start.3
  4.9 0.1 pad_add_fusion.place_ref
  4.9 2.8 %shard_map.84 = (bf16[8,128,512]{2,1,0:T(8,128)(2,1)S(1)}, bf16[16,8,128]{2,1,0:T(8,128)(2,1)S(1)}, bf16[16,8,128]{2,1,0:T(8,128)(2,1)S(1)}) custom-call(s32[2]{0:T(128)S(1)} %pad_add_fusion.place_ref, bf16[16,64,512]{2,1,0:T(8,128)(2,1)} %bitcast.33, bf16[16,8,8,128]{3,2,1,0:T(8,128)(2,1)} %cot_ref.3), custom_call_target="tpu_custom_call" | custom-call | flops 1000000000 | bytes 2000000 | tf_op jit(solution)/shard_map/pallas_call | solution.py:572
  7.7 0.0 collective-permute-done.z_low_ref.z_high_ref
  7.8 0.1 collective-permute-start.2
  7.9 2.0 %collective-permute-start.1 = (bf16[144,128]{1,0:T(8,128)(2,1)S(1)}, bf16[144,128]{1,0:T(8,128)(2,1)S(1)}, u32[]{:S(2)}, u32[]{:S(2)}) collective-permute-start(bf16[144,128]{1,0:T(8,128)(2,1)S(1)} %pad_maximum_fusion), channel_id=1, source_target_pairs={{0,1},{1,0},{2,4},{3,5},{4,2},{5,3},{6,8},{7,9},{8,6},{9,7},{10,12... | collective-permute-start | bytes 110600 | tf_op jit(solution)/shard_map/ppermute | solution.py:631
  9.9 0.0 collective-permute-done.3.refs_1_
  9.9 0.0 copy-done.3
  9.9 0.0 copy-done.1
  9.9 0.0 copy-done.2
  9.9 0.0 copy-start
  9.9 3.3 %shard_map.85 = (bf16[3,160,768]{2,1,0:T(8,128)(2,1)S(1)}, bf16[128,1440]{1,0:T(8,128)(2,1)S(1)}, f32[256,128]{1,0:T(8,128)S(1)}, bf16[256,128]{1,0:T(8,128)(2,1...) custom-call(s32[2]{0:T(128)S(1)} %pad_add_fusion.place_ref, bf16[16,16,27]{2,1,0:T(8,128)(2,1)S(1)} %bitcast.26, ...), custom_call_target="tpu_custom_call" | custom-call | flops 2000000000 | bytes 2000000 | tf_op jit(solution)/shard_map/pallas_call | solution.py:572
  13.2 0.0 copy-done
  13.2 2.3 %shard_map.86 = (bf16[384,1024]{1,0:T(8,128)(2,1)S(1)}, f32[2,160,128]{2,1,0:T(8,128)S(1)}, f32[32,1024]{1,0:T(8,128)S(1)}, f32[48,144]{1,0:T(8,128)S(1)}) custom-call(bf16[16,8,8,128]{3,2,1,0:T(8,128)(2,1)S(1)} %copy-done, bf16[3,160,768]{2,1,0:T(8,128)(2,1)S(1)} %get-tuple-element.31.conv_ref, bf16[768,1536]{1,0:T(8,128)(2,1)S(1)} %get-tuple-element.32.up_ref), custom_call_target="tpu_custom_call" | custom-call | flops 2000000000 | bytes 2000000 | tf_op jit(solution)/shard_map/pallas_call | solution.py:572
  15.5 0.2 collective-permute-start.4
  15.7 0.0 collective-permute-done.2
  15.7 0.0 collective-permute-done.1
  15.7 2.5 %shard_map.87 = bf16[32,40,128]{2,1,0:T(8,128)(2,1)} custom-call(s32[2]{0:T(128)S(1)} %pad_add_fusion.place_ref, bf16[16,8,8,128]{3,2,1,0:T(8,128)(2,1)S(1)} %copy-done, bf16[144,128]{1,0:T(8,128)(2,1)S(1)} %get-tuple-element.61.x_low_ref, bf16[144,128]{1,0:T(8,128)(2,1)S(1)} %get-tuple-element.60.x_high_ref, ...), custom_call_target="tpu_custom_call" | custom-call | flops 2000000000 | bytes 2000000 | tf_op jit(solution)/shard_map/pallas_call | solution.py:572
  18.2 1.5 %collective-permute-done.4 = f32[48,144]{1,0:T(8,128)S(1)} collective-permute-done((f32[48,144]{1,0:T(8,128)S(1)}, f32[48,144]{1,0:T(8,128)S(1)}, u32[]{:S(2)}, u32[]{:S(2)}) %collective-permute-start.4) | collective-permute-done | bytes 27680 | tf_op jit(solution)/shard_map/ppermute | solution.py:596
  19.7 4.9 %all-to-all-start = ((bf16[32,40,128]{2,1,0:T(8,128)(2,1)}), bf16[32,40,128]{2,1,0:T(8,128)(2,1)S(1)}, u32[]{:S(2)}, u32[]{:S(2)}) async-start(bf16[32,40,128]{2,1,0:T(8,128)(2,1)} %shard_map.87), calls=%async_computation | async-start | bytes 655360 | tf_op jit(solution)/shard_map/all_to_all | solution.py:724
  24.6 0.3 collective-permute-start.5
  24.9 1.0 %collective-permute-done.5 = f32[48,144]{1,0:T(8,128)S(1)} collective-permute-done((f32[48,144]{1,0:T(8,128)S(1)}, f32[48,144]{1,0:T(8,128)S(1)}, u32[]{:S(2)}, u32[]{:S(2)}) %collective-permute-start.5) | collective-permute-done | bytes 27680 | tf_op jit(solution)/shard_map/ppermute | solution.py:596
  25.9 1.8 %collective-permute-start.6 = (f32[48,144]{1,0:T(8,128)S(1)}, f32[48,144]{1,0:T(8,128)S(1)}, u32[]{:S(2)}, u32[]{:S(2)}) collective-permute-start(f32[48,144]{1,0:T(8,128)S(1)} %add.20), channel_id=1, source_target_pairs={{0,4},{1,5},{2,6},{3,7},{4,0},{5,1},{6,2},{7,3},{8,12},{9,13},{10,... | collective-permute-start | bytes 82952 | tf_op jit(solution)/shard_map/ppermute | solution.py:596
  27.8 0.9 %shard_map.88 = (bf16[2048,128]{1,0:T(8,128)(2,1)S(1)}, f32[256,128]{1,0:T(8,128)S(1)}, bf16[3,384,64]{2,1,0:T(8,128)(2,1)S(1)}, bf16[3,144,512]{2,1,0:T(8,128)(2,1)S(1)}) custom-call(s32[2]{0:T(128)S(1)} %pad_add_fusion.place_ref, bf16[256,128]{1,0:T(8,128)(2,1)S(1)} %get-tuple-element.39.encoded_ref, f32[256,128]{1,0:T(8,128)S(1)} %get-tuple-element.40.pre_ref, ...), custom_call_target="tpu_custom_call" | custom-call | flops 1000000000 | bytes 2000000 | tf_op jit(solution)/shard_map/pallas_call | solution.py:572
  28.7 3.1 %collective-permute-done.6 = f32[48,144]{1,0:T(8,128)S(1)} collective-permute-done((f32[48,144]{1,0:T(8,128)S(1)}, f32[48,144]{1,0:T(8,128)S(1)}, u32[]{:S(2)}, u32[]{:S(2)}) %collective-permute-start.6) | collective-permute-done | bytes 27680 | tf_op jit(solution)/shard_map/ppermute | solution.py:596
  31.9 3.6 %collective-permute-start.9 = (f32[48,144]{1,0:T(8,128)S(1)}, f32[48,144]{1,0:T(8,128)S(1)}, u32[]{:S(2)}, u32[]{:S(2)}) collective-permute-start(f32[48,144]{1,0:T(8,128)S(1)} %add.21.refs_0_), channel_id=1, source_target_pairs={{0,24},{1,25},{2,26},{3,27},{4,28},{5,29},{6,30},{7,31},{8,16},{9,... | collective-permute-start | bytes 82952 | tf_op jit(solution)/shard_map/ppermute | solution.py:596
  35.5 0.0 collective-permute-start.8
  35.5 0.8 %collective-permute-start.7 = (f32[48,144]{1,0:T(8,128)S(1)}, f32[48,144]{1,0:T(8,128)S(1)}, u32[]{:S(2)}, u32[]{:S(2)}) collective-permute-start(f32[48,144]{1,0:T(8,128)S(1)} %add.21.refs_0_), channel_id=1, source_target_pairs={{0,8},{1,9},{2,10},{3,11},{4,12},{5,13},{6,14},{7,15},{8,0},{9,1},... | collective-permute-start | bytes 82952 | tf_op jit(solution)/shard_map/ppermute | solution.py:596
  36.3 0.0 all-to-all-done.got_ref
  36.3 2.2 %shard_map.89 = (f32[16,16,64]{2,1,0:T(8,128)}, f32[27,64,64]{2,1,0:T(8,128)}, f32[16,16,64]{2,1,0:T(8,128)}, f32[8,128]{1,0:T(8,128)S(1)}) custom-call(bf16[32,40,128]{2,1,0:T(8,128)(2,1)S(1)} %all-to-all-done.got_ref, bf16[2048,128]{1,0:T(8,128)(2,1)S(1)} %get-tuple-element.41.spread_ref, f32[256,128]{1,0:T(8,128)S(1)} %get-tuple-element.42.slope_ref, ...), custom_call_target="tpu_custom_call" | custom-call | flops 2000000000 | bytes 2000000 | tf_op jit(solution)/shard_map/pallas_call | solution.py:572
  38.6 0.0 collective-permute-done.9.refs_3_
  38.6 1.9 %collective-permute-done.8.refs_2_ = f32[48,144]{1,0:T(8,128)S(1)} collective-permute-done((f32[48,144]{1,0:T(8,128)S(1)}, f32[48,144]{1,0:T(8,128)S(1)}, u32[]{:S(2)}, u32[]{:S(2)}) %collective-permute-start.8) | collective-permute-done | bytes 27680 | tf_op jit(solution)/shard_map/ppermute | solution.py:596
  40.5 0.1 collective-permute-done.7.refs_1_
  40.6 0.9 %shard_map.90 = f32[16,16,27]{2,1,0:T(8,128)} custom-call(bf16[3,144,512]{2,1,0:T(8,128)(2,1)S(1)} %get-tuple-element.48.order_ref, f32[8,128]{1,0:T(8,128)S(1)} %get-tuple-element.49.done_ref, f32[48,144]{1,0:T(8,128)S(1)} %add.21.refs_0_, f32[48,144]{1,0:T(8,128)S(1)} %collective-permute-done.7.refs_1_, f32[48,144]{1,0:T(8,128)S(1)} %collective-permute-done.8.refs_2_, ...), custom_call_target="tpu_custom_call" | custom-call | flops 100000000 | bytes 2000000 | tf_op jit(solution)/shard_map/pallas_call | solution.py:572
  (10 shorter events, 0.1 us)
Async XLA Ops:
  0.6 9.3 %copy-start.3 = (bf16[64,16,1,16]{0,3,2,1:T(8,128)(2,1)S(1)}, bf16[64,16,1,16]{0,3,2,1:T(8,128)(2,1)}, u32[]{:S(2)}) copy-start(bf16[64,16,1,16]{0,3,2,1:T(8,128)(2,1)} %param.5) | copy-start | bytes 98308
  0.6 9.3 %copy-start.1 = (bf16[27,64,64]{2,1,0:T(8,128)(2,1)S(1)}, bf16[27,64,64]{2,1,0:T(8,128)(2,1)}, u32[]{:S(2)}) copy-start(bf16[27,64,64]{2,1,0:T(8,128)(2,1)} %enc_ref.3) | copy-start | bytes 663556
  0.7 9.3 %copy-start.2 = (bf16[27,16,16]{0,2,1:T(8,128)(2,1)S(1)}, bf16[27,16,16]{0,2,1:T(8,128)(2,1)}, u32[]{:S(2)}) copy-start(bf16[27,16,16]{0,2,1:T(8,128)(2,1)} %param.8) | copy-start | bytes 41476
  1.8 6.0 %collective-permute-start = (bf16[16,8,128]{2,1,0:T(8,128)(2,1)S(1)}, bf16[16,8,128]{2,1,0:T(8,128)(2,1)S(1)}, u32[]{:S(2)}, u32[]{:S(2)}) collective-permute-start(bf16[16,8,128]{2,1,0:T(8,128)(2,1)S(1)} %bitcast.30), channel_id=1, source_target_pairs={{0,1},{1,0},{2,3},{3,2},{4,5},{5,4},{6,7},{7,6},{8,9},{9,8},{10,11... | collective-permute-start | bytes 98312 | tf_op jit(solution)/shard_map/ppermute | solution.py:606
  4.8 5.1 %collective-permute-start.3 = (bf16[16,16,64]{2,1,0:T(8,128)(2,1)}, bf16[16,16,64]{2,1,0:T(8,128)(2,1)S(1)}, u32[]{:S(2)}, u32[]{:S(2)}) collective-permute-start(bf16[16,16,64]{2,1,0:T(8,128)(2,1)} %bitcast.27), channel_id=1, source_target_pairs={{0,1},{1,0},{2,3},{3,2},{4,5},{5,4},{6,7},{7,6},{8,9},{9,8},{10,11... | collective-permute-start | bytes 98312 | tf_op jit(solution)/shard_map/ppermute | solution.py:604
  7.8 7.9 %collective-permute-start.2 = (bf16[144,128]{1,0:T(8,128)(2,1)S(1)}, bf16[144,128]{1,0:T(8,128)(2,1)S(1)}, u32[]{:S(2)}, u32[]{:S(2)}) collective-permute-start(bf16[144,128]{1,0:T(8,128)(2,1)S(1)} %pad_maximum_fusion.1), channel_id=1, source_target_pairs={{0,2},{1,3},{2,0},{3,1},{4,6},{5,7},{6,4},{7,5},{8,10},{9,11},{10,... | collective-permute-start | bytes 110600 | tf_op jit(solution)/shard_map/ppermute | solution.py:631
  7.9 7.8 %collective-permute-start.1 = (bf16[144,128]{1,0:T(8,128)(2,1)S(1)}, bf16[144,128]{1,0:T(8,128)(2,1)S(1)}, u32[]{:S(2)}, u32[]{:S(2)}) collective-permute-start(bf16[144,128]{1,0:T(8,128)(2,1)S(1)} %pad_maximum_fusion), channel_id=1, source_target_pairs={{0,1},{1,0},{2,4},{3,5},{4,2},{5,3},{6,8},{7,9},{8,6},{9,7},{10,12... | collective-permute-start | bytes 110600 | tf_op jit(solution)/shard_map/ppermute | solution.py:631
  9.9 3.3 %copy-start = (bf16[16,8,8,128]{3,2,1,0:T(8,128)(2,1)S(1)}, bf16[16,8,8,128]{3,2,1,0:T(8,128)(2,1)}, u32[]{:S(2)}) copy-start(bf16[16,8,8,128]{3,2,1,0:T(8,128)(2,1)} %cot_ref.3) | copy-start | bytes 786436
  15.5 4.2 %collective-permute-start.4 = (f32[48,144]{1,0:T(8,128)S(1)}, f32[48,144]{1,0:T(8,128)S(1)}, u32[]{:S(2)}, u32[]{:S(2)}) collective-permute-start(f32[48,144]{1,0:T(8,128)S(1)} %get-tuple-element.50), channel_id=1, source_target_pairs={{0,1},{1,0},{2,3},{3,2},{4,5},{5,4},{6,7},{7,6},{8,9},{9,8},{10,11... | collective-permute-start | bytes 82952 | tf_op jit(solution)/shard_map/ppermute | solution.py:596
  19.7 16.6 %all-to-all-start = ((bf16[32,40,128]{2,1,0:T(8,128)(2,1)}), bf16[32,40,128]{2,1,0:T(8,128)(2,1)S(1)}, u32[]{:S(2)}, u32[]{:S(2)}) async-start(bf16[32,40,128]{2,1,0:T(8,128)(2,1)} %shard_map.87), calls=%async_computation | async-start | bytes 655360 | tf_op jit(solution)/shard_map/all_to_all | solution.py:724
  24.6 1.3 %collective-permute-start.5 = (f32[48,144]{1,0:T(8,128)S(1)}, f32[48,144]{1,0:T(8,128)S(1)}, u32[]{:S(2)}, u32[]{:S(2)}) collective-permute-start(f32[48,144]{1,0:T(8,128)S(1)} %add.19), channel_id=1, source_target_pairs={{0,2},{1,3},{2,0},{3,1},{4,6},{5,7},{6,4},{7,5},{8,10},{9,11},{10,... | collective-permute-start | bytes 82952 | tf_op jit(solution)/shard_map/ppermute | solution.py:596
  25.9 5.9 %collective-permute-start.6 = (f32[48,144]{1,0:T(8,128)S(1)}, f32[48,144]{1,0:T(8,128)S(1)}, u32[]{:S(2)}, u32[]{:S(2)}) collective-permute-start(f32[48,144]{1,0:T(8,128)S(1)} %add.20), channel_id=1, source_target_pairs={{0,4},{1,5},{2,6},{3,7},{4,0},{5,1},{6,2},{7,3},{8,12},{9,13},{10,... | collective-permute-start | bytes 82952 | tf_op jit(solution)/shard_map/ppermute | solution.py:596
  31.9 6.7 %collective-permute-start.9 = (f32[48,144]{1,0:T(8,128)S(1)}, f32[48,144]{1,0:T(8,128)S(1)}, u32[]{:S(2)}, u32[]{:S(2)}) collective-permute-start(f32[48,144]{1,0:T(8,128)S(1)} %add.21.refs_0_), channel_id=1, source_target_pairs={{0,24},{1,25},{2,26},{3,27},{4,28},{5,29},{6,30},{7,31},{8,16},{9,... | collective-permute-start | bytes 82952 | tf_op jit(solution)/shard_map/ppermute | solution.py:596
  35.5 5.0 %collective-permute-start.8 = (f32[48,144]{1,0:T(8,128)S(1)}, f32[48,144]{1,0:T(8,128)S(1)}, u32[]{:S(2)}, u32[]{:S(2)}) collective-permute-start(f32[48,144]{1,0:T(8,128)S(1)} %add.21.refs_0_), channel_id=1, source_target_pairs={{0,16},{1,17},{2,18},{3,19},{4,20},{5,21},{6,22},{7,23},{8,24},{9,... | collective-permute-start | bytes 82952 | tf_op jit(solution)/shard_map/ppermute | solution.py:596
  35.5 5.1 %collective-permute-start.7 = (f32[48,144]{1,0:T(8,128)S(1)}, f32[48,144]{1,0:T(8,128)S(1)}, u32[]{:S(2)}, u32[]{:S(2)}) collective-permute-start(f32[48,144]{1,0:T(8,128)S(1)} %add.21.refs_0_), channel_id=1, source_target_pairs={{0,8},{1,9},{2,10},{3,11},{4,12},{5,13},{6,14},{7,15},{8,0},{9,1},... | collective-permute-start | bytes 82952 | tf_op jit(solution)/shard_map/ppermute | solution.py:596

commit v6 on v5

--- a/solution.py
+++ b/solution.py
@@ -356,7 +356,10 @@
         iota(shape, 1)
         == row_index(shape[0]) % fine_ch * SPAN + 10 - row_index(shape[0]) // fine_ch
     )
-    total_ref[...] = sum(dot_nt(fold, part) for part in split(jnp.concatenate(sums, 0)))
+    total = sum(dot_nt(fold, part) for part in split(jnp.concatenate(sums, 0)))
+    total_ref[...] = jnp.concatenate(
+        [total[b * fine_ch : (b + 1) * fine_ch] for b in range(3)], 1
+    )
 
 
 def spread_kernel(
@@ -466,25 +469,20 @@
                 taps_ref[a, first : first + chans] = jnp.where(
                     (b >= 0) & (b <= 2), tap.astype(F32), 0.0
                 ).astype(BF16)
-    shape = order_ref.shape[1:]
-    fine_ch = shape[0] // 9
+    shape = order_ref.shape
+    fine_ch = shape[0] // 27
     step = shape[1] // fine_ch
     row = row_index(shape[0])
-    column = iota(shape, 1)
-    tap = row // fine_ch // 3 * 9 + row // fine_ch % 3
-    for b in range(3):
-        order_ref[b] = one_hot(column == row % fine_ch * step + tap + 3 * b)
+    tap = row // fine_ch
+    tap = tap // 9 * 3 + tap // 3 % 3 * 9 + tap % 3
+    order_ref[...] = one_hot(iota(shape, 1) == row % fine_ch * step + tap)
 
 
 def final_kernel(order_ref, done_ref, *refs, scale):
     *parts, out_ref = refs
     total = sum(part[...] for part in parts) * scale
     fine_ch = out_ref.shape[0]
-    parts = split(total)
-    field = 0.0
-    for b in range(3):
-        rows = slice(b * fine_ch, (b + 1) * fine_ch)
-        field = field + dot(jnp.concatenate([part[rows] for part in parts], 0), order_ref[b])
+    field = dot(jnp.concatenate(split(total), 0), order_ref[...])
     field = field[:fine_ch] + field[fine_ch : 2 * fine_ch] + field[2 * fine_ch :]
     step = field.shape[1] // fine_ch
     for o in range(fine_ch):
@@ -683,7 +681,7 @@
             ((3 * main, own), BF16),
             ((2, rows, fine_width), F32),
             ((rows - main, own), F32),
-            ((3 * fine_ch, 9 * fine_ch), F32),
+            ((fine_ch, 27 * fine_ch), F32),
         ],
         (cotangent, conv, upsampled),
         flops=2e9,
@@ -728,7 +726,7 @@
             ((cells * RATIO, lanes), BF16),
             ((cells, lanes), F32),
             ((3, 3 * lanes, chans), BF16),
-            ((3, 9 * fine_ch, 32 * fine_ch), BF16),
+            ((27 * fine_ch, 32 * fine_ch), BF16),
         ],
         (where, encoded, enc_pre, w_enc),
         scalars=1,

time: 41.8 us -> 40.7 us (0.974)
  waiting for transfers between devices: 7.65 us -> 6.34 us
    ppermute x6, waiting for transfers between devices: 7.61 us -> 5.27 us  [swapped(): return lax.ppermute(value, AXES, [(i, i ^ step) for i in range(count)])]
    all_to_all x1, waiting for transfers between devices: 0.02 us -> 1.06 us  [on_device(): got = lax.all_to_all(send, AXES, 0, 0, tiled=True)]
  transfers between devices with their start and end apart: 11 -> 11, of which waited for: 5 -> 5; matrix products, arithmetic and copies ran while one was open for 0% -> 0% of each run, Pallas kernels for 34% -> 35%
where the time goes in v6:
time: 40.7 us; the launch traced here: 40.5 us
  starting transfers between devices  16.8 us (41%)
  Pallas kernels  15.3 us (38%)
  waiting for transfers between devices  6.34 us (16%)
  local copies, waits for them, and re-layouts  1.14 us (3%)
  between operations  0.83 us (2%)
    pallas_call x7, Pallas kernels, call(): pl.pallas_call(kernel, out_shape=[jax.ShapeDtypeStruct(*s) for s in out_s...  15.3 us
    ppermute x6, starting transfers between devices, swapped(): return lax.ppermute(value, AXES, [(i, i ^ step) for i in range(count)])  6.73 us
    ppermute x6, waiting for transfers between devices, swapped(): return lax.ppermute(value, AXES, [(i, i ^ step) for i in range(count)])  5.27 us
    all_to_all x1, starting transfers between devices, on_device(): got = lax.all_to_all(send, AXES, 0, 0, tiled=True)  4.9 us
    ppermute x1, starting transfers between devices, exchange_depth(): lax.ppermute(lax.dynamic_index_in_dim(cotangent, z, 2, False), 'narrow',...  3 us
    ppermute x2, starting transfers between devices, exchange_width(): got.append(lax.ppermute(send, AXES, list(partner.items())))  2.07 us
    dynamic_slice x1, local copies, waits for them, and re-layouts, exchange_depth(): lax.dynamic_index_in_dim(cotangent, z, 2, False)  1.08 us
    all_to_all x1, waiting for transfers between devices, on_device(): got = lax.all_to_all(send, AXES, 0, 0, tiled=True)  1.06 us
  transfers between devices with their start and end apart: 11, of which 5 were waited for; matrix products, arithmetic and copies ran while one was open for 0% of the time, Pallas kernels for 35%

profile of v6, /device:TPU:0, one launch (start us, length us, event | category | flops | bytes accessed | tf_op | source)
XLA Modules:
  0.0 40.5 jit_solution(561863524552269892)
XLA Ops:
  0.6 0.0 copy-start.3
  0.6 0.0 copy-start.1
  0.7 0.0 copy-start.2
  0.7 1.1 %constant_dynamic-slice_fusion.2 = bf16[16,8,1,128]{3,2,1,0:T(2,128)(2,1)S(1)} fusion(bf16[16,8,8,128]{3,2,1,0:T(8,128)(2,1)} %cot_ref.3, s32[]{:T(128)S(6)} %select_n.36), kind=kLoop, calls=%fused_computation.9 | loop fusion | bytes 65540 | tf_op jit(solution)/shard_map/jit(dynamic_index_in_dim)/dynamic_slice | solution.py:604
  1.8 3.0 %collective-permute-start = (bf16[16,8,128]{2,1,0:T(8,128)(2,1)S(1)}, bf16[16,8,128]{2,1,0:T(8,128)(2,1)S(1)}, u32[]{:S(2)}, u32[]{:S(2)}) collective-permute-start(bf16[16,8,128]{2,1,0:T(8,128)(2,1)S(1)} %bitcast.30), channel_id=1, source_target_pairs={{0,1},{1,0},{2,3},{3,2},{4,5},{5,4},{6,7},{7,6},{8,9},{9,8},{10,11... | collective-permute-start | bytes 98312 | tf_op jit(solution)/shard_map/ppermute | solution.py:604
  4.8 0.1 collective-permute-start.3
  4.9 0.1 pad_add_fusion.place_ref
  4.9 2.8 %shard_map.84 = (bf16[8,128,512]{2,1,0:T(8,128)(2,1)S(1)}, bf16[16,8,128]{2,1,0:T(8,128)(2,1)S(1)}, bf16[16,8,128]{2,1,0:T(8,128)(2,1)S(1)}) custom-call(s32[2]{0:T(128)S(1)} %pad_add_fusion.place_ref, bf16[16,64,512]{2,1,0:T(8,128)(2,1)} %bitcast.33, bf16[16,8,8,128]{3,2,1,0:T(8,128)(2,1)} %cot_ref.3), custom_call_target="tpu_custom_call" | custom-call | flops 1000000000 | bytes 2000000 | tf_op jit(solution)/shard_map/pallas_call | solution.py:570
  7.7 0.0 collective-permute-done.z_low_ref.z_high_ref
  7.8 0.1 collective-permute-start.2
  7.9 2.0 %collective-permute-start.1 = (bf16[144,128]{1,0:T(8,128)(2,1)S(1)}, bf16[144,128]{1,0:T(8,128)(2,1)S(1)}, u32[]{:S(2)}, u32[]{:S(2)}) collective-permute-start(bf16[144,128]{1,0:T(8,128)(2,1)S(1)} %pad_maximum_fusion), channel_id=1, source_target_pairs={{0,1},{1,0},{2,4},{3,5},{4,2},{5,3},{6,8},{7,9},{8,6},{9,7},{10,12... | collective-permute-start | bytes 110600 | tf_op jit(solution)/shard_map/ppermute | solution.py:629
  9.9 0.0 collective-permute-done.3.refs_1_
  9.9 0.0 copy-done.3
  9.9 0.0 copy-done.1
  9.9 0.0 copy-done.2
  9.9 0.0 copy-start
  9.9 3.3 %shard_map.85 = (bf16[3,160,768]{2,1,0:T(8,128)(2,1)S(1)}, bf16[128,1440]{1,0:T(8,128)(2,1)S(1)}, f32[256,128]{1,0:T(8,128)S(1)}, bf16[256,128]{1,0:T(8,128)(2,1...) custom-call(s32[2]{0:T(128)S(1)} %pad_add_fusion.place_ref, bf16[16,16,27]{2,1,0:T(8,128)(2,1)S(1)} %bitcast.26, ...), custom_call_target="tpu_custom_call" | custom-call | flops 2000000000 | bytes 2000000 | tf_op jit(solution)/shard_map/pallas_call | solution.py:570
  13.2 0.0 copy-done
  13.2 2.4 %shard_map.86 = (bf16[384,1024]{1,0:T(8,128)(2,1)S(1)}, f32[2,160,128]{2,1,0:T(8,128)S(1)}, f32[32,1024]{1,0:T(8,128)S(1)}, f32[16,432]{1,0:T(8,128)S(1)}) custom-call(bf16[16,8,8,128]{3,2,1,0:T(8,128)(2,1)S(1)} %copy-done, bf16[3,160,768]{2,1,0:T(8,128)(2,1)S(1)} %get-tuple-element.31.conv_ref, bf16[768,1536]{1,0:T(8,128)(2,1)S(1)} %get-tuple-element.32.up_ref), custom_call_target="tpu_custom_call" | custom-call | flops 2000000000 | bytes 2000000 | tf_op jit(solution)/shard_map/pallas_call | solution.py:570
  15.6 0.1 collective-permute-start.4
  15.7 0.0 collective-permute-done.2
  15.7 0.0 collective-permute-done.1
  15.7 2.5 %shard_map.87 = bf16[32,40,128]{2,1,0:T(8,128)(2,1)} custom-call(s32[2]{0:T(128)S(1)} %pad_add_fusion.place_ref, bf16[16,8,8,128]{3,2,1,0:T(8,128)(2,1)S(1)} %copy-done, bf16[144,128]{1,0:T(8,128)(2,1)S(1)} %get-tuple-element.61.x_low_ref, bf16[144,128]{1,0:T(8,128)(2,1)S(1)} %get-tuple-element.60.x_high_ref, ...), custom_call_target="tpu_custom_call" | custom-call | flops 2000000000 | bytes 2000000 | tf_op jit(solution)/shard_map/pallas_call | solution.py:570
  18.3 1.3 %collective-permute-done.4 = f32[16,432]{1,0:T(8,128)S(1)} collective-permute-done((f32[16,432]{1,0:T(8,128)S(1)}, f32[16,432]{1,0:T(8,128)S(1)}, u32[]{:S(2)}, u32[]{:S(2)}) %collective-permute-start.4) | collective-permute-done | bytes 27680 | tf_op jit(solution)/shard_map/ppermute | solution.py:594
  19.5 4.9 %all-to-all-start = ((bf16[32,40,128]{2,1,0:T(8,128)(2,1)}), bf16[32,40,128]{2,1,0:T(8,128)(2,1)S(1)}, u32[]{:S(2)}, u32[]{:S(2)}) async-start(bf16[32,40,128]{2,1,0:T(8,128)(2,1)} %shard_map.87), calls=%async_computation | async-start | bytes 655360 | tf_op jit(solution)/shard_map/all_to_all | solution.py:722
  24.5 0.3 collective-permute-start.5
  24.8 1.0 %collective-permute-done.5 = f32[16,432]{1,0:T(8,128)S(1)} collective-permute-done((f32[16,432]{1,0:T(8,128)S(1)}, f32[16,432]{1,0:T(8,128)S(1)}, u32[]{:S(2)}, u32[]{:S(2)}) %collective-permute-start.5) | collective-permute-done | bytes 27680 | tf_op jit(solution)/shard_map/ppermute | solution.py:594
  25.7 1.8 %collective-permute-start.6 = (f32[16,432]{1,0:T(8,128)S(1)}, f32[16,432]{1,0:T(8,128)S(1)}, u32[]{:S(2)}, u32[]{:S(2)}) collective-permute-start(f32[16,432]{1,0:T(8,128)S(1)} %add.20), channel_id=1, source_target_pairs={{0,4},{1,5},{2,6},{3,7},{4,0},{5,1},{6,2},{7,3},{8,12},{9,13},{10,... | collective-permute-start | bytes 82952 | tf_op jit(solution)/shard_map/ppermute | solution.py:594
  27.5 1.2 %shard_map.88 = (bf16[2048,128]{1,0:T(8,128)(2,1)S(1)}, f32[256,128]{1,0:T(8,128)S(1)}, bf16[3,384,64]{2,1,0:T(8,128)(2,1)S(1)}, bf16[432,512]{1,0:T(8,128)(2,1)S(1)}) custom-call(s32[2]{0:T(128)S(1)} %pad_add_fusion.place_ref, bf16[256,128]{1,0:T(8,128)(2,1)S(1)} %get-tuple-element.39.encoded_ref, f32[256,128]{1,0:T(8,128)S(1)} %get-tuple-element.40.pre_ref, ...), custom_call_target="tpu_custom_call" | custom-call | flops 1000000000 | bytes 2000000 | tf_op jit(solution)/shard_map/pallas_call | solution.py:570
  28.7 2.1 %collective-permute-done.6 = f32[16,432]{1,0:T(8,128)S(1)} collective-permute-done((f32[16,432]{1,0:T(8,128)S(1)}, f32[16,432]{1,0:T(8,128)S(1)}, u32[]{:S(2)}, u32[]{:S(2)}) %collective-permute-start.6) | collective-permute-done | bytes 27680 | tf_op jit(solution)/shard_map/ppermute | solution.py:594
  30.8 3.9 %collective-permute-start.9 = (f32[16,432]{1,0:T(8,128)S(1)}, f32[16,432]{1,0:T(8,128)S(1)}, u32[]{:S(2)}, u32[]{:S(2)}) collective-permute-start(f32[16,432]{1,0:T(8,128)S(1)} %add.21.refs_0_), channel_id=1, source_target_pairs={{0,24},{1,25},{2,26},{3,27},{4,28},{5,29},{6,30},{7,31},{8,16},{9,... | collective-permute-start | bytes 82952 | tf_op jit(solution)/shard_map/ppermute | solution.py:594
  34.7 0.0 collective-permute-start.8
  34.7 0.6 %collective-permute-start.7 = (f32[16,432]{1,0:T(8,128)S(1)}, f32[16,432]{1,0:T(8,128)S(1)}, u32[]{:S(2)}, u32[]{:S(2)}) collective-permute-start(f32[16,432]{1,0:T(8,128)S(1)} %add.21.refs_0_), channel_id=1, source_target_pairs={{0,8},{1,9},{2,10},{3,11},{4,12},{5,13},{6,14},{7,15},{8,0},{9,1},... | collective-permute-start | bytes 82952 | tf_op jit(solution)/shard_map/ppermute | solution.py:594
  35.4 1.1 %all-to-all-done.got_ref = bf16[32,40,128]{2,1,0:T(8,128)(2,1)S(1)} async-done(((bf16[32,40,128]{2,1,0:T(8,128)(2,1)}), bf16[32,40,128]{2,1,0:T(8,128)(2,1)S(1)}, u32[]{:S(2)}, u32[]{:S(2)}) %all-to-all-start) | async-done | bytes 327712 | tf_op jit(solution)/shard_map/all_to_all | solution.py:722
  36.4 2.2 %shard_map.89 = (f32[16,16,64]{2,1,0:T(8,128)}, f32[27,64,64]{2,1,0:T(8,128)}, f32[16,16,64]{2,1,0:T(8,128)}, f32[8,128]{1,0:T(8,128)S(1)}) custom-call(bf16[32,40,128]{2,1,0:T(8,128)(2,1)S(1)} %all-to-all-done.got_ref, bf16[2048,128]{1,0:T(8,128)(2,1)S(1)} %get-tuple-element.41.spread_ref, f32[256,128]{1,0:T(8,128)S(1)} %get-tuple-element.42.slope_ref, ...), custom_call_target="tpu_custom_call" | custom-call | flops 2000000000 | bytes 2000000 | tf_op jit(solution)/shard_map/pallas_call | solution.py:570
  38.7 0.0 collective-permute-done.9.refs_3_
  38.7 0.9 %collective-permute-done.8.refs_2_ = f32[16,432]{1,0:T(8,128)S(1)} collective-permute-done((f32[16,432]{1,0:T(8,128)S(1)}, f32[16,432]{1,0:T(8,128)S(1)}, u32[]{:S(2)}, u32[]{:S(2)}) %collective-permute-start.8) | collective-permute-done | bytes 27680 | tf_op jit(solution)/shard_map/ppermute | solution.py:594
  39.5 0.0 collective-permute-done.7.refs_1_
  39.6 0.9 %shard_map.90 = f32[16,16,27]{2,1,0:T(8,128)} custom-call(bf16[432,512]{1,0:T(8,128)(2,1)S(1)} %get-tuple-element.48.order_ref, f32[8,128]{1,0:T(8,128)S(1)} %get-tuple-element.49.done_ref, f32[16,432]{1,0:T(8,128)S(1)} %add.21.refs_0_, f32[16,432]{1,0:T(8,128)S(1)} %collective-permute-done.7.refs_1_, f32[16,432]{1,0:T(8,128)S(1)} %collective-permute-done.8.refs_2_, ...), custom_call_target="tpu_custom_call" | custom-call | flops 100000000 | bytes 2000000 | tf_op jit(solution)/shard_map/pallas_call | solution.py:570
  (10 shorter events, 0.1 us)
Async XLA Ops:
  0.6 9.3 %copy-start.3 = (bf16[64,16,1,16]{0,3,2,1:T(8,128)(2,1)S(1)}, bf16[64,16,1,16]{0,3,2,1:T(8,128)(2,1)}, u32[]{:S(2)}) copy-start(bf16[64,16,1,16]{0,3,2,1:T(8,128)(2,1)} %param.5) | copy-start | bytes 98308
  0.6 9.3 %copy-start.1 = (bf16[27,64,64]{2,1,0:T(8,128)(2,1)S(1)}, bf16[27,64,64]{2,1,0:T(8,128)(2,1)}, u32[]{:S(2)}) copy-start(bf16[27,64,64]{2,1,0:T(8,128)(2,1)} %enc_ref.3) | copy-start | bytes 663556
  0.7 9.3 %copy-start.2 = (bf16[27,16,16]{0,2,1:T(8,128)(2,1)S(1)}, bf16[27,16,16]{0,2,1:T(8,128)(2,1)}, u32[]{:S(2)}) copy-start(bf16[27,16,16]{0,2,1:T(8,128)(2,1)} %param.8) | copy-start | bytes 41476
  1.8 6.0 %collective-permute-start = (bf16[16,8,128]{2,1,0:T(8,128)(2,1)S(1)}, bf16[16,8,128]{2,1,0:T(8,128)(2,1)S(1)}, u32[]{:S(2)}, u32[]{:S(2)}) collective-permute-start(bf16[16,8,128]{2,1,0:T(8,128)(2,1)S(1)} %bitcast.30), channel_id=1, source_target_pairs={{0,1},{1,0},{2,3},{3,2},{4,5},{5,4},{6,7},{7,6},{8,9},{9,8},{10,11... | collective-permute-start | bytes 98312 | tf_op jit(solution)/shard_map/ppermute | solution.py:604
  4.8 5.1 %collective-permute-start.3 = (bf16[16,16,64]{2,1,0:T(8,128)(2,1)}, bf16[16,16,64]{2,1,0:T(8,128)(2,1)S(1)}, u32[]{:S(2)}, u32[]{:S(2)}) collective-permute-start(bf16[16,16,64]{2,1,0:T(8,128)(2,1)} %bitcast.27), channel_id=1, source_target_pairs={{0,1},{1,0},{2,3},{3,2},{4,5},{5,4},{6,7},{7,6},{8,9},{9,8},{10,11... | collective-permute-start | bytes 98312 | tf_op jit(solution)/shard_map/ppermute | solution.py:602
  7.8 7.9 %collective-permute-start.2 = (bf16[144,128]{1,0:T(8,128)(2,1)S(1)}, bf16[144,128]{1,0:T(8,128)(2,1)S(1)}, u32[]{:S(2)}, u32[]{:S(2)}) collective-permute-start(bf16[144,128]{1,0:T(8,128)(2,1)S(1)} %pad_maximum_fusion.1), channel_id=1, source_target_pairs={{0,2},{1,3},{2,0},{3,1},{4,6},{5,7},{6,4},{7,5},{8,10},{9,11},{10,... | collective-permute-start | bytes 110600 | tf_op jit(solution)/shard_map/ppermute | solution.py:629
  7.9 7.8 %collective-permute-start.1 = (bf16[144,128]{1,0:T(8,128)(2,1)S(1)}, bf16[144,128]{1,0:T(8,128)(2,1)S(1)}, u32[]{:S(2)}, u32[]{:S(2)}) collective-permute-start(bf16[144,128]{1,0:T(8,128)(2,1)S(1)} %pad_maximum_fusion), channel_id=1, source_target_pairs={{0,1},{1,0},{2,4},{3,5},{4,2},{5,3},{6,8},{7,9},{8,6},{9,7},{10,12... | collective-permute-start | bytes 110600 | tf_op jit(solution)/shard_map/ppermute | solution.py:629
  9.9 3.3 %copy-start = (bf16[16,8,8,128]{3,2,1,0:T(8,128)(2,1)S(1)}, bf16[16,8,8,128]{3,2,1,0:T(8,128)(2,1)}, u32[]{:S(2)}) copy-start(bf16[16,8,8,128]{3,2,1,0:T(8,128)(2,1)} %cot_ref.3) | copy-start | bytes 786436
  15.6 3.9 %collective-permute-start.4 = (f32[16,432]{1,0:T(8,128)S(1)}, f32[16,432]{1,0:T(8,128)S(1)}, u32[]{:S(2)}, u32[]{:S(2)}) collective-permute-start(f32[16,432]{1,0:T(8,128)S(1)} %get-tuple-element.50), channel_id=1, source_target_pairs={{0,1},{1,0},{2,3},{3,2},{4,5},{5,4},{6,7},{7,6},{8,9},{9,8},{10,11... | collective-permute-start | bytes 82952 | tf_op jit(solution)/shard_map/ppermute | solution.py:594
  19.5 16.9 %all-to-all-start = ((bf16[32,40,128]{2,1,0:T(8,128)(2,1)}), bf16[32,40,128]{2,1,0:T(8,128)(2,1)S(1)}, u32[]{:S(2)}, u32[]{:S(2)}) async-start(bf16[32,40,128]{2,1,0:T(8,128)(2,1)} %shard_map.87), calls=%async_computation | async-start | bytes 655360 | tf_op jit(solution)/shard_map/all_to_all | solution.py:722
  24.5 1.3 %collective-permute-start.5 = (f32[16,432]{1,0:T(8,128)S(1)}, f32[16,432]{1,0:T(8,128)S(1)}, u32[]{:S(2)}, u32[]{:S(2)}) collective-permute-start(f32[16,432]{1,0:T(8,128)S(1)} %add.19), channel_id=1, source_target_pairs={{0,2},{1,3},{2,0},{3,1},{4,6},{5,7},{6,4},{7,5},{8,10},{9,11},{10,... | collective-permute-start | bytes 82952 | tf_op jit(solution)/shard_map/ppermute | solution.py:594
  25.7 5.1 %collective-permute-start.6 = (f32[16,432]{1,0:T(8,128)S(1)}, f32[16,432]{1,0:T(8,128)S(1)}, u32[]{:S(2)}, u32[]{:S(2)}) collective-permute-start(f32[16,432]{1,0:T(8,128)S(1)} %add.20), channel_id=1, source_target_pairs={{0,4},{1,5},{2,6},{3,7},{4,0},{5,1},{6,2},{7,3},{8,12},{9,13},{10,... | collective-permute-start | bytes 82952 | tf_op jit(solution)/shard_map/ppermute | solution.py:594
  30.8 7.8 %collective-permute-start.9 = (f32[16,432]{1,0:T(8,128)S(1)}, f32[16,432]{1,0:T(8,128)S(1)}, u32[]{:S(2)}, u32[]{:S(2)}) collective-permute-start(f32[16,432]{1,0:T(8,128)S(1)} %add.21.refs_0_), channel_id=1, source_target_pairs={{0,24},{1,25},{2,26},{3,27},{4,28},{5,29},{6,30},{7,31},{8,16},{9,... | collective-permute-start | bytes 82952 | tf_op jit(solution)/shard_map/ppermute | solution.py:594
  34.7 4.8 %collective-permute-start.8 = (f32[16,432]{1,0:T(8,128)S(1)}, f32[16,432]{1,0:T(8,128)S(1)}, u32[]{:S(2)}, u32[]{:S(2)}) collective-permute-start(f32[16,432]{1,0:T(8,128)S(1)} %add.21.refs_0_), channel_id=1, source_target_pairs={{0,16},{1,17},{2,18},{3,19},{4,20},{5,21},{6,22},{7,23},{8,24},{9,... | collective-permute-start | bytes 82952 | tf_op jit(solution)/shard_map/ppermute | solution.py:594
  34.7 4.8 %collective-permute-start.7 = (f32[16,432]{1,0:T(8,128)S(1)}, f32[16,432]{1,0:T(8,128)S(1)}, u32[]{:S(2)}, u32[]{:S(2)}) collective-permute-start(f32[16,432]{1,0:T(8,128)S(1)} %add.21.refs_0_), channel_id=1, source_target_pairs={{0,8},{1,9},{2,10},{3,11},{4,12},{5,13},{6,14},{7,15},{8,0},{9,1},... | collective-permute-start | bytes 82952 | tf_op jit(solution)/shard_map/ppermute | solution.py:594

commit v7 on v6

--- a/solution.py
+++ b/solution.py
@@ -364,14 +364,14 @@
 
 def spread_kernel(
     place_ref, cot_ref, x_low_ref, x_high_ref, z_low_ref, z_high_ref, own_ref, outer_ref, edge_ref,
-    back_ref, wide_ref, send_hbm, grad_ref, send_ref, cells_ref, sems, *, planes_x, planes_z
+    back_ref, wide_ref, send_ref, grad_ref, *, planes_x, planes_z
 ):
     fine_ch, planes, depth, width = cot_ref.shape
     main = fine_ch * depth
     own = planes * width
     rows = outer_ref.shape[1]
     chans = wide_ref.shape[2] // RATIO
-    owners, chunk, _ = send_hbm.shape
+    owners, chunk, _ = send_ref.shape
     span = chunk - RATIO
     own_x = place_ref[0]
     own_z = place_ref[1]
@@ -419,9 +419,7 @@
         first = owner * RATIO * RATIO // owners
         x = first // RATIO
         top = first % RATIO * fine_ch
-        send_ref[owner] = turned[top : top + span, x * width : (x + 1) * width]
-    store = pltpu.make_async_copy(send_ref, send_hbm.at[:, :span], sems.at[0])
-    store.start()
+        send_ref[owner, :span] = turned[top : top + span, x * width : (x + 1) * width]
     parts = dot_tn(
         jnp.concatenate([flipped[:, x * width : (x + 1) * width] for x in range(planes)], 0),
         wide_ref[...].reshape(planes * main, RATIO * chans),
@@ -437,11 +435,7 @@
     half = cells.shape[0] // 2
     cells = jnp.where(iota((half, two), 1) < chans, cells[:half], cells[half:]).astype(BF16)
     for owner in range(owners):
-        cells_ref[owner] = cells
-    last = pltpu.make_async_copy(cells_ref, send_hbm.at[:, span:], sems.at[1])
-    last.start()
-    store.wait()
-    last.wait()
+        send_ref[owner, span:] = cells
 
 
 def widen_kernel(
@@ -557,7 +551,7 @@
     up_out[...] = (sums * scale).reshape(pairs * RATIO, fine_ch, chans)
 
 
-def call(kernel, out_shape, args, scratch=(), scalars=0, flops=1e8, hbm=(), hbm_out=()):
+def call(kernel, out_shape, args, scratch=(), scalars=0, flops=1e8, hbm=()):
     specs = [pl.BlockSpec(memory_space=pltpu.SMEM)] * scalars
     specs += [
         pl.BlockSpec(memory_space=pltpu.HBM if n in hbm else VMEM)
@@ -571,10 +565,7 @@
         kernel,
         out_shape=[jax.ShapeDtypeStruct(*s) for s in out_shape],
         in_specs=specs,
-        out_specs=[
-            pl.BlockSpec(memory_space=pltpu.HBM if n in hbm_out else VMEM)
-            for n in range(len(out_shape))
-        ],
+        out_specs=[pl.BlockSpec(memory_space=VMEM)] * len(out_shape),
         scratch_shapes=list(scratch),
         compiler_params=pltpu.CompilerParams(vmem_limit_bytes=VMEM_LIMIT),
         cost_estimate=pl.CostEstimate(
@@ -696,13 +687,9 @@
         ),
         scratch=[
             VMEM((3 * rows, own + 2 * fine_width), BF16),
-            VMEM((owners, chunk - RATIO, fine_width), BF16),
-            VMEM((owners, RATIO, fine_width), BF16),
-            pltpu.SemaphoreType.DMA((2,)),
         ],
         scalars=1,
         flops=2e9,
-        hbm_out=(0,),
     )
     steps = [1 << n for n in range(owners.bit_length() - 1)]
     if owners & (owners - 1):

time: 40.7 us -> 40.7 us (level)
  transfers between devices with their start and end apart: 11 -> 11, of which waited for: 5 -> 5; matrix products, arithmetic and copies ran while one was open for 0% -> 0% of each run, Pallas kernels for 35% -> 36%
where the time goes in v7:
time: 40.7 us; the launch traced here: 40.5 us
  starting transfers between devices  16.8 us (41%)
  Pallas kernels  15.4 us (38%)
  waiting for transfers between devices  6.26 us (15%)
  local copies, waits for them, and re-layouts  1.14 us (3%)
  between operations  0.83 us (2%)
    pallas_call x7, Pallas kernels, call(): pl.pallas_call(kernel, out_shape=[jax.ShapeDtypeStruct(*s) for s in out_s...  15.4 us
    ppermute x6, starting transfers between devices, swapped(): return lax.ppermute(value, AXES, [(i, i ^ step) for i in range(count)])  6.73 us
    ppermute x6, waiting for transfers between devices, swapped(): return lax.ppermute(value, AXES, [(i, i ^ step) for i in range(count)])  5.2 us
    all_to_all x1, starting transfers between devices, on_device(): got = lax.all_to_all(send, AXES, 0, 0, tiled=True)  4.9 us
    ppermute x1, starting transfers between devices, exchange_depth(): lax.ppermute(lax.dynamic_index_in_dim(cotangent, z, 2, False), 'narrow',...  3 us
    ppermute x2, starting transfers between devices, exchange_width(): got.append(lax.ppermute(send, AXES, list(partner.items())))  2.07 us
    dynamic_slice x1, local copies, waits for them, and re-layouts, exchange_depth(): lax.dynamic_index_in_dim(cotangent, z, 2, False)  1.08 us
    all_to_all x1, waiting for transfers between devices, on_device(): got = lax.all_to_all(send, AXES, 0, 0, tiled=True)  1.06 us
  transfers between devices with their start and end apart: 11, of which 5 were waited for; matrix products, arithmetic and copies ran while one was open for 0% of the time, Pallas kernels for 36%

profile of v7, /device:TPU:0, one launch (start us, length us, event | category | flops | bytes accessed | tf_op | source)
XLA Modules:
  0.0 40.5 jit_solution(17835804647588656865)
XLA Ops:
  0.6 0.0 copy-start.3
  0.6 0.0 copy-start.1
  0.7 0.0 copy-start.2
  0.7 1.1 %constant_dynamic-slice_fusion.2 = bf16[16,8,1,128]{3,2,1,0:T(2,128)(2,1)S(1)} fusion(bf16[16,8,8,128]{3,2,1,0:T(8,128)(2,1)} %cot_ref.3, s32[]{:T(128)S(6)} %select_n.36), kind=kLoop, calls=%fused_computation.9 | loop fusion | bytes 65540 | tf_op jit(solution)/shard_map/jit(dynamic_index_in_dim)/dynamic_slice | solution.py:595
  1.8 3.0 %collective-permute-start = (bf16[16,8,128]{2,1,0:T(8,128)(2,1)S(1)}, bf16[16,8,128]{2,1,0:T(8,128)(2,1)S(1)}, u32[]{:S(2)}, u32[]{:S(2)}) collective-permute-start(bf16[16,8,128]{2,1,0:T(8,128)(2,1)S(1)} %bitcast.30), channel_id=1, source_target_pairs={{0,1},{1,0},{2,3},{3,2},{4,5},{5,4},{6,7},{7,6},{8,9},{9,8},{10,11... | collective-permute-start | bytes 98312 | tf_op jit(solution)/shard_map/ppermute | solution.py:595
  4.8 0.1 collective-permute-start.3
  4.9 0.1 pad_add_fusion.place_ref
  4.9 2.8 %shard_map.84 = (bf16[8,128,512]{2,1,0:T(8,128)(2,1)S(1)}, bf16[16,8,128]{2,1,0:T(8,128)(2,1)S(1)}, bf16[16,8,128]{2,1,0:T(8,128)(2,1)S(1)}) custom-call(s32[2]{0:T(128)S(1)} %pad_add_fusion.place_ref, bf16[16,64,512]{2,1,0:T(8,128)(2,1)} %bitcast.33, bf16[16,8,8,128]{3,2,1,0:T(8,128)(2,1)} %cot_ref.3), custom_call_target="tpu_custom_call" | custom-call | flops 1000000000 | bytes 2000000 | tf_op jit(solution)/shard_map/pallas_call | solution.py:564
  7.7 0.0 collective-permute-done.z_low_ref.z_high_ref
  7.8 0.1 collective-permute-start.2
  7.9 2.0 %collective-permute-start.1 = (bf16[144,128]{1,0:T(8,128)(2,1)S(1)}, bf16[144,128]{1,0:T(8,128)(2,1)S(1)}, u32[]{:S(2)}, u32[]{:S(2)}) collective-permute-start(bf16[144,128]{1,0:T(8,128)(2,1)S(1)} %pad_maximum_fusion), channel_id=1, source_target_pairs={{0,1},{1,0},{2,4},{3,5},{4,2},{5,3},{6,8},{7,9},{8,6},{9,7},{10,12... | collective-permute-start | bytes 110600 | tf_op jit(solution)/shard_map/ppermute | solution.py:620
  9.9 0.0 collective-permute-done.3.refs_1_
  9.9 0.0 copy-done.3
  9.9 0.0 copy-done.1
  9.9 0.0 copy-done.2
  9.9 0.0 copy-start
  9.9 3.3 %shard_map.85 = (bf16[3,160,768]{2,1,0:T(8,128)(2,1)S(1)}, bf16[128,1440]{1,0:T(8,128)(2,1)S(1)}, f32[256,128]{1,0:T(8,128)S(1)}, bf16[256,128]{1,0:T(8,128)(2,1...) custom-call(s32[2]{0:T(128)S(1)} %pad_add_fusion.place_ref, bf16[16,16,27]{2,1,0:T(8,128)(2,1)S(1)} %bitcast.26, ...), custom_call_target="tpu_custom_call" | custom-call | flops 2000000000 | bytes 2000000 | tf_op jit(solution)/shard_map/pallas_call | solution.py:564
  13.2 0.0 copy-done
  13.2 2.4 %shard_map.86 = (bf16[384,1024]{1,0:T(8,128)(2,1)S(1)}, f32[2,160,128]{2,1,0:T(8,128)S(1)}, f32[32,1024]{1,0:T(8,128)S(1)}, f32[16,432]{1,0:T(8,128)S(1)}) custom-call(bf16[16,8,8,128]{3,2,1,0:T(8,128)(2,1)S(1)} %copy-done, bf16[3,160,768]{2,1,0:T(8,128)(2,1)S(1)} %get-tuple-element.31.conv_ref, bf16[768,1536]{1,0:T(8,128)(2,1)S(1)} %get-tuple-element.32.up_ref), custom_call_target="tpu_custom_call" | custom-call | flops 2000000000 | bytes 2000000 | tf_op jit(solution)/shard_map/pallas_call | solution.py:564
  15.6 0.1 collective-permute-start.4
  15.7 0.0 collective-permute-done.2
  15.7 0.0 collective-permute-done.1
  15.7 2.6 %shard_map.87 = bf16[32,40,128]{2,1,0:T(8,128)(2,1)} custom-call(s32[2]{0:T(128)S(1)} %pad_add_fusion.place_ref, bf16[16,8,8,128]{3,2,1,0:T(8,128)(2,1)S(1)} %copy-done, bf16[144,128]{1,0:T(8,128)(2,1)S(1)} %get-tuple-element.61.x_low_ref, bf16[144,128]{1,0:T(8,128)(2,1)S(1)} %get-tuple-element.60.x_high_ref, ...), custom_call_target="tpu_custom_call" | custom-call | flops 2000000000 | bytes 2000000 | tf_op jit(solution)/shard_map/pallas_call | solution.py:564
  18.3 1.2 %collective-permute-done.4 = f32[16,432]{1,0:T(8,128)S(1)} collective-permute-done((f32[16,432]{1,0:T(8,128)S(1)}, f32[16,432]{1,0:T(8,128)S(1)}, u32[]{:S(2)}, u32[]{:S(2)}) %collective-permute-start.4) | collective-permute-done | bytes 27680 | tf_op jit(solution)/shard_map/ppermute | solution.py:585
  19.5 4.9 %all-to-all-start = ((bf16[32,40,128]{2,1,0:T(8,128)(2,1)}), bf16[32,40,128]{2,1,0:T(8,128)(2,1)S(1)}, u32[]{:S(2)}, u32[]{:S(2)}) async-start(bf16[32,40,128]{2,1,0:T(8,128)(2,1)} %shard_map.87), calls=%async_computation | async-start | bytes 655360 | tf_op jit(solution)/shard_map/all_to_all | solution.py:709
  24.5 0.3 collective-permute-start.5
  24.8 1.0 %collective-permute-done.5 = f32[16,432]{1,0:T(8,128)S(1)} collective-permute-done((f32[16,432]{1,0:T(8,128)S(1)}, f32[16,432]{1,0:T(8,128)S(1)}, u32[]{:S(2)}, u32[]{:S(2)}) %collective-permute-start.5) | collective-permute-done | bytes 27680 | tf_op jit(solution)/shard_map/ppermute | solution.py:585
  25.7 1.8 %collective-permute-start.6 = (f32[16,432]{1,0:T(8,128)S(1)}, f32[16,432]{1,0:T(8,128)S(1)}, u32[]{:S(2)}, u32[]{:S(2)}) collective-permute-start(f32[16,432]{1,0:T(8,128)S(1)} %add.20), channel_id=1, source_target_pairs={{0,4},{1,5},{2,6},{3,7},{4,0},{5,1},{6,2},{7,3},{8,12},{9,13},{10,... | collective-permute-start | bytes 82952 | tf_op jit(solution)/shard_map/ppermute | solution.py:585
  27.5 1.2 %shard_map.88 = (bf16[2048,128]{1,0:T(8,128)(2,1)S(1)}, f32[256,128]{1,0:T(8,128)S(1)}, bf16[3,384,64]{2,1,0:T(8,128)(2,1)S(1)}, bf16[432,512]{1,0:T(8,128)(2,1)S(1)}) custom-call(s32[2]{0:T(128)S(1)} %pad_add_fusion.place_ref, bf16[256,128]{1,0:T(8,128)(2,1)S(1)} %get-tuple-element.39.encoded_ref, f32[256,128]{1,0:T(8,128)S(1)} %get-tuple-element.40.pre_ref, ...), custom_call_target="tpu_custom_call" | custom-call | flops 1000000000 | bytes 2000000 | tf_op jit(solution)/shard_map/pallas_call | solution.py:564
  28.7 2.1 %collective-permute-done.6 = f32[16,432]{1,0:T(8,128)S(1)} collective-permute-done((f32[16,432]{1,0:T(8,128)S(1)}, f32[16,432]{1,0:T(8,128)S(1)}, u32[]{:S(2)}, u32[]{:S(2)}) %collective-permute-start.6) | collective-permute-done | bytes 27680 | tf_op jit(solution)/shard_map/ppermute | solution.py:585
  30.8 3.9 %collective-permute-start.9 = (f32[16,432]{1,0:T(8,128)S(1)}, f32[16,432]{1,0:T(8,128)S(1)}, u32[]{:S(2)}, u32[]{:S(2)}) collective-permute-start(f32[16,432]{1,0:T(8,128)S(1)} %add.21.refs_0_), channel_id=1, source_target_pairs={{0,24},{1,25},{2,26},{3,27},{4,28},{5,29},{6,30},{7,31},{8,16},{9,... | collective-permute-start | bytes 82952 | tf_op jit(solution)/shard_map/ppermute | solution.py:585
  34.7 0.0 collective-permute-start.8
  34.7 0.6 %collective-permute-start.7 = (f32[16,432]{1,0:T(8,128)S(1)}, f32[16,432]{1,0:T(8,128)S(1)}, u32[]{:S(2)}, u32[]{:S(2)}) collective-permute-start(f32[16,432]{1,0:T(8,128)S(1)} %add.21.refs_0_), channel_id=1, source_target_pairs={{0,8},{1,9},{2,10},{3,11},{4,12},{5,13},{6,14},{7,15},{8,0},{9,1},... | collective-permute-start | bytes 82952 | tf_op jit(solution)/shard_map/ppermute | solution.py:585
  35.4 1.1 %all-to-all-done.got_ref = bf16[32,40,128]{2,1,0:T(8,128)(2,1)S(1)} async-done(((bf16[32,40,128]{2,1,0:T(8,128)(2,1)}), bf16[32,40,128]{2,1,0:T(8,128)(2,1)S(1)}, u32[]{:S(2)}, u32[]{:S(2)}) %all-to-all-start) | async-done | bytes 327712 | tf_op jit(solution)/shard_map/all_to_all | solution.py:709
  36.4 2.2 %shard_map.89 = (f32[16,16,64]{2,1,0:T(8,128)}, f32[27,64,64]{2,1,0:T(8,128)}, f32[16,16,64]{2,1,0:T(8,128)}, f32[8,128]{1,0:T(8,128)S(1)}) custom-call(bf16[32,40,128]{2,1,0:T(8,128)(2,1)S(1)} %all-to-all-done.got_ref, bf16[2048,128]{1,0:T(8,128)(2,1)S(1)} %get-tuple-element.41.spread_ref, f32[256,128]{1,0:T(8,128)S(1)} %get-tuple-element.42.slope_ref, ...), custom_call_target="tpu_custom_call" | custom-call | flops 2000000000 | bytes 2000000 | tf_op jit(solution)/shard_map/pallas_call | solution.py:564
  38.7 0.0 collective-permute-done.9.refs_3_
  38.7 0.9 %collective-permute-done.8.refs_2_ = f32[16,432]{1,0:T(8,128)S(1)} collective-permute-done((f32[16,432]{1,0:T(8,128)S(1)}, f32[16,432]{1,0:T(8,128)S(1)}, u32[]{:S(2)}, u32[]{:S(2)}) %collective-permute-start.8) | collective-permute-done | bytes 27680 | tf_op jit(solution)/shard_map/ppermute | solution.py:585
  39.5 0.0 collective-permute-done.7.refs_1_
  39.6 0.9 %shard_map.90 = f32[16,16,27]{2,1,0:T(8,128)} custom-call(bf16[432,512]{1,0:T(8,128)(2,1)S(1)} %get-tuple-element.48.order_ref, f32[8,128]{1,0:T(8,128)S(1)} %get-tuple-element.49.done_ref, f32[16,432]{1,0:T(8,128)S(1)} %add.21.refs_0_, f32[16,432]{1,0:T(8,128)S(1)} %collective-permute-done.7.refs_1_, f32[16,432]{1,0:T(8,128)S(1)} %collective-permute-done.8.refs_2_, ...), custom_call_target="tpu_custom_call" | custom-call | flops 100000000 | bytes 2000000 | tf_op jit(solution)/shard_map/pallas_call | solution.py:564
  (10 shorter events, 0.1 us)
Async XLA Ops:
  0.6 9.3 %copy-start.3 = (bf16[64,16,1,16]{0,3,2,1:T(8,128)(2,1)S(1)}, bf16[64,16,1,16]{0,3,2,1:T(8,128)(2,1)}, u32[]{:S(2)}) copy-start(bf16[64,16,1,16]{0,3,2,1:T(8,128)(2,1)} %param.5) | copy-start | bytes 98308
  0.6 9.3 %copy-start.1 = (bf16[27,64,64]{2,1,0:T(8,128)(2,1)S(1)}, bf16[27,64,64]{2,1,0:T(8,128)(2,1)}, u32[]{:S(2)}) copy-start(bf16[27,64,64]{2,1,0:T(8,128)(2,1)} %enc_ref.3) | copy-start | bytes 663556
  0.7 9.3 %copy-start.2 = (bf16[27,16,16]{0,2,1:T(8,128)(2,1)S(1)}, bf16[27,16,16]{0,2,1:T(8,128)(2,1)}, u32[]{:S(2)}) copy-start(bf16[27,16,16]{0,2,1:T(8,128)(2,1)} %param.8) | copy-start | bytes 41476
  1.8 6.0 %collective-permute-start = (bf16[16,8,128]{2,1,0:T(8,128)(2,1)S(1)}, bf16[16,8,128]{2,1,0:T(8,128)(2,1)S(1)}, u32[]{:S(2)}, u32[]{:S(2)}) collective-permute-start(bf16[16,8,128]{2,1,0:T(8,128)(2,1)S(1)} %bitcast.30), channel_id=1, source_target_pairs={{0,1},{1,0},{2,3},{3,2},{4,5},{5,4},{6,7},{7,6},{8,9},{9,8},{10,11... | collective-permute-start | bytes 98312 | tf_op jit(solution)/shard_map/ppermute | solution.py:595
  4.8 5.1 %collective-permute-start.3 = (bf16[16,16,64]{2,1,0:T(8,128)(2,1)}, bf16[16,16,64]{2,1,0:T(8,128)(2,1)S(1)}, u32[]{:S(2)}, u32[]{:S(2)}) collective-permute-start(bf16[16,16,64]{2,1,0:T(8,128)(2,1)} %bitcast.27), channel_id=1, source_target_pairs={{0,1},{1,0},{2,3},{3,2},{4,5},{5,4},{6,7},{7,6},{8,9},{9,8},{10,11... | collective-permute-start | bytes 98312 | tf_op jit(solution)/shard_map/ppermute | solution.py:593
  7.8 7.9 %collective-permute-start.2 = (bf16[144,128]{1,0:T(8,128)(2,1)S(1)}, bf16[144,128]{1,0:T(8,128)(2,1)S(1)}, u32[]{:S(2)}, u32[]{:S(2)}) collective-permute-start(bf16[144,128]{1,0:T(8,128)(2,1)S(1)} %pad_maximum_fusion.1), channel_id=1, source_target_pairs={{0,2},{1,3},{2,0},{3,1},{4,6},{5,7},{6,4},{7,5},{8,10},{9,11},{10,... | collective-permute-start | bytes 110600 | tf_op jit(solution)/shard_map/ppermute | solution.py:620
  7.9 7.8 %collective-permute-start.1 = (bf16[144,128]{1,0:T(8,128)(2,1)S(1)}, bf16[144,128]{1,0:T(8,128)(2,1)S(1)}, u32[]{:S(2)}, u32[]{:S(2)}) collective-permute-start(bf16[144,128]{1,0:T(8,128)(2,1)S(1)} %pad_maximum_fusion), channel_id=1, source_target_pairs={{0,1},{1,0},{2,4},{3,5},{4,2},{5,3},{6,8},{7,9},{8,6},{9,7},{10,12... | collective-permute-start | bytes 110600 | tf_op jit(solution)/shard_map/ppermute | solution.py:620
  9.9 3.3 %copy-start = (bf16[16,8,8,128]{3,2,1,0:T(8,128)(2,1)S(1)}, bf16[16,8,8,128]{3,2,1,0:T(8,128)(2,1)}, u32[]{:S(2)}) copy-start(bf16[16,8,8,128]{3,2,1,0:T(8,128)(2,1)} %cot_ref.3) | copy-start | bytes 786436
  15.6 3.9 %collective-permute-start.4 = (f32[16,432]{1,0:T(8,128)S(1)}, f32[16,432]{1,0:T(8,128)S(1)}, u32[]{:S(2)}, u32[]{:S(2)}) collective-permute-start(f32[16,432]{1,0:T(8,128)S(1)} %get-tuple-element.50), channel_id=1, source_target_pairs={{0,1},{1,0},{2,3},{3,2},{4,5},{5,4},{6,7},{7,6},{8,9},{9,8},{10,11... | collective-permute-start | bytes 82952 | tf_op jit(solution)/shard_map/ppermute | solution.py:585
  19.5 16.9 %all-to-all-start = ((bf16[32,40,128]{2,1,0:T(8,128)(2,1)}), bf16[32,40,128]{2,1,0:T(8,128)(2,1)S(1)}, u32[]{:S(2)}, u32[]{:S(2)}) async-start(bf16[32,40,128]{2,1,0:T(8,128)(2,1)} %shard_map.87), calls=%async_computation | async-start | bytes 655360 | tf_op jit(solution)/shard_map/all_to_all | solution.py:709
  24.5 1.3 %collective-permute-start.5 = (f32[16,432]{1,0:T(8,128)S(1)}, f32[16,432]{1,0:T(8,128)S(1)}, u32[]{:S(2)}, u32[]{:S(2)}) collective-permute-start(f32[16,432]{1,0:T(8,128)S(1)} %add.19), channel_id=1, source_target_pairs={{0,2},{1,3},{2,0},{3,1},{4,6},{5,7},{6,4},{7,5},{8,10},{9,11},{10,... | collective-permute-start | bytes 82952 | tf_op jit(solution)/shard_map/ppermute | solution.py:585
  25.7 5.1 %collective-permute-start.6 = (f32[16,432]{1,0:T(8,128)S(1)}, f32[16,432]{1,0:T(8,128)S(1)}, u32[]{:S(2)}, u32[]{:S(2)}) collective-permute-start(f32[16,432]{1,0:T(8,128)S(1)} %add.20), channel_id=1, source_target_pairs={{0,4},{1,5},{2,6},{3,7},{4,0},{5,1},{6,2},{7,3},{8,12},{9,13},{10,... | collective-permute-start | bytes 82952 | tf_op jit(solution)/shard_map/ppermute | solution.py:585
  30.8 7.8 %collective-permute-start.9 = (f32[16,432]{1,0:T(8,128)S(1)}, f32[16,432]{1,0:T(8,128)S(1)}, u32[]{:S(2)}, u32[]{:S(2)}) collective-permute-start(f32[16,432]{1,0:T(8,128)S(1)} %add.21.refs_0_), channel_id=1, source_target_pairs={{0,24},{1,25},{2,26},{3,27},{4,28},{5,29},{6,30},{7,31},{8,16},{9,... | collective-permute-start | bytes 82952 | tf_op jit(solution)/shard_map/ppermute | solution.py:585
  34.7 4.8 %collective-permute-start.8 = (f32[16,432]{1,0:T(8,128)S(1)}, f32[16,432]{1,0:T(8,128)S(1)}, u32[]{:S(2)}, u32[]{:S(2)}) collective-permute-start(f32[16,432]{1,0:T(8,128)S(1)} %add.21.refs_0_), channel_id=1, source_target_pairs={{0,16},{1,17},{2,18},{3,19},{4,20},{5,21},{6,22},{7,23},{8,24},{9,... | collective-permute-start | bytes 82952 | tf_op jit(solution)/shard_map/ppermute | solution.py:585
  34.7 4.8 %collective-permute-start.7 = (f32[16,432]{1,0:T(8,128)S(1)}, f32[16,432]{1,0:T(8,128)S(1)}, u32[]{:S(2)}, u32[]{:S(2)}) collective-permute-start(f32[16,432]{1,0:T(8,128)S(1)} %add.21.refs_0_), channel_id=1, source_target_pairs={{0,8},{1,9},{2,10},{3,11},{4,12},{5,13},{6,14},{7,15},{8,0},{9,1},... | collective-permute-start | bytes 82952 | tf_op jit(solution)/shard_map/ppermute | solution.py:585

commit v8 on v7

--- a/solution.py
+++ b/solution.py
@@ -357,9 +357,10 @@
         == row_index(shape[0]) % fine_ch * SPAN + 10 - row_index(shape[0]) // fine_ch
     )
     total = sum(dot_nt(fold, part) for part in split(jnp.concatenate(sums, 0)))
-    total_ref[...] = jnp.concatenate(
-        [total[b * fine_ch : (b + 1) * fine_ch] for b in range(3)], 1
-    )
+    total = jnp.concatenate([total[b * fine_ch : (b + 1) * fine_ch] for b in range(3)], 1)
+    rest = total[:, 3 * 128 :]
+    rest = jnp.concatenate([rest[:8], rest[8:], jnp.zeros((8, 32), F32)], 1)
+    total_ref[...] = jnp.concatenate([total[:, n * 128 : (n + 1) * 128] for n in range(3)] + [rest], 0)
 
 
 def spread_kernel(
@@ -476,6 +477,11 @@
     *parts, out_ref = refs
     total = sum(part[...] for part in parts) * scale
     fine_ch = out_ref.shape[0]
+    rest = total[3 * fine_ch :]
+    rest = jnp.concatenate([rest[:, :48], rest[:, 48:96]], 0)
+    total = jnp.concatenate(
+        [total[n * fine_ch : (n + 1) * fine_ch] for n in range(3)] + [rest], 1
+    )
     field = dot(jnp.concatenate(split(total), 0), order_ref[...])
     field = field[:fine_ch] + field[fine_ch : 2 * fine_ch] + field[2 * fine_ch :]
     step = field.shape[1] // fine_ch
@@ -672,7 +678,7 @@
             ((3 * main, own), BF16),
             ((2, rows, fine_width), F32),
             ((rows - main, own), F32),
-            ((fine_ch, 27 * fine_ch), F32),
+            ((3 * fine_ch + 8, 128), F32),
         ],
         (cotangent, conv, upsampled),
         flops=2e9,

time: 40.7 us -> 40.6 us (level)
    ppermute x6, waiting for transfers between devices: 5.2 us -> 4.62 us  [swapped(): return lax.ppermute(value, AXES, [(i, i ^ step) for i in range(count)])]
where the time goes in v8:
time: 40.6 us; the launch traced here: 40.2 us
  starting transfers between devices  16.6 us (41%)
  Pallas kernels  15.4 us (38%)
  waiting for transfers between devices  6 us (15%)
  local copies, waits for them, and re-layouts  1.14 us (3%)
  between operations  0.83 us (2%)
    pallas_call x7, Pallas kernels, call(): pl.pallas_call(kernel, out_shape=[jax.ShapeDtypeStruct(*s) for s in out_s...  15.4 us
    ppermute x6, starting transfers between devices, swapped(): return lax.ppermute(value, AXES, [(i, i ^ step) for i in range(count)])  6.58 us
    all_to_all x1, starting transfers between devices, on_device(): got = lax.all_to_all(send, AXES, 0, 0, tiled=True)  4.9 us
    ppermute x6, waiting for transfers between devices, swapped(): return lax.ppermute(value, AXES, [(i, i ^ step) for i in range(count)])  4.62 us
    ppermute x1, starting transfers between devices, exchange_depth(): lax.ppermute(lax.dynamic_index_in_dim(cotangent, z, 2, False), 'narrow',...  3 us
    ppermute x2, starting transfers between devices, exchange_width(): got.append(lax.ppermute(send, AXES, list(partner.items())))  2.07 us
    all_to_all x1, waiting for transfers between devices, on_device(): got = lax.all_to_all(send, AXES, 0, 0, tiled=True)  1.37 us
    dynamic_slice x1, local copies, waits for them, and re-layouts, exchange_depth(): lax.dynamic_index_in_dim(cotangent, z, 2, False)  1.08 us
  transfers between devices with their start and end apart: 11, of which 5 were waited for; matrix products, arithmetic and copies ran while one was open for 0% of the time, Pallas kernels for 36%

profile of v8, /device:TPU:0, one launch (start us, length us, event | category | flops | bytes accessed | tf_op | source)
XLA Modules:
  0.0 40.2 jit_solution(10459354551539304231)
XLA Ops:
  0.6 0.0 copy-start.3
  0.6 0.0 copy-start.1
  0.7 0.0 copy-start.2
  0.7 1.1 %constant_dynamic-slice_fusion.2 = bf16[16,8,1,128]{3,2,1,0:T(2,128)(2,1)S(1)} fusion(bf16[16,8,8,128]{3,2,1,0:T(8,128)(2,1)} %cot_ref.3, s32[]{:T(128)S(6)} %select_n.36), kind=kLoop, calls=%fused_computation.9 | loop fusion | bytes 65540 | tf_op jit(solution)/shard_map/jit(dynamic_index_in_dim)/dynamic_slice | solution.py:601
  1.8 3.0 %collective-permute-start = (bf16[16,8,128]{2,1,0:T(8,128)(2,1)S(1)}, bf16[16,8,128]{2,1,0:T(8,128)(2,1)S(1)}, u32[]{:S(2)}, u32[]{:S(2)}) collective-permute-start(bf16[16,8,128]{2,1,0:T(8,128)(2,1)S(1)} %bitcast.30), channel_id=1, source_target_pairs={{0,1},{1,0},{2,3},{3,2},{4,5},{5,4},{6,7},{7,6},{8,9},{9,8},{10,11... | collective-permute-start | bytes 98312 | tf_op jit(solution)/shard_map/ppermute | solution.py:601
  4.8 0.1 collective-permute-start.3
  4.9 0.1 pad_add_fusion.place_ref
  4.9 2.8 %shard_map.84 = (bf16[8,128,512]{2,1,0:T(8,128)(2,1)S(1)}, bf16[16,8,128]{2,1,0:T(8,128)(2,1)S(1)}, bf16[16,8,128]{2,1,0:T(8,128)(2,1)S(1)}) custom-call(s32[2]{0:T(128)S(1)} %pad_add_fusion.place_ref, bf16[16,64,512]{2,1,0:T(8,128)(2,1)} %bitcast.33, bf16[16,8,8,128]{3,2,1,0:T(8,128)(2,1)} %cot_ref.3), custom_call_target="tpu_custom_call" | custom-call | flops 1000000000 | bytes 2000000 | tf_op jit(solution)/shard_map/pallas_call | solution.py:570
  7.7 0.0 collective-permute-done.z_low_ref.z_high_ref
  7.8 0.1 collective-permute-start.2
  7.9 2.0 %collective-permute-start.1 = (bf16[144,128]{1,0:T(8,128)(2,1)S(1)}, bf16[144,128]{1,0:T(8,128)(2,1)S(1)}, u32[]{:S(2)}, u32[]{:S(2)}) collective-permute-start(bf16[144,128]{1,0:T(8,128)(2,1)S(1)} %pad_maximum_fusion), channel_id=1, source_target_pairs={{0,1},{1,0},{2,4},{3,5},{4,2},{5,3},{6,8},{7,9},{8,6},{9,7},{10,12... | collective-permute-start | bytes 110600 | tf_op jit(solution)/shard_map/ppermute | solution.py:626
  9.9 0.0 collective-permute-done.3.refs_1_
  9.9 0.0 copy-done.3
  9.9 0.0 copy-done.1
  9.9 0.0 copy-done.2
  9.9 0.0 copy-start
  9.9 3.3 %shard_map.85 = (bf16[3,160,768]{2,1,0:T(8,128)(2,1)S(1)}, bf16[128,1440]{1,0:T(8,128)(2,1)S(1)}, f32[256,128]{1,0:T(8,128)S(1)}, bf16[256,128]{1,0:T(8,128)(2,1...) custom-call(s32[2]{0:T(128)S(1)} %pad_add_fusion.place_ref, bf16[16,16,27]{2,1,0:T(8,128)(2,1)S(1)} %bitcast.26, ...), custom_call_target="tpu_custom_call" | custom-call | flops 2000000000 | bytes 2000000 | tf_op jit(solution)/shard_map/pallas_call | solution.py:570
  13.2 0.0 copy-done
  13.2 2.5 %shard_map.86 = (bf16[384,1024]{1,0:T(8,128)(2,1)S(1)}, f32[2,160,128]{2,1,0:T(8,128)S(1)}, f32[32,1024]{1,0:T(8,128)S(1)}, f32[56,128]{1,0:T(8,128)S(1)}) custom-call(bf16[16,8,8,128]{3,2,1,0:T(8,128)(2,1)S(1)} %copy-done, bf16[3,160,768]{2,1,0:T(8,128)(2,1)S(1)} %get-tuple-element.31.conv_ref, bf16[768,1536]{1,0:T(8,128)(2,1)S(1)} %get-tuple-element.32.up_ref), custom_call_target="tpu_custom_call" | custom-call | flops 2000000000 | bytes 2000000 | tf_op jit(solution)/shard_map/pallas_call | solution.py:570
  15.7 0.1 collective-permute-start.4
  15.8 0.0 collective-permute-done.2
  15.8 0.0 collective-permute-done.1
  15.8 2.6 %shard_map.87 = bf16[32,40,128]{2,1,0:T(8,128)(2,1)} custom-call(s32[2]{0:T(128)S(1)} %pad_add_fusion.place_ref, bf16[16,8,8,128]{3,2,1,0:T(8,128)(2,1)S(1)} %copy-done, bf16[144,128]{1,0:T(8,128)(2,1)S(1)} %get-tuple-element.61.x_low_ref, bf16[144,128]{1,0:T(8,128)(2,1)S(1)} %get-tuple-element.60.x_high_ref, ...), custom_call_target="tpu_custom_call" | custom-call | flops 2000000000 | bytes 2000000 | tf_op jit(solution)/shard_map/pallas_call | solution.py:570
  18.4 1.2 %collective-permute-done.4 = f32[56,128]{1,0:T(8,128)S(1)} collective-permute-done((f32[56,128]{1,0:T(8,128)S(1)}, f32[56,128]{1,0:T(8,128)S(1)}, u32[]{:S(2)}, u32[]{:S(2)}) %collective-permute-start.4) | collective-permute-done | bytes 28704 | tf_op jit(solution)/shard_map/ppermute | solution.py:591
  19.6 4.9 %all-to-all-start = ((bf16[32,40,128]{2,1,0:T(8,128)(2,1)}), bf16[32,40,128]{2,1,0:T(8,128)(2,1)S(1)}, u32[]{:S(2)}, u32[]{:S(2)}) async-start(bf16[32,40,128]{2,1,0:T(8,128)(2,1)} %shard_map.87), calls=%async_computation | async-start | bytes 655360 | tf_op jit(solution)/shard_map/all_to_all | solution.py:715
  24.5 0.3 collective-permute-start.5
  24.8 0.9 %collective-permute-done.5 = f32[56,128]{1,0:T(8,128)S(1)} collective-permute-done((f32[56,128]{1,0:T(8,128)S(1)}, f32[56,128]{1,0:T(8,128)S(1)}, u32[]{:S(2)}, u32[]{:S(2)}) %collective-permute-start.5) | collective-permute-done | bytes 28704 | tf_op jit(solution)/shard_map/ppermute | solution.py:591
  25.8 1.8 %collective-permute-start.6 = (f32[56,128]{1,0:T(8,128)S(1)}, f32[56,128]{1,0:T(8,128)S(1)}, u32[]{:S(2)}, u32[]{:S(2)}) collective-permute-start(f32[56,128]{1,0:T(8,128)S(1)} %add.20), channel_id=1, source_target_pairs={{0,4},{1,5},{2,6},{3,7},{4,0},{5,1},{6,2},{7,3},{8,12},{9,13},{10,... | collective-permute-start | bytes 86024 | tf_op jit(solution)/shard_map/ppermute | solution.py:591
  27.5 1.2 %shard_map.88 = (bf16[2048,128]{1,0:T(8,128)(2,1)S(1)}, f32[256,128]{1,0:T(8,128)S(1)}, bf16[3,384,64]{2,1,0:T(8,128)(2,1)S(1)}, bf16[432,512]{1,0:T(8,128)(2,1)S(1)}) custom-call(s32[2]{0:T(128)S(1)} %pad_add_fusion.place_ref, bf16[256,128]{1,0:T(8,128)(2,1)S(1)} %get-tuple-element.39.encoded_ref, f32[256,128]{1,0:T(8,128)S(1)} %get-tuple-element.40.pre_ref, ...), custom_call_target="tpu_custom_call" | custom-call | flops 1000000000 | bytes 2000000 | tf_op jit(solution)/shard_map/pallas_call | solution.py:570
  28.7 2.0 %collective-permute-done.6 = f32[56,128]{1,0:T(8,128)S(1)} collective-permute-done((f32[56,128]{1,0:T(8,128)S(1)}, f32[56,128]{1,0:T(8,128)S(1)}, u32[]{:S(2)}, u32[]{:S(2)}) %collective-permute-start.6) | collective-permute-done | bytes 28704 | tf_op jit(solution)/shard_map/ppermute | solution.py:591
  30.7 3.7 %collective-permute-start.9 = (f32[56,128]{1,0:T(8,128)S(1)}, f32[56,128]{1,0:T(8,128)S(1)}, u32[]{:S(2)}, u32[]{:S(2)}) collective-permute-start(f32[56,128]{1,0:T(8,128)S(1)} %add.21.refs_0_), channel_id=1, source_target_pairs={{0,24},{1,25},{2,26},{3,27},{4,28},{5,29},{6,30},{7,31},{8,16},{9,... | collective-permute-start | bytes 86024 | tf_op jit(solution)/shard_map/ppermute | solution.py:591
  34.4 0.0 collective-permute-start.8
  34.4 0.7 %collective-permute-start.7 = (f32[56,128]{1,0:T(8,128)S(1)}, f32[56,128]{1,0:T(8,128)S(1)}, u32[]{:S(2)}, u32[]{:S(2)}) collective-permute-start(f32[56,128]{1,0:T(8,128)S(1)} %add.21.refs_0_), channel_id=1, source_target_pairs={{0,8},{1,9},{2,10},{3,11},{4,12},{5,13},{6,14},{7,15},{8,0},{9,1},... | collective-permute-start | bytes 86024 | tf_op jit(solution)/shard_map/ppermute | solution.py:591
  35.1 1.4 %all-to-all-done.got_ref = bf16[32,40,128]{2,1,0:T(8,128)(2,1)S(1)} async-done(((bf16[32,40,128]{2,1,0:T(8,128)(2,1)}), bf16[32,40,128]{2,1,0:T(8,128)(2,1)S(1)}, u32[]{:S(2)}, u32[]{:S(2)}) %all-to-all-start) | async-done | bytes 327712 | tf_op jit(solution)/shard_map/all_to_all | solution.py:715
  36.5 2.2 %shard_map.89 = (f32[16,16,64]{2,1,0:T(8,128)}, f32[27,64,64]{2,1,0:T(8,128)}, f32[16,16,64]{2,1,0:T(8,128)}, f32[8,128]{1,0:T(8,128)S(1)}) custom-call(bf16[32,40,128]{2,1,0:T(8,128)(2,1)S(1)} %all-to-all-done.got_ref, bf16[2048,128]{1,0:T(8,128)(2,1)S(1)} %get-tuple-element.41.spread_ref, f32[256,128]{1,0:T(8,128)S(1)} %get-tuple-element.42.slope_ref, ...), custom_call_target="tpu_custom_call" | custom-call | flops 2000000000 | bytes 2000000 | tf_op jit(solution)/shard_map/pallas_call | solution.py:570
  38.7 0.0 collective-permute-done.9.refs_3_
  38.7 0.5 %collective-permute-done.8.refs_2_ = f32[56,128]{1,0:T(8,128)S(1)} collective-permute-done((f32[56,128]{1,0:T(8,128)S(1)}, f32[56,128]{1,0:T(8,128)S(1)}, u32[]{:S(2)}, u32[]{:S(2)}) %collective-permute-start.8) | collective-permute-done | bytes 28704 | tf_op jit(solution)/shard_map/ppermute | solution.py:591
  39.2 0.0 collective-permute-done.7.refs_1_
  39.2 0.9 %shard_map.90 = f32[16,16,27]{2,1,0:T(8,128)} custom-call(bf16[432,512]{1,0:T(8,128)(2,1)S(1)} %get-tuple-element.48.order_ref, f32[8,128]{1,0:T(8,128)S(1)} %get-tuple-element.49.done_ref, f32[56,128]{1,0:T(8,128)S(1)} %add.21.refs_0_, f32[56,128]{1,0:T(8,128)S(1)} %collective-permute-done.7.refs_1_, f32[56,128]{1,0:T(8,128)S(1)} %collective-permute-done.8.refs_2_, ...), custom_call_target="tpu_custom_call" | custom-call | flops 100000000 | bytes 2000000 | tf_op jit(solution)/shard_map/pallas_call | solution.py:570
  (10 shorter events, 0.1 us)
Async XLA Ops:
  0.6 9.3 %copy-start.3 = (bf16[64,16,1,16]{0,3,2,1:T(8,128)(2,1)S(1)}, bf16[64,16,1,16]{0,3,2,1:T(8,128)(2,1)}, u32[]{:S(2)}) copy-start(bf16[64,16,1,16]{0,3,2,1:T(8,128)(2,1)} %param.5) | copy-start | bytes 98308
  0.6 9.3 %copy-start.1 = (bf16[27,64,64]{2,1,0:T(8,128)(2,1)S(1)}, bf16[27,64,64]{2,1,0:T(8,128)(2,1)}, u32[]{:S(2)}) copy-start(bf16[27,64,64]{2,1,0:T(8,128)(2,1)} %enc_ref.3) | copy-start | bytes 663556
  0.7 9.3 %copy-start.2 = (bf16[27,16,16]{0,2,1:T(8,128)(2,1)S(1)}, bf16[27,16,16]{0,2,1:T(8,128)(2,1)}, u32[]{:S(2)}) copy-start(bf16[27,16,16]{0,2,1:T(8,128)(2,1)} %param.8) | copy-start | bytes 41476
  1.8 6.0 %collective-permute-start = (bf16[16,8,128]{2,1,0:T(8,128)(2,1)S(1)}, bf16[16,8,128]{2,1,0:T(8,128)(2,1)S(1)}, u32[]{:S(2)}, u32[]{:S(2)}) collective-permute-start(bf16[16,8,128]{2,1,0:T(8,128)(2,1)S(1)} %bitcast.30), channel_id=1, source_target_pairs={{0,1},{1,0},{2,3},{3,2},{4,5},{5,4},{6,7},{7,6},{8,9},{9,8},{10,11... | collective-permute-start | bytes 98312 | tf_op jit(solution)/shard_map/ppermute | solution.py:601
  4.8 5.1 %collective-permute-start.3 = (bf16[16,16,64]{2,1,0:T(8,128)(2,1)}, bf16[16,16,64]{2,1,0:T(8,128)(2,1)S(1)}, u32[]{:S(2)}, u32[]{:S(2)}) collective-permute-start(bf16[16,16,64]{2,1,0:T(8,128)(2,1)} %bitcast.27), channel_id=1, source_target_pairs={{0,1},{1,0},{2,3},{3,2},{4,5},{5,4},{6,7},{7,6},{8,9},{9,8},{10,11... | collective-permute-start | bytes 98312 | tf_op jit(solution)/shard_map/ppermute | solution.py:599
  7.8 8.0 %collective-permute-start.2 = (bf16[144,128]{1,0:T(8,128)(2,1)S(1)}, bf16[144,128]{1,0:T(8,128)(2,1)S(1)}, u32[]{:S(2)}, u32[]{:S(2)}) collective-permute-start(bf16[144,128]{1,0:T(8,128)(2,1)S(1)} %pad_maximum_fusion.1), channel_id=1, source_target_pairs={{0,2},{1,3},{2,0},{3,1},{4,6},{5,7},{6,4},{7,5},{8,10},{9,11},{10,... | collective-permute-start | bytes 110600 | tf_op jit(solution)/shard_map/ppermute | solution.py:626
  7.9 7.9 %collective-permute-start.1 = (bf16[144,128]{1,0:T(8,128)(2,1)S(1)}, bf16[144,128]{1,0:T(8,128)(2,1)S(1)}, u32[]{:S(2)}, u32[]{:S(2)}) collective-permute-start(bf16[144,128]{1,0:T(8,128)(2,1)S(1)} %pad_maximum_fusion), channel_id=1, source_target_pairs={{0,1},{1,0},{2,4},{3,5},{4,2},{5,3},{6,8},{7,9},{8,6},{9,7},{10,12... | collective-permute-start | bytes 110600 | tf_op jit(solution)/shard_map/ppermute | solution.py:626
  9.9 3.3 %copy-start = (bf16[16,8,8,128]{3,2,1,0:T(8,128)(2,1)S(1)}, bf16[16,8,8,128]{3,2,1,0:T(8,128)(2,1)}, u32[]{:S(2)}) copy-start(bf16[16,8,8,128]{3,2,1,0:T(8,128)(2,1)} %cot_ref.3) | copy-start | bytes 786436
  15.7 3.9 %collective-permute-start.4 = (f32[56,128]{1,0:T(8,128)S(1)}, f32[56,128]{1,0:T(8,128)S(1)}, u32[]{:S(2)}, u32[]{:S(2)}) collective-permute-start(f32[56,128]{1,0:T(8,128)S(1)} %get-tuple-element.50), channel_id=1, source_target_pairs={{0,1},{1,0},{2,3},{3,2},{4,5},{5,4},{6,7},{7,6},{8,9},{9,8},{10,11... | collective-permute-start | bytes 86024 | tf_op jit(solution)/shard_map/ppermute | solution.py:591
  19.6 16.9 %all-to-all-start = ((bf16[32,40,128]{2,1,0:T(8,128)(2,1)}), bf16[32,40,128]{2,1,0:T(8,128)(2,1)S(1)}, u32[]{:S(2)}, u32[]{:S(2)}) async-start(bf16[32,40,128]{2,1,0:T(8,128)(2,1)} %shard_map.87), calls=%async_computation | async-start | bytes 655360 | tf_op jit(solution)/shard_map/all_to_all | solution.py:715
  24.5 1.3 %collective-permute-start.5 = (f32[56,128]{1,0:T(8,128)S(1)}, f32[56,128]{1,0:T(8,128)S(1)}, u32[]{:S(2)}, u32[]{:S(2)}) collective-permute-start(f32[56,128]{1,0:T(8,128)S(1)} %add.19), channel_id=1, source_target_pairs={{0,2},{1,3},{2,0},{3,1},{4,6},{5,7},{6,4},{7,5},{8,10},{9,11},{10,... | collective-permute-start | bytes 86024 | tf_op jit(solution)/shard_map/ppermute | solution.py:591
  25.8 5.0 %collective-permute-start.6 = (f32[56,128]{1,0:T(8,128)S(1)}, f32[56,128]{1,0:T(8,128)S(1)}, u32[]{:S(2)}, u32[]{:S(2)}) collective-permute-start(f32[56,128]{1,0:T(8,128)S(1)} %add.20), channel_id=1, source_target_pairs={{0,4},{1,5},{2,6},{3,7},{4,0},{5,1},{6,2},{7,3},{8,12},{9,13},{10,... | collective-permute-start | bytes 86024 | tf_op jit(solution)/shard_map/ppermute | solution.py:591
  30.7 8.0 %collective-permute-start.9 = (f32[56,128]{1,0:T(8,128)S(1)}, f32[56,128]{1,0:T(8,128)S(1)}, u32[]{:S(2)}, u32[]{:S(2)}) collective-permute-start(f32[56,128]{1,0:T(8,128)S(1)} %add.21.refs_0_), channel_id=1, source_target_pairs={{0,24},{1,25},{2,26},{3,27},{4,28},{5,29},{6,30},{7,31},{8,16},{9,... | collective-permute-start | bytes 86024 | tf_op jit(solution)/shard_map/ppermute | solution.py:591
  34.4 4.8 %collective-permute-start.8 = (f32[56,128]{1,0:T(8,128)S(1)}, f32[56,128]{1,0:T(8,128)S(1)}, u32[]{:S(2)}, u32[]{:S(2)}) collective-permute-start(f32[56,128]{1,0:T(8,128)S(1)} %add.21.refs_0_), channel_id=1, source_target_pairs={{0,16},{1,17},{2,18},{3,19},{4,20},{5,21},{6,22},{7,23},{8,24},{9,... | collective-permute-start | bytes 86024 | tf_op jit(solution)/shard_map/ppermute | solution.py:591
  34.4 4.8 %collective-permute-start.7 = (f32[56,128]{1,0:T(8,128)S(1)}, f32[56,128]{1,0:T(8,128)S(1)}, u32[]{:S(2)}, u32[]{:S(2)}) collective-permute-start(f32[56,128]{1,0:T(8,128)S(1)} %add.21.refs_0_), channel_id=1, source_target_pairs={{0,8},{1,9},{2,10},{3,11},{4,12},{5,13},{6,14},{7,15},{8,0},{9,1},... | collective-permute-start | bytes 86024 | tf_op jit(solution)/shard_map/ppermute | solution.py:591
